TPU v7x, 512 devices: a whole 4x4x16 slice. The times are simulated.
512 devices in a mesh: node: 8 (over y, z_hi), fsdp: 32 (over x, z_lo), rep: 2 (over core).
Axes of the slice: x: 4, y: 4, z: 16 (z_hi: 2, z_lo: 8; z = z_hi * 8 + z_lo), core: 2. Of those that a mesh axis runs over, the one named last changes fastest.
Arguments:
- hidden_in: bfloat16 [131072, 4096], P(('node', 'fsdp', 'rep')), may hold values from -24 to 24
- inv_rms: bfloat16 [131072], P(('node', 'fsdp', 'rep')), may hold values from 0.5 to 2
- norm_gain: float32 [4096], replicated, may hold values from 0.25 to 1.75
- key_grad: bfloat16 [131072, 512], P(('node', 'fsdp', 'rep')), may hold values from -0.015625 to 0.015625
- value_grad: bfloat16 [131072, 512], P(('node', 'fsdp', 'rep')), may hold values from -0.015625 to 0.015625
- key_weight: bfloat16 [4096, 512], P('node'), may hold values from -0.09375 to 0.09375
- value_weight: bfloat16 [4096, 512], P('node'), may hold values from -0.09375 to 0.09375
Outputs:
- key_scaled: float32 [4096, 512], P(('node', 'fsdp'))
- value_scaled: float32 [4096, 512], P(('node', 'fsdp'))
- grad_amax: float32 [2], replicated
- gain_grad: float32 [4096], replicated
All inputs are finite; a program needn't handle non-finite values. Where the computation divides by a largest or mean magnitude, that divisor is 1e-20 or more.
Results may differ from a plain program's by a relative error of at most 0.0053.
Values may be sent and summed in bfloat16 or wider, within the bound.
No kernel may reach another device: no remote copies, remote signals or barrier semaphores. Data moves between devices by JAX's collectives and lax.ppermute only.
A program may use at most 128 MiB of HBM per device.

v0:
```python
import jax
import jax.numpy as jnp
from jax import lax
from jax.sharding import PartitionSpec as P


def per_device(hidden_in, inv_rms, norm_gain, key_grad, value_grad, key_weight, value_weight):
    node_count = lax.axis_size("node")
    feat_all = hidden_in.shape[1]
    width = 2 * key_grad.shape[1]
    kv_width = key_grad.shape[1]
    rows_node = feat_all // node_count
    both_grads = jnp.concatenate([key_grad, value_grad], axis=1)
    scaled = hidden_in.astype(jnp.float32) * inv_rms.astype(jnp.float32)[:, None]
    normed = (scaled * norm_gain[None, :]).astype(jnp.bfloat16)
    partial_value = lax.dot_general(
        normed, both_grads, (((0,), (0,)), ((), ())), preferred_element_type=jnp.float32
    )
    stacked = partial_value.astype(jnp.bfloat16).reshape(node_count, rows_node, width)
    received = lax.all_to_all(stacked, "node", split_axis=0, concat_axis=0, tiled=True)
    node_sum = jnp.sum(received.astype(jnp.float32), axis=0)
    joined = jnp.concatenate(
        [
            lax.all_gather(key_weight, "node", axis=0, tiled=True),
            lax.all_gather(value_weight, "node", axis=0, tiled=True),
        ],
        axis=1,
    )
    back = lax.dot_general(
        both_grads, joined, (((1,), (1,)), ((), ())), preferred_element_type=jnp.float32
    )
    gain_local = jnp.sum(back * scaled, axis=0)
    owner_count = lax.axis_size("fsdp")
    owner_rows = rows_node // owner_count
    to_owners = node_sum.astype(jnp.bfloat16).reshape(owner_count, owner_rows, width)
    arrived = lax.all_to_all(to_owners, "fsdp", split_axis=0, concat_axis=0, tiled=True)
    owned = jnp.sum(arrived.astype(jnp.float32), axis=0)
    owned = lax.psum(owned, "rep")
    gain_grad = lax.psum(gain_local, ("node", "fsdp", "rep"))
    key_part = owned[:, :kv_width]
    value_part = owned[:, kv_width:]
    local_peak = jnp.stack([jnp.max(jnp.abs(key_part)), jnp.max(jnp.abs(value_part))])
    grad_amax = lax.pmax(local_peak, ("node", "fsdp"))
    key_scaled = key_part * (6.0 / (grad_amax[0] + 1e-06))
    value_scaled = value_part * (6.0 / (grad_amax[1] + 1e-06))
    return (key_scaled, value_scaled, grad_amax, gain_grad)


def solution(mesh):
    return jax.shard_map(
        per_device,
        mesh=mesh,
        in_specs=(
            P(("node", "fsdp", "rep"), None),
            P(("node", "fsdp", "rep")),
            P(),
            P(("node", "fsdp", "rep"), None),
            P(("node", "fsdp", "rep"), None),
            P("node", None),
            P("node", None),
        ),
        out_specs=(P(("node", "fsdp"), None), P(("node", "fsdp"), None), P(), P()),
        check_vma=False,
    )
```

profile of v0, /device:TPU:2, one launch (start us, length us, event | category | flops | bytes accessed | tf_op | source)
XLA Modules:
  0.0 1677.0 jit_solution(16777436502897984974)
XLA Ops:
  8.0 0.7 convert_element_type.18
  8.7 1.0 constant_dynamic-update-slice_fusion.1
  9.6 1.0 constant_dynamic-update-slice_fusion
  10.6 0.0 copy-start.1
  10.6 7.6 convolution_convert_fusion
  18.2 0.0 copy-done.1
  18.2 17.7 %all-to-all-start = ((bf16[8,512,1024]{2,1,0:T(8,128)(2,1)}), bf16[8,512,1024]{2,1,0:T(8,128)(2,1)}, u32[]{:S(2)}, u32[]{:S(2)}) async-start(bf16[8,512,1024]{2,1,0:T(8,128)(2,1)} %bitcast.8), calls=%async_computation | async-start | bytes 16777216 | tf_op jit(solution)/shard_map/all_to_all | solution.py:20
  35.9 0.0 all-gather.3.cloned.1.call-start
  36.0 0.7 all-gather.3.cloned.1.call-update
  36.7 0.0 all-gather.5.cloned.1.call-start
  36.7 0.7 all-gather.5.cloned.1.call-update
  37.4 0.0 copy-start
  37.4 0.0 all-reduce.2.cloned.1.call-start
  37.5 330.1 %all-to-all-done = bf16[8,512,1024]{2,1,0:T(8,128)(2,1)} async-done(((bf16[8,512,1024]{2,1,0:T(8,128)(2,1)}), bf16[8,512,1024]{2,1,0:T(8,128)(2,1)}, u32[]{:S(2)}, u32[]{:S(2)}) %all-to-all-start) | async-done | bytes 8388640 | tf_op jit(solution)/shard_map/all_to_all | solution.py:20
  367.6 5.7 reduce_sum.30
  373.2 233.0 %all_to_all.10 = bf16[32,16,1024]{2,1,0:T(8,128)(2,1)S(1)} all-to-all(bf16[32,16,1024]{2,1,0:T(8,128)(2,1)S(1)} %bitcast.9), channel_id=1, replica_groups=mesh['node'=8,'fsdp'=32,'rep'=2] {'fsdp'}, dimensions={0} | all-to-all | bytes 2097152 | tf_op jit(solution)/shard_map/all_to_all | solution.py:36
  606.2 0.8 convert_reduce_fusion
  607.0 0.0 all-reduce.2.cloned.1.call-update
  607.0 0.0 all-gather.3.cloned.1.call-done
  607.0 129.4 %all-gather.5.cloned.1.call-done = bf16[4096,512]{1,0:T(8,128)(2,1)} async-done(((bf16[512,512]{1,0:T(8,128)(2,1)}), bf16[4096,512]{1,0:T(8,128)(2,1)}) %all-gather.5.cloned.1.call-update) | async-done | bytes 4194320 | tf_op jit(solution)/shard_map/all_gather | solution.py:25
  736.4 0.0 copy-done
  736.4 6.1 fusion.9
  742.5 0.0 all-reduce.2.cloned.1.call-done
  742.5 1.4 abs_reduce_fusion.1
  743.9 1.4 pad_maximum_fusion
  745.3 99.0 %psum.15 = f32[4096]{0:T(1024)} all-reduce(f32[4096]{0:T(1024)S(1)} %fusion.9), channel_id=1, replica_groups=mesh['node'=8,'fsdp'=32,'rep'=2] {'node','fsdp','rep'}, use_global_device_ids=true, to_apply=%region_7.0 | all-reduce | flops 4096 | bytes 32768 | tf_op jit(solution)/shard_map/psum | solution.py:39
  844.3 821.9 %pmax.7 = f32[2]{0:T(128)S(1)} all-reduce(f32[2]{0:T(128)S(1)} %pad_maximum_fusion), channel_id=1, replica_groups=mesh['node'=8,'fsdp'=32,'rep'=2] {'node','fsdp'}, use_global_device_ids=true, to_apply=%region_5.0 | all-reduce | flops 2 | bytes 16 | tf_op jit(solution)/shard_map/pmax | solution.py:43
  1666.2 0.0 copy-start.2
  1666.2 0.6 fusion.13
  1668.1 1.4 slice_multiply_fusion
  1669.5 0.0 copy-done.2
Async XLA Ops:
  10.6 7.6 copy-start.1
  18.2 349.3 %all-to-all-start = ((bf16[8,512,1024]{2,1,0:T(8,128)(2,1)}), bf16[8,512,1024]{2,1,0:T(8,128)(2,1)}, u32[]{:S(2)}, u32[]{:S(2)}) async-start(bf16[8,512,1024]{2,1,0:T(8,128)(2,1)} %bitcast.8), calls=%async_computation | async-start | bytes 16777216 | tf_op jit(solution)/shard_map/all_to_all | solution.py:20
  35.9 571.1 %all-gather.3.cloned.1.call-start = ((), (), s32[]{:S(2)}) async-start(), calls=%async_computation.3 | async-start | bytes 4718592 | tf_op jit(solution)/shard_map/all_gather | solution.py:24
  36.7 699.7 %all-gather.5.cloned.1.call-start = ((), (), s32[]{:S(2)}) async-start(), calls=%async_computation.4 | async-start | bytes 4718592 | tf_op jit(solution)/shard_map/all_gather | solution.py:25
  37.4 699.0 %copy-start = (bf16[256,4096]{1,0:T(8,128)(2,1)S(1)}, bf16[256,4096]{1,0:T(8,128)(2,1)}, u32[]{:S(2)}) copy-start(bf16[256,4096]{1,0:T(8,128)(2,1)} %param.7) | copy-start | bytes 6291460
  37.4 705.1 %all-reduce.2.cloned.1.call-start = ((), (), s32[]{:S(2)}) async-start(), calls=%async_computation.2 | async-start | bytes 131072 | tf_op jit(solution)/shard_map/psum | solution.py:38
  1666.2 3.4 copy-start.2
Sparse Core Ops, SparseCore 0:
  40.0 403.7 all-gather.2
  447.0 289.3 all-gather.4
Sparse Core Ops, SparseCore 1:
  607.1 38.9 all-reduce.1
where the time goes:
time: 1680 us
  blocking collectives  1150 us (68%)
  waiting for transfers between devices  461 us (27%)
  starting transfers between devices  17.8 us (1%)
  between operations  16.9 us (1%)
    pmax x1, blocking collectives, per_device(): grad_amax = lax.pmax(local_peak, ('node', 'fsdp'))  822 us
    all_to_all x1, waiting for transfers between devices, per_device(): lax.all_to_all(stacked, 'node', split_axis=0, concat_axis=0, tiled=True)  330 us
    all_to_all x1, blocking collectives, per_device(): lax.all_to_all(to_owners, 'fsdp', split_axis=0, concat_axis=0, tiled=True)  233 us
    all_gather x1, waiting for transfers between devices, per_device(): lax.all_gather(value_weight, 'node', axis=0, tiled=True)  129 us
    psum x1, blocking collectives, per_device(): gain_grad = lax.psum(gain_local, ('node', 'fsdp', 'rep'))  99 us
  transfers between devices with their start and end apart: 4, of which 2 were waited for; matrix products, arithmetic and copies ran while one was open for 1% of the time, Pallas kernels for 0%

commit v1 on v0

v1 whole, which is shorter than its diff:
```python
import functools

import jax
import jax.numpy as jnp
import numpy as np
from jax import lax
from jax.experimental import pallas as pl
from jax.experimental.pallas import tpu as pltpu
from jax.sharding import PartitionSpec as P

ALL = ("node", "fsdp", "rep")
OWNERS = ("node", "fsdp")
NY, NZH, NX, NZL, NC = 4, 2, 4, 8, 2
INDEX = np.arange(NY * NZH * NX * NZL * NC).reshape(NY, NZH, NX, NZL, NC)
TILE = 128


def core_of(stream, y, x):
    return (stream + x + y) % 2


def plane_groups(first_axis):
    groups = []
    for zh in range(NZH):
        for zl in range(NZL):
            for stream in range(2):
                along_x = (first_axis == "x") == (stream == 0)
                for fixed in range(4):
                    members = [(fixed, x) for x in range(4)] if along_x else [(y, fixed) for y in range(4)]
                    groups.append([int(INDEX[y, zh, x, zl, core_of(stream, y, x)]) for y, x in members])
    return groups


def z_groups():
    return [
        [int(INDEX[y, z // NZL, x, z % NZL, c]) for z in range(NZH * NZL)]
        for y in range(NY) for x in range(NX) for c in range(NC)
    ]


SWAP = [(d, d ^ 1) for d in range(INDEX.size)]


def product_kernel(stream_ref, own_ref, other_ref, own_grad_ref, other_grad_ref, out_ref):
    first = pl.program_id(0)
    x_first = stream_ref[0] == 0
    for second in range(4):
        y = jnp.where(x_first, second, first)
        x = jnp.where(x_first, first, second)
        for zh in range(NZH):
            columns = pl.ds(pl.multiple_of((y * 8 + zh * 4 + x) * TILE, TILE), TILE)
            total = sum(
                lax.dot_general(
                    tokens[:, columns], grads[...], (((0,), (0,)), ((), ())), preferred_element_type=jnp.float32
                )
                for tokens, grads in ((own_ref, own_grad_ref), (other_ref, other_grad_ref))
            )
            rows = pl.ds((second * NZH + zh) * TILE, TILE)
            out_ref[0, rows, :] = total.astype(jnp.bfloat16)


def partial_product(stream, own, other, own_grad, other_grad):
    width = own_grad.shape[1]
    feats = own.shape[1]
    whole = lambda a: pl.BlockSpec(a.shape, lambda i, s: (0, 0))
    return pl.pallas_call(
        product_kernel,
        out_shape=jax.ShapeDtypeStruct((4, feats // 4, width), jnp.bfloat16),
        grid_spec=pltpu.PrefetchScalarGridSpec(
            num_scalar_prefetch=1,
            grid=(4,),
            in_specs=[whole(own), whole(other), whole(own_grad), whole(other_grad)],
            out_specs=pl.BlockSpec((1, feats // 4, width), lambda i, s: (i, 0, 0)),
        ),
        compiler_params=pltpu.CompilerParams(vmem_limit_bytes=40 * 1024 * 1024),
    )(stream, own, other, own_grad, other_grad)


def exchange_sum(parts, groups, kept):
    arrived = lax.all_to_all(parts, ALL, 0, 0, tiled=True, axis_index_groups=groups)
    return jnp.sum(arrived.astype(jnp.float32), axis=0).astype(kept)


def per_device(hidden_in, inv_rms, norm_gain, key_grad, value_grad, key_weight, value_weight):
    node, fsdp, core = lax.axis_index("node"), lax.axis_index("fsdp"), lax.axis_index("rep")
    y, x = node // NZH, fsdp // NZL
    stream = (core + x + y) % 2
    keys_here = stream == 0
    own_grad = jnp.where(keys_here, key_grad, value_grad)
    sent_grad = jnp.where(keys_here, value_grad, key_grad)
    other_grad = lax.ppermute(sent_grad, ALL, SWAP)
    scaled = hidden_in.astype(jnp.float32) * inv_rms.astype(jnp.float32)[:, None]
    normed = (scaled * norm_gain[None, :]).astype(jnp.bfloat16)
    other = lax.ppermute(normed, ALL, SWAP)
    width = key_grad.shape[1]
    parts = partial_product(stream.astype(jnp.int32).reshape(1), normed, other, own_grad, other_grad)
    line_sum = exchange_sum(parts, plane_groups("x"), jnp.bfloat16)
    plane_sum = exchange_sum(line_sum.reshape(4, -1, width), plane_groups("y"), jnp.bfloat16)
    owned = exchange_sum(plane_sum.reshape(NZH * NZL, -1, width), z_groups(), jnp.float32)
    arrived = lax.ppermute(owned, ALL, SWAP)
    key_part = jnp.where(keys_here, owned, arrived)
    value_part = jnp.where(keys_here, arrived, owned)

    rows = key_part.shape[0]
    key_rows = lax.dynamic_slice_in_dim(key_weight, fsdp * rows, rows, 0).astype(jnp.float32)
    value_rows = lax.dynamic_slice_in_dim(value_weight, fsdp * rows, rows, 0).astype(jnp.float32)
    gain_rows = lax.dynamic_slice_in_dim(norm_gain, (node * NX * NZL + fsdp) * rows, rows, 0)
    gain_local = (jnp.sum(key_part * key_rows, axis=1) + jnp.sum(value_part * value_rows, axis=1)) / gain_rows
    peaks = jnp.stack([jnp.max(jnp.abs(key_part)), jnp.max(jnp.abs(value_part))])
    told = jnp.concatenate([gain_local, peaks, jnp.zeros((TILE - rows - 2,), jnp.float32)])
    owners = lax.axis_size("node") * lax.axis_size("fsdp")
    heard = lax.all_to_all(jnp.broadcast_to(told[None, :], (owners, TILE)), OWNERS, 0, 0, tiled=True)
    gain_grad = heard[:, :rows].reshape(-1)
    grad_amax = jnp.max(heard[:, rows:rows + 2], axis=0)
    key_scaled = key_part * (6.0 / (grad_amax[0] + 1e-06))
    value_scaled = value_part * (6.0 / (grad_amax[1] + 1e-06))
    return (key_scaled, value_scaled, grad_amax, gain_grad)


def solution(mesh):
    return jax.shard_map(
        per_device,
        mesh=mesh,
        in_specs=(
            P(("node", "fsdp", "rep"), None),
            P(("node", "fsdp", "rep")),
            P(),
            P(("node", "fsdp", "rep"), None),
            P(("node", "fsdp", "rep"), None),
            P("node", None),
            P("node", None),
        ),
        out_specs=(P(("node", "fsdp"), None), P(("node", "fsdp"), None), P(), P()),
        check_vma=False,
    )
```

time: 1680 us -> 138 us (0.08)
  the two profiles are of different devices: /device:TPU:2 before, /device:TPU:1 now
where the time goes in v1:
time: 138 us; the launch traced here: 137 us
  blocking collectives  95.4 us (69%)
  starting transfers between devices  19.6 us (14%)
  other arithmetic  11 us (8%)
  Pallas kernels  4.74 us (3%)
  waiting for transfers between devices  2.93 us (2%)
  between operations  2.17 us (2%)
    all_to_all x3, blocking collectives, exchange_sum(): lax.all_to_all(parts, ALL, 0, 0, tiled=True, axis_index_groups=groups)  68.4 us
    all_to_all x1, blocking collectives, per_device(): lax.all_to_all(jnp.broadcast_to(told[None, :], (owners, TILE)), OWNERS, 0...  27 us
    ppermute x1, starting transfers between devices, per_device(): arrived = lax.ppermute(owned, ALL, SWAP)  8.84 us
    ppermute x1, starting transfers between devices, per_device(): other = lax.ppermute(normed, ALL, SWAP)  8.79 us
    pallas_call x1, Pallas kernels, partial_product(): pl.pallas_call(product_kernel, out_shape=jax.ShapeDtypeStruct((4, feats /...  4.74 us
    reduce_sum x3, other arithmetic, exchange_sum(): return jnp.sum(arrived.astype(jnp.float32), axis=0).astype(kept)  3.78 us
  transfers between devices with their start and end apart: 3, of which 2 were waited for; matrix products, arithmetic and copies ran while one was open for 0% of the time, Pallas kernels for 0%

profile of v1, /device:TPU:1, one launch (start us, length us, event | category | flops | bytes accessed | tf_op | source)
XLA Modules:
  0.0 137.2 jit_solution(15512217475368012692)
XLA Ops:
  0.6 0.0 copy-start.1
  0.6 0.0 copy-start
  0.7 0.7 convert_element_type.23
  1.4 2.2 %multiply_convert_fusion.own_ref = bf16[256,4096]{1,0:T(8,128)(2,1)S(1)} fusion(bf16[256,4096]{1,0:T(8,128)(2,1)} %param.7, f32[4096]{0:T(1024)} %param.9, f32[256]{0:T(256)S(1)} %convert_element_type.23), kind=kLoop, calls=%fused_computation | loop fusion | flops 4194304 | bytes 4211712 | tf_op jit(solution)/shard_map/convert_element_type | solution.py:93
  3.6 8.8 %collective-permute-start = (bf16[256,4096]{1,0:T(8,128)(2,1)S(1)}, bf16[256,4096]{1,0:T(8,128)(2,1)}, u32[]{:S(2)}, u32[]{:S(2)}) collective-permute-start(bf16[256,4096]{1,0:T(8,128)(2,1)S(1)} %multiply_convert_fusion.own_ref), channel_id=1, source_target_pairs={{0,1},{1,0},{2,3},{3,2},{4,5},{5,4},{6,7},{7,6},{8,9},{9,8},{10,11... | collective-permute-start | bytes 6291464 | tf_op jit(solution)/shard_map/ppermute | solution.py:94
  12.4 0.0 copy-done.1
  12.4 0.0 copy-done
  12.5 1.9 %collective-permute-start.1 = (bf16[256,512]{1,0:T(8,128)(2,1)S(1)}, bf16[256,512]{1,0:T(8,128)(2,1)S(1)}, u32[]{:S(2)}, u32[]{:S(2)}) collective-permute-start(bf16[256,512]{1,0:T(8,128)(2,1)S(1)} %get-tuple-element.10), channel_id=1, source_target_pairs={{0,1},{1,0},{2,3},{3,2},{4,5},{5,4},{6,7},{7,6},{8,9},{9,8},{10,11... | collective-permute-start | bytes 786440 | tf_op jit(solution)/shard_map/ppermute | solution.py:91
  14.4 2.1 %collective-permute-done.1.other_grad_ref = bf16[256,512]{1,0:T(8,128)(2,1)S(1)} collective-permute-done((bf16[256,512]{1,0:T(8,128)(2,1)S(1)}, bf16[256,512]{1,0:T(8,128)(2,1)S(1)}, u32[]{:S(2)}, u32[]{:S(2)}) %collective-permute-start.1) | collective-permute-done | bytes 262176 | tf_op jit(solution)/shard_map/ppermute | solution.py:91
  16.5 0.0 collective-permute-done.other_ref
  16.5 4.7 %shard_map.102 = bf16[4,1024,512]{2,1,0:T(8,128)(2,1)S(1)} custom-call(s32[1]{0:T(128)} %bitcast.stream_ref, bf16[256,4096]{1,0:T(8,128)(2,1)S(1)} %multiply_convert_fusion.own_ref, bf16[256,4096]{1,0:T(8,128)(2,1)} %collective-permute-done.other_ref, bf16[256,512]{1,0:T(8,128)(2,1)S(1)} %get-tuple-element.11.own_grad_ref, ...), custom_call_target="tpu_custom_call" | custom-call | tf_op jit(solution)/shard_map/pallas_call | solution.py:66
  21.3 30.5 %all_to_all.24 = bf16[4,1024,512]{2,1,0:T(8,128)(2,1)} all-to-all(bf16[4,1024,512]{2,1,0:T(8,128)(2,1)S(1)} %shard_map.102), channel_id=1, replica_groups={{0,17,32,49},{129,144,161,176},{256,273,288,305},{385,400,417,432},{1,1..., dimensions={0} | all-to-all | bytes 8388608 | tf_op jit(solution)/shard_map/all_to_all | solution.py:80
  51.7 3.5 %reduce_sum.51 = bf16[1024,512]{1,0:T(8,128)(2,1)S(1)} reduce(bf16[4,1024,512]{2,1,0:T(8,128)(2,1)} %all_to_all.24, bf16[]{:T(256)} %constant.66.clone.1), dimensions={0}, to_apply=%region_0.1 | reduce | flops 1572864 | bytes 5242882 | tf_op jit(solution)/shard_map/reduce_sum | solution.py:81
  55.2 12.6 %all_to_all.25 = bf16[4,256,512]{2,1,0:T(8,128)(2,1)S(1)} all-to-all(bf16[4,256,512]{2,1,0:T(8,128)(2,1)S(1)} %bitcast.9), channel_id=1, replica_groups={{0,129,256,385},{17,144,273,400},{32,161,288,417},{49,176,305,432},{1,1..., dimensions={0} | all-to-all | bytes 2097152 | tf_op jit(solution)/shard_map/all_to_all | solution.py:80
  67.8 0.2 reduce_sum.52
  68.1 25.3 %all_to_all.26 = bf16[16,16,512]{2,1,0:T(8,128)(2,1)S(1)} all-to-all(bf16[16,16,512]{2,1,0:T(8,128)(2,1)S(1)} %bitcast.12), channel_id=1, replica_groups={{0,2,4,6,8,10,12,14,64,66,68,70,72,74,76,78},{1,3,5,7,9,11,13,15,65,67,..., dimensions={0} | all-to-all | bytes 524288 | tf_op jit(solution)/shard_map/all_to_all | solution.py:80
  93.4 8.8 %collective-permute-start.2 = (f32[16,512]{1,0:T(8,128)S(1)}, f32[16,512]{1,0:T(8,128)S(1)}, u32[]{:S(2)}, u32[]{:S(2)}) collective-permute-start(f32[16,512]{1,0:T(8,128)S(1)} %convert_reduce_fusion), channel_id=1, source_target_pairs={{0,1},{1,0},{2,3},{3,2},{4,5},{5,4},{6,7},{7,6},{8,9},{9,8},{10,11... | collective-permute-start | bytes 98312 | tf_op jit(solution)/shard_map/ppermute | solution.py:100
  102.3 0.8 collective-permute-done.2
  103.1 1.4 %multiply_reduce_fusion = (f32[16]{0:T(128)S(1)}, f32[]{:T(128)}, f32[16,512]{1,0:T(8,128)S(1)}, f32[]{:T(128)}, f32[16]{0:T(128)S(1)}, /*index=5*/f32[16,512]{1,0:T(8,128)S(1)}) fusion(bf16[512,512]{1,0:T(8,128)(2,1)} %param.13, s32[]{:T(128)S(6)} %select_n.53, f32[16,512]{1,0:T(8,128)S(1)} %collective-permute-done.2, f32[16,512]{1,0:T(8,128)S(1)} %convert_reduce_fusion, ...), kind=kLoop, calls=%fused_computation.7 | loop fusion | flops 98270 | bytes 163981 | tf_op jit(solution)/shard_map/reduce_sum | solution.py:108
  104.5 0.8 dynamic-slice_divide_fusion
  105.3 1.4 %pad_maximum_fusion = f32[128]{0:T(128)S(1)} fusion(f32[110]{0:T(128)S(1)} %broadcast_in_dim.4, f32[1]{0:T(128)} %bitcast.4, f32[1]{0:T(128)} %bitcast.3, f32[16]{0:T(128)S(1)} %dynamic-slice_divide_fusion), kind=kLoop, calls=%fused_computation.13 | loop fusion | flops 384 | bytes 1024 | tf_op jit(solution)/shard_map/concatenate | solution.py:110
  106.7 0.1 broadcast_in_dim.5
  106.7 27.0 %all_to_all.27 = f32[256,1,128]{2,1,0:T(1,128)S(1)} all-to-all(f32[256,1,128]{2,1,0:T(1,128)S(1)} %broadcast_in_dim.5), channel_id=1, replica_groups=mesh['node'=8,'fsdp'=32,'rep'=2] {'node','fsdp'}, dimensions={0} | all-to-all | bytes 262144 | tf_op jit(solution)/shard_map/all_to_all | solution.py:112
  133.7 0.1 slice_reduce_fusion
  133.8 0.0 copy-start.2
  133.9 0.6 fusion
  135.8 0.7 reshape.39
  136.5 0.6 broadcast_multiply_fusion
  137.2 0.0 copy-done.2
  (3 shorter events, 0.1 us)
Async XLA Ops:
  0.6 11.8 %copy-start.1 = (bf16[256,512]{1,0:T(8,128)(2,1)S(1)}, bf16[256,512]{1,0:T(8,128)(2,1)}, u32[]{:S(2)}) copy-start(bf16[256,512]{1,0:T(8,128)(2,1)} %param.10) | copy-start | bytes 786436
  0.6 11.8 %copy-start = (bf16[256,512]{1,0:T(8,128)(2,1)S(1)}, bf16[256,512]{1,0:T(8,128)(2,1)}, u32[]{:S(2)}) copy-start(bf16[256,512]{1,0:T(8,128)(2,1)} %param.11) | copy-start | bytes 786436
  3.6 12.9 %collective-permute-start = (bf16[256,4096]{1,0:T(8,128)(2,1)S(1)}, bf16[256,4096]{1,0:T(8,128)(2,1)}, u32[]{:S(2)}, u32[]{:S(2)}) collective-permute-start(bf16[256,4096]{1,0:T(8,128)(2,1)S(1)} %multiply_convert_fusion.own_ref), channel_id=1, source_target_pairs={{0,1},{1,0},{2,3},{3,2},{4,5},{5,4},{6,7},{7,6},{8,9},{9,8},{10,11... | collective-permute-start | bytes 6291464 | tf_op jit(solution)/shard_map/ppermute | solution.py:94
  12.5 4.0 %collective-permute-start.1 = (bf16[256,512]{1,0:T(8,128)(2,1)S(1)}, bf16[256,512]{1,0:T(8,128)(2,1)S(1)}, u32[]{:S(2)}, u32[]{:S(2)}) collective-permute-start(bf16[256,512]{1,0:T(8,128)(2,1)S(1)} %get-tuple-element.10), channel_id=1, source_target_pairs={{0,1},{1,0},{2,3},{3,2},{4,5},{5,4},{6,7},{7,6},{8,9},{9,8},{10,11... | collective-permute-start | bytes 786440 | tf_op jit(solution)/shard_map/ppermute | solution.py:91
  93.4 9.7 %collective-permute-start.2 = (f32[16,512]{1,0:T(8,128)S(1)}, f32[16,512]{1,0:T(8,128)S(1)}, u32[]{:S(2)}, u32[]{:S(2)}) collective-permute-start(f32[16,512]{1,0:T(8,128)S(1)} %convert_reduce_fusion), channel_id=1, source_target_pairs={{0,1},{1,0},{2,3},{3,2},{4,5},{5,4},{6,7},{7,6},{8,9},{9,8},{10,11... | collective-permute-start | bytes 98312 | tf_op jit(solution)/shard_map/ppermute | solution.py:100
  133.8 3.3 %copy-start.2 = (f32[2]{0:T(128)}, f32[2]{0:T(128)S(1)}, u32[]{:S(2)}) copy-start(f32[2]{0:T(128)S(1)} %slice_reduce_fusion) | copy-start | bytes 28

commit v2 on v1

v2 whole, which is shorter than its diff:
```python
import functools

import jax
import jax.numpy as jnp
import numpy as np
from jax import lax
from jax.experimental import pallas as pl
from jax.experimental.pallas import tpu as pltpu
from jax.sharding import PartitionSpec as P

ALL = ("node", "fsdp", "rep")
OWNERS = ("node", "fsdp")
NY, NZH, NX, NZL, NC = 4, 2, 4, 8, 2
INDEX = np.arange(NY * NZH * NX * NZL * NC).reshape(NY, NZH, NX, NZL, NC)
TILE = 128


def core_of(stream, y, x):
    return (stream + x + y) % 2


def plane_pairs(stage, offset):
    pairs = []
    for y, zh, x, zl, c in np.ndindex(*INDEX.shape):
        stream = core_of(c, y, x)
        along_x = stage == stream
        to_y, to_x = (y, (x + offset) % 4) if along_x else ((y + offset) % 4, x)
        target = INDEX[to_y, zh, to_x, zl, core_of(stream, to_y, to_x)]
        pairs.append((int(INDEX[y, zh, x, zl, c]), int(target)))
    return pairs


def z_groups():
    return [
        [int(INDEX[y, z // NZL, x, z % NZL, c]) for z in range(NZH * NZL)]
        for y in range(NY) for x in range(NX) for c in range(NC)
    ]


SWAP = [(d, d ^ 1) for d in range(INDEX.size)]


def product_kernel(width, place_ref, own_ref, other_ref, own_pack_ref, other_pack_ref, gain_ref, out_ref):
    x_first = place_ref[0] == 0
    first = place_ref[1]
    for step in range(4):
        second = lax.rem(place_ref[2] + step, 4)
        y = jnp.where(x_first, second, first)
        x = jnp.where(x_first, first, second)
        for zh in range(NZH):
            columns = pl.ds(pl.multiple_of((y * 8 + zh * 4 + x) * TILE, TILE), TILE)
            gain = gain_ref[:, columns]
            total = None
            for tokens, pack in ((own_ref, own_pack_ref), (other_ref, other_pack_ref)):
                inv_rms = pack[:, width:width + 1].astype(jnp.float32)
                normed = (tokens[:, columns].astype(jnp.float32) * inv_rms * gain).astype(jnp.bfloat16)
                term = lax.dot_general(
                    normed, pack[:, :width], (((0,), (0,)), ((), ())), preferred_element_type=jnp.float32
                )
                total = term if total is None else total + term
            rows = pl.ds((step * NZH + zh) * TILE, TILE)
            out_ref[rows, :] = total.astype(jnp.bfloat16)


def chunk_product(place, own, other, own_pack, other_pack, gain, width):
    tokens, feats = own.shape
    rows = feats // 4
    return pl.pallas_call(
        functools.partial(product_kernel, width),
        out_shape=jax.ShapeDtypeStruct((rows, width), jnp.bfloat16),
        in_specs=[pl.BlockSpec(memory_space=pltpu.SMEM)] + [pl.BlockSpec(memory_space=pltpu.VMEM)] * 5,
        out_specs=pl.BlockSpec(memory_space=pltpu.VMEM),
        cost_estimate=pl.CostEstimate(
            flops=4 * tokens * rows * width, bytes_accessed=rows * (4 * tokens + 2 * width), transcendentals=0
        ),
        compiler_params=pltpu.CompilerParams(vmem_limit_bytes=32 * 1024 * 1024),
    )(place, own, other, own_pack, other_pack, gain)


def total_of(arrays):
    total = arrays[0].astype(jnp.float32)
    for array in arrays[1:]:
        total = total + array.astype(jnp.float32)
    return total.astype(jnp.bfloat16)


def per_device(hidden_in, inv_rms, norm_gain, key_grad, value_grad, key_weight, value_weight):
    node, fsdp, core = lax.axis_index("node"), lax.axis_index("fsdp"), lax.axis_index("rep")
    y, x = node // NZH, fsdp // NZL
    stream = (core + x + y) % 2
    keys_here = stream == 0
    width = key_grad.shape[1]
    other = lax.ppermute(hidden_in, ALL, SWAP)
    inv_lanes = jnp.broadcast_to(inv_rms[:, None], (inv_rms.shape[0], TILE))
    own_pack = jnp.concatenate([jnp.where(keys_here, key_grad, value_grad), inv_lanes], axis=1)
    sent_pack = jnp.concatenate([jnp.where(keys_here, value_grad, key_grad), inv_lanes], axis=1)
    other_pack = lax.ppermute(sent_pack, ALL, SWAP)
    first = jnp.where(keys_here, x, y)
    second = jnp.where(keys_here, y, x)
    chunks = []
    for offset in (2, 1, 3, 0):
        place = jnp.stack([stream, (first + offset) % 4, second]).astype(jnp.int32)
        chunk = chunk_product(place, hidden_in, other, own_pack, other_pack, norm_gain[None, :], width)
        if offset:
            chunk = lax.ppermute(chunk, ALL, plane_pairs(0, offset))
        chunks.append(chunk.reshape(4, -1, width))
    planes = []
    for offset in (2, 1, 3, 0):
        line_sum = total_of([chunk[offset] for chunk in chunks])
        if offset:
            line_sum = lax.ppermute(line_sum, ALL, plane_pairs(1, offset))
        planes.append(line_sum)
    plane_sum = total_of(planes).reshape(NZH * NZL, -1, width)
    heard = lax.all_to_all(plane_sum, ALL, 0, 0, tiled=True, axis_index_groups=z_groups())
    owned = jnp.sum(heard.astype(jnp.float32), axis=0)
    arrived = lax.ppermute(owned, ALL, SWAP)
    key_part = jnp.where(keys_here, owned, arrived)
    value_part = jnp.where(keys_here, arrived, owned)

    rows = key_part.shape[0]
    key_rows = lax.dynamic_slice_in_dim(key_weight, fsdp * rows, rows, 0).astype(jnp.float32)
    value_rows = lax.dynamic_slice_in_dim(value_weight, fsdp * rows, rows, 0).astype(jnp.float32)
    gain_rows = lax.dynamic_slice_in_dim(norm_gain, (node * NX * NZL + fsdp) * rows, rows, 0)
    gain_local = (jnp.sum(key_part * key_rows, axis=1) + jnp.sum(value_part * value_rows, axis=1)) / gain_rows
    peaks = jnp.stack([jnp.max(jnp.abs(key_part)), jnp.max(jnp.abs(value_part))])
    told = jnp.concatenate([gain_local, peaks, jnp.zeros((TILE - rows - 2,), jnp.float32)])
    owners = lax.axis_size("node") * lax.axis_size("fsdp")
    heard = lax.all_to_all(jnp.broadcast_to(told[None, :], (owners, TILE)), OWNERS, 0, 0, tiled=True)
    gain_grad = heard[:, :rows].reshape(-1)
    grad_amax = jnp.max(heard[:, rows:rows + 2], axis=0)
    key_scaled = key_part * (6.0 / (grad_amax[0] + 1e-06))
    value_scaled = value_part * (6.0 / (grad_amax[1] + 1e-06))
    return (key_scaled, value_scaled, grad_amax, gain_grad)


def solution(mesh):
    return jax.shard_map(
        per_device,
        mesh=mesh,
        in_specs=(
            P(("node", "fsdp", "rep"), None),
            P(("node", "fsdp", "rep")),
            P(),
            P(("node", "fsdp", "rep"), None),
            P(("node", "fsdp", "rep"), None),
            P("node", None),
            P("node", None),
        ),
        out_specs=(P(("node", "fsdp"), None), P(("node", "fsdp"), None), P(), P()),
        check_vma=False,
    )
```

time: 138 us -> 139 us (level)
  blocking collectives: 95.4 us -> 60.4 us
  waiting for transfers between devices: 2.93 us -> 18.3 us
  Pallas kernels: 4.74 us -> 15.8 us
  starting transfers between devices: 19.6 us -> 30.4 us
  other arithmetic: 11 us -> 8.41 us
    all_to_all x3 -> x1, blocking collectives: 68.4 us -> 31.9 us  [per_device(): lax.all_to_all(plane_sum, ALL, 0, 0, tiled=True, axis_index_groups=z_grou...]
    ppermute x2 -> x8, starting transfers between devices: 10.7 us -> 27 us  [the longest x1 8.92 us: per_device(): other = lax.ppermute(hidden_in, ALL, SWAP)]
    ppermute x2 -> x8, waiting for transfers between devices: 2.1 us -> 17.5 us  [the longest x3 9.47 us: per_device(): chunk = lax.ppermute(chunk, ALL, plane_pairs(0, offset))]
    pallas_call x1 -> x4, Pallas kernels: 4.74 us -> 15.8 us  [chunk_product(): pl.pallas_call(functools.partial(product_kernel, width), out_shape=jax.Sh...]
    ppermute x1, starting transfers between devices: 8.84 us -> 3.34 us  [per_device(): arrived = lax.ppermute(owned, ALL, SWAP)]
    reduce_sum x3 -> x1, other arithmetic: 3.78 us -> 0.04 us  [per_device(): owned = jnp.sum(heard.astype(jnp.float32), axis=0)]
    all_to_all x1, blocking collectives: 27 us -> 28.5 us  [per_device(): lax.all_to_all(jnp.broadcast_to(told[None, :], (owners, TILE)), OWNERS, 0...]
  transfers between devices with their start and end apart: 3 -> 9, of which waited for: 2 -> 7; matrix products, arithmetic and copies ran while one was open for 0% -> 2% of each run, Pallas kernels for 0% -> 8%
where the time goes in v2:
time: 139 us; the launch traced here: 138 us
  blocking collectives  60.4 us (43%)
  starting transfers between devices  30.4 us (22%)
  waiting for transfers between devices  18.3 us (13%)
  Pallas kernels  15.8 us (11%)
  other arithmetic  8.41 us (6%)
  between operations  2.3 us (2%)
  local copies, waits for them, and re-layouts  2.13 us (2%)
    all_to_all x1, blocking collectives, per_device(): lax.all_to_all(plane_sum, ALL, 0, 0, tiled=True, axis_index_groups=z_grou...  31.9 us
    all_to_all x1, blocking collectives, per_device(): lax.all_to_all(jnp.broadcast_to(told[None, :], (owners, TILE)), OWNERS, 0...  28.5 us
    pallas_call x4, Pallas kernels, chunk_product(): pl.pallas_call(functools.partial(product_kernel, width), out_shape=jax.Sh...  15.8 us
    ppermute x3, waiting for transfers between devices, per_device(): chunk = lax.ppermute(chunk, ALL, plane_pairs(0, offset))  9.47 us
    ppermute x1, starting transfers between devices, per_device(): other = lax.ppermute(hidden_in, ALL, SWAP)  8.92 us
    ppermute x3, starting transfers between devices, per_device(): chunk = lax.ppermute(chunk, ALL, plane_pairs(0, offset))  8.66 us
    ppermute x3, starting transfers between devices, per_device(): line_sum = lax.ppermute(line_sum, ALL, plane_pairs(1, offset))  7.55 us
    ppermute x3, waiting for transfers between devices, per_device(): line_sum = lax.ppermute(line_sum, ALL, plane_pairs(1, offset))  6.72 us
  transfers between devices with their start and end apart: 9, of which 7 were waited for; matrix products, arithmetic and copies ran while one was open for 2% of the time, Pallas kernels for 8%

profile of v2, /device:TPU:1, one launch (start us, length us, event | category | flops | bytes accessed | tf_op | source)
XLA Modules:
  0.0 137.7 jit_solution(3552823994561198494)
XLA Ops:
  0.6 0.0 copy-start
  0.6 0.0 copy-start.1
  0.7 8.9 %collective-permute-start = (bf16[256,4096]{1,0:T(8,128)(2,1)}, bf16[256,4096]{1,0:T(8,128)(2,1)}, u32[]{:S(2)}, u32[]{:S(2)}) collective-permute-start(bf16[256,4096]{1,0:T(8,128)(2,1)} %own_ref.7), channel_id=1, source_target_pairs={{0,1},{1,0},{2,3},{3,2},{4,5},{5,4},{6,7},{7,6},{8,9},{9,8},{10,11... | collective-permute-start | bytes 6291464 | tf_op jit(solution)/shard_map/ppermute | solution.py:93
  9.6 1.1 broadcast_select_fusion
  10.7 0.8 broadcast_in_dim.8
  11.5 0.1 pad_maximum_fusion
  11.5 1.9 %collective-permute-start.1 = (bf16[256,640]{1,0:T(8,128)(2,1)S(1)}, bf16[256,640]{1,0:T(8,128)(2,1)S(1)}, u32[]{:S(2)}, u32[]{:S(2)}) collective-permute-start(bf16[256,640]{1,0:T(8,128)(2,1)S(1)} %get-tuple-element.18), channel_id=1, source_target_pairs={{0,1},{1,0},{2,3},{3,2},{4,5},{5,4},{6,7},{7,6},{8,9},{9,8},{10,11... | collective-permute-start | bytes 983048 | tf_op jit(solution)/shard_map/ppermute | solution.py:97
  13.5 0.1 add_add_fusion.place_ref
  13.6 0.1 add_add_fusion.1.place_ref
  13.7 0.1 add_add_fusion.2.place_ref
  13.7 1.3 collective-permute-done.1.other_pack_ref
  15.0 0.0 collective-permute-done.other_ref
  15.0 0.0 copy-done
  15.0 0.0 copy-done.1
  15.1 4.2 %shard_map.102 = bf16[1024,512]{1,0:T(8,128)(2,1)} custom-call(s32[3]{0:T(128)S(1)} %add_add_fusion.place_ref, bf16[256,4096]{1,0:T(8,128)(2,1)S(1)} %copy-done, bf16[256,4096]{1,0:T(8,128)(2,1)} %collective-permute-done.other_ref, bf16[256,640]{1,0:T(8,128)(2,1)S(1)} %get-tuple-element.19.own_pack_ref, ...), custom_call_target="tpu_custom_call" | custom-call | flops 536870912 | bytes 2097152 | tf_op jit(solution)/shard_map/pallas_call | solution.py:68
  19.3 1.9 %collective-permute-start.2 = (bf16[1024,512]{1,0:T(8,128)(2,1)}, bf16[1024,512]{1,0:T(8,128)(2,1)}, u32[]{:S(2)}, u32[]{:S(2)}) collective-permute-start(bf16[1024,512]{1,0:T(8,128)(2,1)} %shard_map.102), channel_id=1, source_target_pairs={{0,32},{1,257},{2,34},{3,259},{4,36},{5,261},{6,38},{7,263},{8,40}... | collective-permute-start | bytes 3145736 | tf_op jit(solution)/shard_map/ppermute | solution.py:105
  21.2 4.2 %shard_map.103 = bf16[1024,512]{1,0:T(8,128)(2,1)} custom-call(s32[3]{0:T(128)S(1)} %add_add_fusion.1.place_ref, bf16[256,4096]{1,0:T(8,128)(2,1)S(1)} %copy-done, bf16[256,4096]{1,0:T(8,128)(2,1)} %collective-permute-done.other_ref, bf16[256,640]{1,0:T(8,128)(2,1)S(1)} %get-tuple-element.19.own_pack_ref, ...), custom_call_target="tpu_custom_call" | custom-call | flops 536870912 | bytes 2097152 | tf_op jit(solution)/shard_map/pallas_call | solution.py:68
  25.4 1.9 %collective-permute-start.3 = (bf16[1024,512]{1,0:T(8,128)(2,1)}, bf16[1024,512]{1,0:T(8,128)(2,1)}, u32[]{:S(2)}, u32[]{:S(2)}) collective-permute-start(bf16[1024,512]{1,0:T(8,128)(2,1)} %shard_map.103), channel_id=1, source_target_pairs={{0,17},{1,128},{2,19},{3,130},{4,21},{5,132},{6,23},{7,134},{8,25}... | collective-permute-start | bytes 3145736 | tf_op jit(solution)/shard_map/ppermute | solution.py:105
  27.3 4.2 %shard_map.104 = bf16[1024,512]{1,0:T(8,128)(2,1)} custom-call(s32[3]{0:T(128)S(1)} %add_add_fusion.2.place_ref, bf16[256,4096]{1,0:T(8,128)(2,1)S(1)} %copy-done, bf16[256,4096]{1,0:T(8,128)(2,1)} %collective-permute-done.other_ref, bf16[256,640]{1,0:T(8,128)(2,1)S(1)} %get-tuple-element.19.own_pack_ref, ...), custom_call_target="tpu_custom_call" | custom-call | flops 536870912 | bytes 2097152 | tf_op jit(solution)/shard_map/pallas_call | solution.py:68
  31.5 4.8 %collective-permute-start.4 = (bf16[1024,512]{1,0:T(8,128)(2,1)}, bf16[1024,512]{1,0:T(8,128)(2,1)}, u32[]{:S(2)}, u32[]{:S(2)}) collective-permute-start(bf16[1024,512]{1,0:T(8,128)(2,1)} %shard_map.104), channel_id=1, source_target_pairs={{0,49},{1,384},{2,51},{3,386},{4,53},{5,388},{6,55},{7,390},{8,57}... | collective-permute-start | bytes 3145736 | tf_op jit(solution)/shard_map/ppermute | solution.py:105
  36.4 0.1 add_add_fusion.3.place_ref
  36.4 3.2 %shard_map.105 = bf16[1024,512]{1,0:T(8,128)(2,1)S(1)} custom-call(s32[3]{0:T(128)S(1)} %add_add_fusion.3.place_ref, bf16[256,4096]{1,0:T(8,128)(2,1)S(1)} %copy-done, bf16[256,4096]{1,0:T(8,128)(2,1)} %collective-permute-done.other_ref, bf16[256,640]{1,0:T(8,128)(2,1)S(1)} %get-tuple-element.19.own_pack_ref, ...), custom_call_target="tpu_custom_call" | custom-call | flops 536870912 | bytes 2097152 | tf_op jit(solution)/shard_map/pallas_call | solution.py:68
  39.6 0.0 collective-permute-done.2
  39.7 8.5 %collective-permute-done.3 = bf16[1024,512]{1,0:T(8,128)(2,1)} collective-permute-done((bf16[1024,512]{1,0:T(8,128)(2,1)}, bf16[1024,512]{1,0:T(8,128)(2,1)}, u32[]{:S(2)}, u32[]{:S(2)}) %collective-permute-start.3) | collective-permute-done | bytes 1048608 | tf_op jit(solution)/shard_map/ppermute | solution.py:105
  48.2 1.0 collective-permute-done.4
  49.1 2.0 %add_convert_fusion.4 = (bf16[256,512]{1,0:T(8,128)(2,1)S(1)}, bf16[256,512]{1,0:T(8,128)(2,1)S(1)}, bf16[256,512]{1,0:T(8,128)(2,1)S(1)}) fusion(bf16[1024,512]{1,0:T(8,128)(2,1)S(1)} %shard_map.105, bf16[1024,512]{1,0:T(8,128)(2,1)} %collective-permute-done.4, bf16[1024,512]{1,0:T(8,128)(2,1)} %collective-permute-done.3, ...), kind=kLoop, calls=%fused_computation.5 | loop fusion | flops 3145728 | bytes 3932160 | tf_op jit(solution)/shard_map/convert_element_type | solution.py:84
  51.1 2.0 %collective-permute-start.5 = (bf16[256,512]{1,0:T(8,128)(2,1)S(1)}, bf16[256,512]{1,0:T(8,128)(2,1)S(1)}, u32[]{:S(2)}, u32[]{:S(2)}) collective-permute-start(bf16[256,512]{1,0:T(8,128)(2,1)S(1)} %get-tuple-element.10), channel_id=1, source_target_pairs={{0,256},{1,33},{2,258},{3,35},{4,260},{5,37},{6,262},{7,39},{8,264... | collective-permute-start | bytes 786440 | tf_op jit(solution)/shard_map/ppermute | solution.py:111
  53.1 3.4 %collective-permute-start.7 = (bf16[256,512]{1,0:T(8,128)(2,1)S(1)}, bf16[256,512]{1,0:T(8,128)(2,1)S(1)}, u32[]{:S(2)}, u32[]{:S(2)}) collective-permute-start(bf16[256,512]{1,0:T(8,128)(2,1)S(1)} %get-tuple-element.11), channel_id=1, source_target_pairs={{0,385},{1,48},{2,387},{3,50},{4,389},{5,52},{6,391},{7,54},{8,393... | collective-permute-start | bytes 786440 | tf_op jit(solution)/shard_map/ppermute | solution.py:111
  56.5 2.2 %collective-permute-start.6 = (bf16[256,512]{1,0:T(8,128)(2,1)S(1)}, bf16[256,512]{1,0:T(8,128)(2,1)S(1)}, u32[]{:S(2)}, u32[]{:S(2)}) collective-permute-start(bf16[256,512]{1,0:T(8,128)(2,1)S(1)} %get-tuple-element.12), channel_id=1, source_target_pairs={{0,129},{1,16},{2,131},{3,18},{4,133},{5,20},{6,135},{7,22},{8,137... | collective-permute-start | bytes 786440 | tf_op jit(solution)/shard_map/ppermute | solution.py:111
  58.7 1.3 collective-permute-done.5
  60.0 1.1 collective-permute-done.7
  61.1 4.3 %collective-permute-done.6 = bf16[256,512]{1,0:T(8,128)(2,1)S(1)} collective-permute-done((bf16[256,512]{1,0:T(8,128)(2,1)S(1)}, bf16[256,512]{1,0:T(8,128)(2,1)S(1)}, u32[]{:S(2)}, u32[]{:S(2)}) %collective-permute-start.6) | collective-permute-done | bytes 262176 | tf_op jit(solution)/shard_map/ppermute | solution.py:111
  65.4 1.3 add_convert_fusion
  66.8 31.9 %all_to_all.14 = bf16[16,16,512]{2,1,0:T(8,128)(2,1)S(1)} all-to-all(bf16[16,16,512]{2,1,0:T(8,128)(2,1)S(1)} %bitcast.20), channel_id=1, replica_groups={{0,2,4,6,8,10,12,14,64,66,68,70,72,74,76,78},{1,3,5,7,9,11,13,15,65,67,..., dimensions={0} | all-to-all | bytes 524288 | tf_op jit(solution)/shard_map/all_to_all | solution.py:114
  98.7 3.3 %collective-permute-start.8 = (f32[16,512]{1,0:T(8,128)S(1)}, f32[16,512]{1,0:T(8,128)S(1)}, u32[]{:S(2)}, u32[]{:S(2)}) collective-permute-start(f32[16,512]{1,0:T(8,128)S(1)} %convert_reduce_fusion), channel_id=1, source_target_pairs={{0,1},{1,0},{2,3},{3,2},{4,5},{5,4},{6,7},{7,6},{8,9},{9,8},{10,11... | collective-permute-start | bytes 98312 | tf_op jit(solution)/shard_map/ppermute | solution.py:116
  102.0 0.8 collective-permute-done.8
  102.8 1.4 %multiply_reduce_fusion = (f32[16]{0:T(128)S(1)}, f32[]{:T(128)}, f32[16,512]{1,0:T(8,128)S(1)}, f32[]{:T(128)}, f32[16]{0:T(128)S(1)}, /*index=5*/f32[16,512]{1,0:T(8,128)S(1)}) fusion(bf16[512,512]{1,0:T(8,128)(2,1)} %param.13, s32[]{:T(128)S(6)} %select_n.81, f32[16,512]{1,0:T(8,128)S(1)} %collective-permute-done.8, f32[16,512]{1,0:T(8,128)S(1)} %convert_reduce_fusion, ...), kind=kLoop, calls=%fused_computation.13 | loop fusion | flops 98270 | bytes 163981 | tf_op jit(solution)/shard_map/reduce_sum | solution.py:124
  104.2 0.1 dynamic-slice_divide_fusion
  104.3 1.4 pad_maximum_fusion.2
  105.7 0.1 broadcast_in_dim.11
  105.8 28.5 %all_to_all.15 = f32[256,1,128]{2,1,0:T(1,128)S(1)} all-to-all(f32[256,1,128]{2,1,0:T(1,128)S(1)} %broadcast_in_dim.11), channel_id=1, replica_groups=mesh['node'=8,'fsdp'=32,'rep'=2] {'node','fsdp'}, dimensions={0} | all-to-all | bytes 262144 | tf_op jit(solution)/shard_map/all_to_all | solution.py:128
  134.3 0.1 slice_reduce_fusion
  134.4 0.0 copy-start.2
  134.4 0.6 fusion
  136.4 0.7 reshape.66
  137.1 0.6 broadcast_multiply_fusion
  137.7 0.0 copy-done.2
  (2 shorter events, 0.0 us)
Async XLA Ops:
  0.6 14.4 %copy-start = (bf16[256,4096]{1,0:T(8,128)(2,1)S(1)}, bf16[256,4096]{1,0:T(8,128)(2,1)}, u32[]{:S(2)}) copy-start(bf16[256,4096]{1,0:T(8,128)(2,1)} %own_ref.7) | copy-start | bytes 6291460
  0.6 14.4 %copy-start.1 = (f32[4096]{0:T(1024)S(1)}, f32[4096]{0:T(1024)}, u32[]{:S(2)}) copy-start(f32[4096]{0:T(1024)} %param.9) | copy-start | bytes 49156
  0.7 14.4 %collective-permute-start = (bf16[256,4096]{1,0:T(8,128)(2,1)}, bf16[256,4096]{1,0:T(8,128)(2,1)}, u32[]{:S(2)}, u32[]{:S(2)}) collective-permute-start(bf16[256,4096]{1,0:T(8,128)(2,1)} %own_ref.7), channel_id=1, source_target_pairs={{0,1},{1,0},{2,3},{3,2},{4,5},{5,4},{6,7},{7,6},{8,9},{9,8},{10,11... | collective-permute-start | bytes 6291464 | tf_op jit(solution)/shard_map/ppermute | solution.py:93
  11.5 3.5 %collective-permute-start.1 = (bf16[256,640]{1,0:T(8,128)(2,1)S(1)}, bf16[256,640]{1,0:T(8,128)(2,1)S(1)}, u32[]{:S(2)}, u32[]{:S(2)}) collective-permute-start(bf16[256,640]{1,0:T(8,128)(2,1)S(1)} %get-tuple-element.18), channel_id=1, source_target_pairs={{0,1},{1,0},{2,3},{3,2},{4,5},{5,4},{6,7},{7,6},{8,9},{9,8},{10,11... | collective-permute-start | bytes 983048 | tf_op jit(solution)/shard_map/ppermute | solution.py:97
  19.3 20.4 %collective-permute-start.2 = (bf16[1024,512]{1,0:T(8,128)(2,1)}, bf16[1024,512]{1,0:T(8,128)(2,1)}, u32[]{:S(2)}, u32[]{:S(2)}) collective-permute-start(bf16[1024,512]{1,0:T(8,128)(2,1)} %shard_map.102), channel_id=1, source_target_pairs={{0,32},{1,257},{2,34},{3,259},{4,36},{5,261},{6,38},{7,263},{8,40}... | collective-permute-start | bytes 3145736 | tf_op jit(solution)/shard_map/ppermute | solution.py:105
  25.4 22.8 %collective-permute-start.3 = (bf16[1024,512]{1,0:T(8,128)(2,1)}, bf16[1024,512]{1,0:T(8,128)(2,1)}, u32[]{:S(2)}, u32[]{:S(2)}) collective-permute-start(bf16[1024,512]{1,0:T(8,128)(2,1)} %shard_map.103), channel_id=1, source_target_pairs={{0,17},{1,128},{2,19},{3,130},{4,21},{5,132},{6,23},{7,134},{8,25}... | collective-permute-start | bytes 3145736 | tf_op jit(solution)/shard_map/ppermute | solution.py:105
  31.5 17.6 %collective-permute-start.4 = (bf16[1024,512]{1,0:T(8,128)(2,1)}, bf16[1024,512]{1,0:T(8,128)(2,1)}, u32[]{:S(2)}, u32[]{:S(2)}) collective-permute-start(bf16[1024,512]{1,0:T(8,128)(2,1)} %shard_map.104), channel_id=1, source_target_pairs={{0,49},{1,384},{2,51},{3,386},{4,53},{5,388},{6,55},{7,390},{8,57}... | collective-permute-start | bytes 3145736 | tf_op jit(solution)/shard_map/ppermute | solution.py:105
  51.1 8.9 %collective-permute-start.5 = (bf16[256,512]{1,0:T(8,128)(2,1)S(1)}, bf16[256,512]{1,0:T(8,128)(2,1)S(1)}, u32[]{:S(2)}, u32[]{:S(2)}) collective-permute-start(bf16[256,512]{1,0:T(8,128)(2,1)S(1)} %get-tuple-element.10), channel_id=1, source_target_pairs={{0,256},{1,33},{2,258},{3,35},{4,260},{5,37},{6,262},{7,39},{8,264... | collective-permute-start | bytes 786440 | tf_op jit(solution)/shard_map/ppermute | solution.py:111
  53.1 8.0 %collective-permute-start.7 = (bf16[256,512]{1,0:T(8,128)(2,1)S(1)}, bf16[256,512]{1,0:T(8,128)(2,1)S(1)}, u32[]{:S(2)}, u32[]{:S(2)}) collective-permute-start(bf16[256,512]{1,0:T(8,128)(2,1)S(1)} %get-tuple-element.11), channel_id=1, source_target_pairs={{0,385},{1,48},{2,387},{3,50},{4,389},{5,52},{6,391},{7,54},{8,393... | collective-permute-start | bytes 786440 | tf_op jit(solution)/shard_map/ppermute | solution.py:111
  56.5 8.9 %collective-permute-start.6 = (bf16[256,512]{1,0:T(8,128)(2,1)S(1)}, bf16[256,512]{1,0:T(8,128)(2,1)S(1)}, u32[]{:S(2)}, u32[]{:S(2)}) collective-permute-start(bf16[256,512]{1,0:T(8,128)(2,1)S(1)} %get-tuple-element.12), channel_id=1, source_target_pairs={{0,129},{1,16},{2,131},{3,18},{4,133},{5,20},{6,135},{7,22},{8,137... | collective-permute-start | bytes 786440 | tf_op jit(solution)/shard_map/ppermute | solution.py:111
  98.7 4.2 %collective-permute-start.8 = (f32[16,512]{1,0:T(8,128)S(1)}, f32[16,512]{1,0:T(8,128)S(1)}, u32[]{:S(2)}, u32[]{:S(2)}) collective-permute-start(f32[16,512]{1,0:T(8,128)S(1)} %convert_reduce_fusion), channel_id=1, source_target_pairs={{0,1},{1,0},{2,3},{3,2},{4,5},{5,4},{6,7},{7,6},{8,9},{9,8},{10,11... | collective-permute-start | bytes 98312 | tf_op jit(solution)/shard_map/ppermute | solution.py:116
  134.4 3.3 %copy-start.2 = (f32[2]{0:T(128)}, f32[2]{0:T(128)S(1)}, u32[]{:S(2)}) copy-start(f32[2]{0:T(128)S(1)} %slice_reduce_fusion) | copy-start | bytes 28

commit v3 on v2

v3 whole, which is shorter than its diff:
```python
import functools

import jax
import jax.numpy as jnp
import numpy as np
from jax import lax
from jax.experimental import pallas as pl
from jax.experimental.pallas import tpu as pltpu
from jax.sharding import PartitionSpec as P

ALL = ("node", "fsdp", "rep")
OWNERS = ("node", "fsdp")
NY, NZH, NX, NZL, NC = 4, 2, 4, 8, 2
INDEX = np.arange(NY * NZH * NX * NZL * NC).reshape(NY, NZH, NX, NZL, NC)
TILE = 128


def plane_pairs(stage, offset):
    pairs = []
    for y, zh, x, zl, c in np.ndindex(*INDEX.shape):
        along_x = stage == c
        to_y, to_x = (y, (x + offset) % 4) if along_x else ((y + offset) % 4, x)
        target = INDEX[to_y, zh, to_x, zl, c]
        pairs.append((int(INDEX[y, zh, x, zl, c]), int(target)))
    return pairs


def z_groups():
    return [
        [int(INDEX[y, z // NZL, x, z % NZL, c]) for z in range(NZH * NZL)]
        for y in range(NY) for x in range(NX) for c in range(NC)
    ]


SWAP = [(d, d ^ 1) for d in range(INDEX.size)]


def coordinates():
    node, fsdp = lax.axis_index("node"), lax.axis_index("fsdp")
    return fsdp // NZL, node // NZH, fsdp % NZL, lax.axis_index("rep") == 0


def column_kernel(key_grad_ref, value_grad_ref, own_ref, sent_ref):
    keys_here = coordinates()[3]
    own_ref[...] = jnp.where(keys_here, key_grad_ref[...], value_grad_ref[...])
    sent_ref[...] = jnp.where(keys_here, value_grad_ref[...], key_grad_ref[...])


def product_kernel(offset, own_ref, other_ref, own_grad_ref, other_grad_ref, out_ref):
    x_here, y_here, _, x_first = coordinates()
    first = lax.rem(jnp.where(x_first, x_here, y_here) + offset, 4)
    for step in range(4):
        second = lax.rem(jnp.where(x_first, y_here, x_here) + step, 4)
        y = jnp.where(x_first, second, first)
        x = jnp.where(x_first, first, second)
        for zh in range(NZH):
            columns = pl.ds(pl.multiple_of((y * 8 + zh * 4 + x) * TILE, TILE), TILE)
            total = sum(
                lax.dot_general(
                    tokens[:, columns], grads[...], (((0,), (0,)), ((), ())), preferred_element_type=jnp.float32
                )
                for tokens, grads in ((own_ref, own_grad_ref), (other_ref, other_grad_ref))
            )
            rows = pl.ds((step * NZH + zh) * TILE, TILE)
            out_ref[rows, :] = total.astype(jnp.bfloat16)


VMEM_BLOCK = pl.BlockSpec(memory_space=pltpu.VMEM)
SMEM_BLOCK = pl.BlockSpec(memory_space=pltpu.SMEM)
SMALL = pltpu.CompilerParams(vmem_limit_bytes=4 * 1024 * 1024)


def columns_of(key_grad, value_grad):
    shape = jax.ShapeDtypeStruct(key_grad.shape, key_grad.dtype)
    return pl.pallas_call(
        column_kernel,
        out_shape=(shape, shape),
        in_specs=[VMEM_BLOCK] * 2,
        out_specs=(VMEM_BLOCK, VMEM_BLOCK),
        compiler_params=SMALL,
    )(key_grad, value_grad)


def chunk_product(offset, own, other, own_grad, other_grad):
    tokens, feats = own.shape
    rows, width = feats // 4, own_grad.shape[1]
    return pl.pallas_call(
        functools.partial(product_kernel, offset),
        out_shape=jax.ShapeDtypeStruct((rows, width), jnp.bfloat16),
        in_specs=[VMEM_BLOCK] * 4,
        out_specs=VMEM_BLOCK,
        cost_estimate=pl.CostEstimate(
            flops=4 * tokens * rows * width, bytes_accessed=rows * (4 * tokens + 2 * width), transcendentals=0
        ),
        compiler_params=pltpu.CompilerParams(vmem_limit_bytes=12 * 1024 * 1024),
    )(own, other, own_grad, other_grad)


def total_of(arrays):
    total = arrays[0].astype(jnp.float32)
    for array in arrays[1:]:
        total = total + array.astype(jnp.float32)
    return total.astype(jnp.bfloat16)


def rows_of_both(owned_ref, arrived_ref):
    keys_here = coordinates()[3]
    owned, arrived = owned_ref[...], arrived_ref[...]
    return jnp.where(keys_here, owned, arrived), jnp.where(keys_here, arrived, owned)


def told_kernel(owned_ref, arrived_ref, key_weight_ref, value_weight_ref, gain_ref, told_ref):
    key_part, value_part = rows_of_both(owned_ref, arrived_ref)
    rows = key_part.shape[0]
    z_lo = coordinates()[2]
    node, fsdp = lax.axis_index("node"), lax.axis_index("fsdp")
    here = pl.ds(pl.multiple_of(fsdp * rows, rows), rows)
    products = key_part * key_weight_ref[here, :].astype(jnp.float32)
    products += value_part * value_weight_ref[here, :].astype(jnp.float32)
    gain_column = jnp.sum(products, axis=1, keepdims=True)
    lane = lax.broadcasted_iota(jnp.int32, (rows, TILE), 1)
    row = lax.broadcasted_iota(jnp.int32, (rows, TILE), 0)
    terms = jnp.sum(jnp.where(lane == z_lo * rows + row, gain_column, 0.0), axis=0, keepdims=True)
    terms = terms / gain_ref[pl.ds((node * NX * NZL + fsdp) // NZL, 1), :]
    key_peak = jnp.max(jnp.abs(key_part))
    value_peak = jnp.max(jnp.abs(value_part))
    free = jnp.where(z_lo < NZL // 2, TILE // 2, 0)
    lane = lane[:1]
    terms = jnp.where(lane == free, key_peak, terms)
    told_ref[...] = jnp.where(lane == free + 1, value_peak, terms)


def output_kernel(owned_ref, arrived_ref, heard_ref, key_scaled_ref, value_scaled_ref, amax_ref, gain_grad_ref):
    key_part, value_part = rows_of_both(owned_ref, arrived_ref)
    heard = heard_ref[...]
    lane = lax.broadcasted_iota(jnp.int32, heard.shape, 1)
    row = lax.broadcasted_iota(jnp.int32, heard.shape, 0)
    is_gain = (row % NZL < NZL // 2) == (lane < TILE // 2)
    gain_grad_ref[...] = jnp.sum(jnp.where(is_gain, heard, 0.0).reshape(-1, NZL, TILE), axis=1)
    peaks = jnp.max(jnp.where(is_gain, 0.0, heard), axis=0, keepdims=True)
    place = lane[:1] % (TILE // 2)
    for which, (part, out_ref) in enumerate(((key_part, key_scaled_ref), (value_part, value_scaled_ref))):
        peak = jnp.max(jnp.where(place == which, peaks, 0.0), axis=1, keepdims=True)
        out_ref[...] = part * (6.0 / (peak + 1e-06))
        amax_ref[which] = peak[0, 0]


def tell(owned, arrived, key_weight, value_weight, gain):
    return pl.pallas_call(
        told_kernel,
        out_shape=jax.ShapeDtypeStruct((1, TILE), jnp.float32),
        in_specs=[VMEM_BLOCK] * 5,
        out_specs=VMEM_BLOCK,
        compiler_params=SMALL,
    )(owned, arrived, key_weight, value_weight, gain)


def outputs(owned, arrived, heard):
    return pl.pallas_call(
        output_kernel,
        out_shape=(
            jax.ShapeDtypeStruct(owned.shape, jnp.float32),
            jax.ShapeDtypeStruct(owned.shape, jnp.float32),
            jax.ShapeDtypeStruct((2,), jnp.float32),
            jax.ShapeDtypeStruct((heard.shape[0] // NZL, TILE), jnp.float32),
        ),
        in_specs=[VMEM_BLOCK] * 3,
        out_specs=(VMEM_BLOCK, VMEM_BLOCK, SMEM_BLOCK, VMEM_BLOCK),
        compiler_params=SMALL,
    )(owned, arrived, heard)


def per_device(hidden_in, inv_rms, norm_gain, key_grad, value_grad, key_weight, value_weight):
    width = key_grad.shape[1]
    own_grad, sent_grad = columns_of(key_grad, value_grad)
    other_grad = lax.ppermute(sent_grad, ALL, SWAP)
    scaled = hidden_in.astype(jnp.float32) * inv_rms.astype(jnp.float32)[:, None]
    own = (scaled * norm_gain[None, :]).astype(jnp.bfloat16)
    other = lax.ppermute(own, ALL, SWAP)
    chunks = []
    for offset in (2, 1, 3, 0):
        chunk = chunk_product(offset, own, other, own_grad, other_grad)
        if offset:
            chunk = lax.ppermute(chunk, ALL, plane_pairs(0, offset))
        chunks.append(chunk.reshape(4, -1, width))
    planes = []
    for offset in (2, 1, 3, 0):
        line_sum = total_of([chunk[offset] for chunk in chunks])
        if offset:
            line_sum = lax.ppermute(line_sum, ALL, plane_pairs(1, offset))
        planes.append(line_sum)
    plane_sum = total_of(planes).reshape(NZH * NZL, -1, width)
    heard = lax.all_to_all(plane_sum, ALL, 0, 0, tiled=True, axis_index_groups=z_groups())
    owned = jnp.sum(heard.astype(jnp.float32), axis=0)
    arrived = lax.ppermute(owned, ALL, SWAP)
    told = tell(owned, arrived, key_weight, value_weight, norm_gain.reshape(-1, TILE))
    owners = lax.axis_size("node") * lax.axis_size("fsdp")
    heard = lax.all_to_all(jnp.broadcast_to(told, (owners, TILE)), OWNERS, 0, 0, tiled=True)
    key_scaled, value_scaled, grad_amax, gain_grad = outputs(owned, arrived, heard)
    return (key_scaled, value_scaled, grad_amax, gain_grad.reshape(-1))


def solution(mesh):
    return jax.shard_map(
        per_device,
        mesh=mesh,
        in_specs=(
            P(("node", "fsdp", "rep"), None),
            P(("node", "fsdp", "rep")),
            P(),
            P(("node", "fsdp", "rep"), None),
            P(("node", "fsdp", "rep"), None),
            P("node", None),
            P("node", None),
        ),
        out_specs=(P(("node", "fsdp"), None), P(("node", "fsdp"), None), P(), P()),
        check_vma=False,
    )
```

time: 139 us -> 125 us (0.90)
  Pallas kernels: 15.8 us -> 4.19 us
  waiting for transfers between devices: 18.3 us -> 26.5 us
  blocking collectives: 60.4 us -> 53.4 us
  starting transfers between devices: 30.4 us -> 35.4 us
  other arithmetic: 8.41 us -> 3.65 us
  local copies, waits for them, and re-layouts: 2.13 us -> 0.1 us
  between operations: 2.3 us -> 0.82 us
    pallas_call x4 -> x7, Pallas kernels: 15.8 us -> 4.19 us  [the longest x4 3.22 us: chunk_product(): pl.pallas_call(functools.partial(product_kernel, offset), out_shape=jax.S...]
    ppermute x3, waiting for transfers between devices: 9.47 us -> 17.7 us  [per_device(): chunk = lax.ppermute(chunk, ALL, plane_pairs(0, offset))]
    all_to_all x1, blocking collectives: 31.9 us -> 25.5 us  [per_device(): lax.all_to_all(plane_sum, ALL, 0, 0, tiled=True, axis_index_groups=z_grou...]
    ppermute x1, starting transfers between devices: 3.34 us -> 8.96 us  [per_device(): arrived = lax.ppermute(owned, ALL, SWAP)]
    convert_element_type x0 -> x2, other arithmetic: none -> 2.93 us  [the longest x1 2.27 us: per_device(): own = (scaled * norm_gain[None, :]).astype(jnp.bfloat16)]
    convert_element_type x2, other arithmetic: 3.35 us -> 0.68 us  [total_of(): return total.astype(jnp.bfloat16)]
    concatenate x2 -> x0, other arithmetic: 1.43 us -> none  [the longest x1 1.37 us: per_device(): jnp.concatenate([gain_local, peaks, jnp.zeros((TILE - rows - 2,), jnp.flo...]
    reduce_sum x1 -> x0, other arithmetic: 1.4 us -> none  [per_device(): jnp.sum(value_part * value_rows, axis=1)]
  transfers between devices with their start and end apart: 9 -> 9, of which waited for: 7 -> 7; matrix products, arithmetic and copies ran while one was open for 2% -> 0% of each run, Pallas kernels for 8% -> 2%
where the time goes in v3:
time: 125 us; the launch traced here: 124 us
  blocking collectives  53.4 us (43%)
  starting transfers between devices  35.4 us (28%)
  waiting for transfers between devices  26.5 us (21%)
  Pallas kernels  4.19 us (3%)
  other arithmetic  3.65 us (3%)
    all_to_all x1, blocking collectives, per_device(): lax.all_to_all(jnp.broadcast_to(told, (owners, TILE)), OWNERS, 0, 0, tile...  27.9 us
    all_to_all x1, blocking collectives, per_device(): lax.all_to_all(plane_sum, ALL, 0, 0, tiled=True, axis_index_groups=z_grou...  25.5 us
    ppermute x3, waiting for transfers between devices, per_device(): chunk = lax.ppermute(chunk, ALL, plane_pairs(0, offset))  17.7 us
    ppermute x1, starting transfers between devices, per_device(): arrived = lax.ppermute(owned, ALL, SWAP)  8.96 us
    ppermute x1, starting transfers between devices, per_device(): other = lax.ppermute(own, ALL, SWAP)  8.79 us
    ppermute x3, starting transfers between devices, per_device(): chunk = lax.ppermute(chunk, ALL, plane_pairs(0, offset))  8.41 us
    ppermute x3, starting transfers between devices, per_device(): line_sum = lax.ppermute(line_sum, ALL, plane_pairs(1, offset))  7.33 us
    ppermute x3, waiting for transfers between devices, per_device(): line_sum = lax.ppermute(line_sum, ALL, plane_pairs(1, offset))  5.82 us
  transfers between devices with their start and end apart: 9, of which 7 were waited for; matrix products, arithmetic and copies ran while one was open for 0% of the time, Pallas kernels for 2%

profile of v3, /device:TPU:1, one launch (start us, length us, event | category | flops | bytes accessed | tf_op | source)
XLA Modules:
  0.0 124.0 jit_solution(11061658932641858609)
XLA Ops:
  0.6 0.7 convert_element_type.88
  1.3 0.0 copy-start.2
  1.3 0.0 copy-start.3
  1.3 2.3 %multiply_convert_fusion.own_ref = bf16[256,4096]{1,0:T(8,128)(2,1)S(1)} fusion(bf16[256,4096]{1,0:T(8,128)(2,1)} %param.7, f32[4096]{0:T(1024)} %param.9, f32[256]{0:T(256)S(1)} %convert_element_type.88), kind=kLoop, calls=%fused_computation | loop fusion | flops 4194304 | bytes 4211712 | tf_op jit(solution)/shard_map/convert_element_type | solution.py:178
  3.6 8.8 %collective-permute-start = (bf16[256,4096]{1,0:T(8,128)(2,1)S(1)}, bf16[256,4096]{1,0:T(8,128)(2,1)S(1)}, u32[]{:S(2)}, u32[]{:S(2)}) collective-permute-start(bf16[256,4096]{1,0:T(8,128)(2,1)S(1)} %multiply_convert_fusion.own_ref), channel_id=1, source_target_pairs={{0,1},{1,0},{2,3},{3,2},{4,5},{5,4},{6,7},{7,6},{8,9},{9,8},{10,11... | collective-permute-start | bytes 6291464 | tf_op jit(solution)/shard_map/ppermute | solution.py:179
  12.4 0.0 copy-done.2
  12.4 0.0 copy-done.3
  12.4 0.1 shard_map.102
  12.4 1.9 %collective-permute-start.1 = (bf16[256,512]{1,0:T(8,128)(2,1)S(1)}, bf16[256,512]{1,0:T(8,128)(2,1)S(1)}, u32[]{:S(2)}, u32[]{:S(2)}) collective-permute-start(bf16[256,512]{1,0:T(8,128)(2,1)S(1)} %get-tuple-element.11), channel_id=1, source_target_pairs={{0,1},{1,0},{2,3},{3,2},{4,5},{5,4},{6,7},{7,6},{8,9},{9,8},{10,11... | collective-permute-start | bytes 786440 | tf_op jit(solution)/shard_map/ppermute | solution.py:176
  14.4 2.1 %collective-permute-done.1.other_grad_ref = bf16[256,512]{1,0:T(8,128)(2,1)S(1)} collective-permute-done((bf16[256,512]{1,0:T(8,128)(2,1)S(1)}, bf16[256,512]{1,0:T(8,128)(2,1)S(1)}, u32[]{:S(2)}, u32[]{:S(2)}) %collective-permute-start.1) | collective-permute-done | bytes 262176 | tf_op jit(solution)/shard_map/ppermute | solution.py:176
  16.5 0.0 collective-permute-done.other_ref
  16.5 0.8 shard_map.103
  17.3 1.9 %collective-permute-start.2 = (bf16[1024,512]{1,0:T(8,128)(2,1)S(1)}, bf16[1024,512]{1,0:T(8,128)(2,1)S(1)}, u32[]{:S(2)}, u32[]{:S(2)}) collective-permute-start(bf16[1024,512]{1,0:T(8,128)(2,1)S(1)} %shard_map.103), channel_id=1, source_target_pairs={{0,32},{1,257},{2,34},{3,259},{4,36},{5,261},{6,38},{7,263},{8,40}... | collective-permute-start | bytes 3145736 | tf_op jit(solution)/shard_map/ppermute | solution.py:184
  19.3 0.8 shard_map.104
  20.1 1.9 %collective-permute-start.3 = (bf16[1024,512]{1,0:T(8,128)(2,1)S(1)}, bf16[1024,512]{1,0:T(8,128)(2,1)S(1)}, u32[]{:S(2)}, u32[]{:S(2)}) collective-permute-start(bf16[1024,512]{1,0:T(8,128)(2,1)S(1)} %shard_map.104), channel_id=1, source_target_pairs={{0,16},{1,129},{2,18},{3,131},{4,20},{5,133},{6,22},{7,135},{8,24}... | collective-permute-start | bytes 3145736 | tf_op jit(solution)/shard_map/ppermute | solution.py:184
  22.0 0.8 shard_map.105
  22.8 4.6 %collective-permute-start.4 = (bf16[1024,512]{1,0:T(8,128)(2,1)S(1)}, bf16[1024,512]{1,0:T(8,128)(2,1)S(1)}, u32[]{:S(2)}, u32[]{:S(2)}) collective-permute-start(bf16[1024,512]{1,0:T(8,128)(2,1)S(1)} %shard_map.105), channel_id=1, source_target_pairs={{0,48},{1,385},{2,50},{3,387},{4,52},{5,389},{6,54},{7,391},{8,56}... | collective-permute-start | bytes 3145736 | tf_op jit(solution)/shard_map/ppermute | solution.py:184
  27.4 0.8 shard_map.106
  28.2 6.5 %collective-permute-done.2 = bf16[1024,512]{1,0:T(8,128)(2,1)S(1)} collective-permute-done((bf16[1024,512]{1,0:T(8,128)(2,1)S(1)}, bf16[1024,512]{1,0:T(8,128)(2,1)S(1)}, u32[]{:S(2)}, u32[]{:S(2)}) %collective-permute-start.2) | collective-permute-done | bytes 1048608 | tf_op jit(solution)/shard_map/ppermute | solution.py:184
  34.7 11.2 %collective-permute-done.3 = bf16[1024,512]{1,0:T(8,128)(2,1)S(1)} collective-permute-done((bf16[1024,512]{1,0:T(8,128)(2,1)S(1)}, bf16[1024,512]{1,0:T(8,128)(2,1)S(1)}, u32[]{:S(2)}, u32[]{:S(2)}) %collective-permute-start.3) | collective-permute-done | bytes 1048608 | tf_op jit(solution)/shard_map/ppermute | solution.py:184
  45.9 0.0 collective-permute-done.4
  45.9 0.4 add_convert_fusion.4
  46.3 0.0 copy-start
  46.4 0.0 copy-start.1
  46.4 0.0 copy-start.4
  46.4 2.1 %collective-permute-start.5 = (bf16[256,512]{1,0:T(8,128)(2,1)S(1)}, bf16[256,512]{1,0:T(8,128)(2,1)S(1)}, u32[]{:S(2)}, u32[]{:S(2)}) collective-permute-start(bf16[256,512]{1,0:T(8,128)(2,1)S(1)} %get-tuple-element.16), channel_id=1, source_target_pairs={{0,256},{1,33},{2,258},{3,35},{4,260},{5,37},{6,262},{7,39},{8,264... | collective-permute-start | bytes 786440 | tf_op jit(solution)/shard_map/ppermute | solution.py:190
  48.4 1.9 %collective-permute-start.7 = (bf16[256,512]{1,0:T(8,128)(2,1)S(1)}, bf16[256,512]{1,0:T(8,128)(2,1)S(1)}, u32[]{:S(2)}, u32[]{:S(2)}) collective-permute-start(bf16[256,512]{1,0:T(8,128)(2,1)S(1)} %get-tuple-element.17), channel_id=1, source_target_pairs={{0,384},{1,49},{2,386},{3,51},{4,388},{5,53},{6,390},{7,55},{8,392... | collective-permute-start | bytes 786440 | tf_op jit(solution)/shard_map/ppermute | solution.py:190
  50.4 3.4 %collective-permute-start.6 = (bf16[256,512]{1,0:T(8,128)(2,1)S(1)}, bf16[256,512]{1,0:T(8,128)(2,1)S(1)}, u32[]{:S(2)}, u32[]{:S(2)}) collective-permute-start(bf16[256,512]{1,0:T(8,128)(2,1)S(1)} %get-tuple-element.18), channel_id=1, source_target_pairs={{0,128},{1,17},{2,130},{3,19},{4,132},{5,21},{6,134},{7,23},{8,136... | collective-permute-start | bytes 786440 | tf_op jit(solution)/shard_map/ppermute | solution.py:190
  53.7 1.7 %collective-permute-done.5 = bf16[256,512]{1,0:T(8,128)(2,1)S(1)} collective-permute-done((bf16[256,512]{1,0:T(8,128)(2,1)S(1)}, bf16[256,512]{1,0:T(8,128)(2,1)S(1)}, u32[]{:S(2)}, u32[]{:S(2)}) %collective-permute-start.5) | collective-permute-done | bytes 262176 | tf_op jit(solution)/shard_map/ppermute | solution.py:190
  55.4 0.4 collective-permute-done.7
  55.9 3.7 %collective-permute-done.6 = bf16[256,512]{1,0:T(8,128)(2,1)S(1)} collective-permute-done((bf16[256,512]{1,0:T(8,128)(2,1)S(1)}, bf16[256,512]{1,0:T(8,128)(2,1)S(1)}, u32[]{:S(2)}, u32[]{:S(2)}) %collective-permute-start.6) | collective-permute-done | bytes 262176 | tf_op jit(solution)/shard_map/ppermute | solution.py:190
  59.6 0.2 add_convert_fusion
  59.8 25.5 %all_to_all.13 = bf16[16,16,512]{2,1,0:T(8,128)(2,1)S(1)} all-to-all(bf16[16,16,512]{2,1,0:T(8,128)(2,1)S(1)} %bitcast.8), channel_id=1, replica_groups={{0,2,4,6,8,10,12,14,64,66,68,70,72,74,76,78},{1,3,5,7,9,11,13,15,65,67,..., dimensions={0} | all-to-all | bytes 524288 | tf_op jit(solution)/shard_map/all_to_all | solution.py:193
  85.4 9.0 %collective-permute-start.8 = (f32[16,512]{1,0:T(8,128)S(1)}, f32[16,512]{1,0:T(8,128)S(1)}, u32[]{:S(2)}, u32[]{:S(2)}) collective-permute-start(f32[16,512]{1,0:T(8,128)S(1)} %convert_reduce_fusion.owned_ref), channel_id=1, source_target_pairs={{0,1},{1,0},{2,3},{3,2},{4,5},{5,4},{6,7},{7,6},{8,9},{9,8},{10,11... | collective-permute-start | bytes 98312 | tf_op jit(solution)/shard_map/ppermute | solution.py:195
  94.3 0.8 collective-permute-done.8.arrived_ref
  95.2 0.0 copy-done
  95.2 0.0 copy-done.1
  95.2 0.0 copy-done.4
  95.2 0.1 shard_map.107
  95.3 0.1 broadcast_in_dim.2
  95.4 27.9 %all_to_all.14 = f32[256,1,128]{2,1,0:T(1,128)S(1)} all-to-all(f32[256,1,128]{2,1,0:T(1,128)S(1)} %broadcast_in_dim.2), channel_id=1, replica_groups=mesh['node'=8,'fsdp'=32,'rep'=2] {'node','fsdp'}, dimensions={0} | all-to-all | bytes 262144 | tf_op jit(solution)/shard_map/all_to_all | solution.py:198
  123.3 0.8 shard_map.108
  (1 shorter events, 0.0 us)
Async XLA Ops:
  1.3 11.1 %copy-start.2 = (bf16[256,512]{1,0:T(8,128)(2,1)S(1)}, bf16[256,512]{1,0:T(8,128)(2,1)}, u32[]{:S(2)}) copy-start(bf16[256,512]{1,0:T(8,128)(2,1)} %key_grad_ref.1) | copy-start | bytes 786436
  1.3 11.1 %copy-start.3 = (bf16[256,512]{1,0:T(8,128)(2,1)S(1)}, bf16[256,512]{1,0:T(8,128)(2,1)}, u32[]{:S(2)}) copy-start(bf16[256,512]{1,0:T(8,128)(2,1)} %value_grad_ref.1) | copy-start | bytes 786436
  3.6 12.9 %collective-permute-start = (bf16[256,4096]{1,0:T(8,128)(2,1)S(1)}, bf16[256,4096]{1,0:T(8,128)(2,1)S(1)}, u32[]{:S(2)}, u32[]{:S(2)}) collective-permute-start(bf16[256,4096]{1,0:T(8,128)(2,1)S(1)} %multiply_convert_fusion.own_ref), channel_id=1, source_target_pairs={{0,1},{1,0},{2,3},{3,2},{4,5},{5,4},{6,7},{7,6},{8,9},{9,8},{10,11... | collective-permute-start | bytes 6291464 | tf_op jit(solution)/shard_map/ppermute | solution.py:179
  12.4 4.1 %collective-permute-start.1 = (bf16[256,512]{1,0:T(8,128)(2,1)S(1)}, bf16[256,512]{1,0:T(8,128)(2,1)S(1)}, u32[]{:S(2)}, u32[]{:S(2)}) collective-permute-start(bf16[256,512]{1,0:T(8,128)(2,1)S(1)} %get-tuple-element.11), channel_id=1, source_target_pairs={{0,1},{1,0},{2,3},{3,2},{4,5},{5,4},{6,7},{7,6},{8,9},{9,8},{10,11... | collective-permute-start | bytes 786440 | tf_op jit(solution)/shard_map/ppermute | solution.py:176
  17.3 17.4 %collective-permute-start.2 = (bf16[1024,512]{1,0:T(8,128)(2,1)S(1)}, bf16[1024,512]{1,0:T(8,128)(2,1)S(1)}, u32[]{:S(2)}, u32[]{:S(2)}) collective-permute-start(bf16[1024,512]{1,0:T(8,128)(2,1)S(1)} %shard_map.103), channel_id=1, source_target_pairs={{0,32},{1,257},{2,34},{3,259},{4,36},{5,261},{6,38},{7,263},{8,40}... | collective-permute-start | bytes 3145736 | tf_op jit(solution)/shard_map/ppermute | solution.py:184
  20.1 25.8 %collective-permute-start.3 = (bf16[1024,512]{1,0:T(8,128)(2,1)S(1)}, bf16[1024,512]{1,0:T(8,128)(2,1)S(1)}, u32[]{:S(2)}, u32[]{:S(2)}) collective-permute-start(bf16[1024,512]{1,0:T(8,128)(2,1)S(1)} %shard_map.104), channel_id=1, source_target_pairs={{0,16},{1,129},{2,18},{3,131},{4,20},{5,133},{6,22},{7,135},{8,24}... | collective-permute-start | bytes 3145736 | tf_op jit(solution)/shard_map/ppermute | solution.py:184
  22.8 23.1 %collective-permute-start.4 = (bf16[1024,512]{1,0:T(8,128)(2,1)S(1)}, bf16[1024,512]{1,0:T(8,128)(2,1)S(1)}, u32[]{:S(2)}, u32[]{:S(2)}) collective-permute-start(bf16[1024,512]{1,0:T(8,128)(2,1)S(1)} %shard_map.105), channel_id=1, source_target_pairs={{0,48},{1,385},{2,50},{3,387},{4,52},{5,389},{6,54},{7,391},{8,56}... | collective-permute-start | bytes 3145736 | tf_op jit(solution)/shard_map/ppermute | solution.py:184
  46.3 48.8 %copy-start = (bf16[512,512]{1,0:T(8,128)(2,1)S(1)}, bf16[512,512]{1,0:T(8,128)(2,1)}, u32[]{:S(2)}) copy-start(bf16[512,512]{1,0:T(8,128)(2,1)} %key_weight_ref.1) | copy-start | bytes 1572868
  46.4 48.8 %copy-start.1 = (bf16[512,512]{1,0:T(8,128)(2,1)S(1)}, bf16[512,512]{1,0:T(8,128)(2,1)}, u32[]{:S(2)}) copy-start(bf16[512,512]{1,0:T(8,128)(2,1)} %value_weight_ref.1) | copy-start | bytes 1572868
  46.4 48.8 %copy-start.4 = (f32[4096]{0:T(1024)S(1)}, f32[4096]{0:T(1024)}, u32[]{:S(2)}) copy-start(f32[4096]{0:T(1024)} %param.9) | copy-start | bytes 49156
  46.4 9.0 %collective-permute-start.5 = (bf16[256,512]{1,0:T(8,128)(2,1)S(1)}, bf16[256,512]{1,0:T(8,128)(2,1)S(1)}, u32[]{:S(2)}, u32[]{:S(2)}) collective-permute-start(bf16[256,512]{1,0:T(8,128)(2,1)S(1)} %get-tuple-element.16), channel_id=1, source_target_pairs={{0,256},{1,33},{2,258},{3,35},{4,260},{5,37},{6,262},{7,39},{8,264... | collective-permute-start | bytes 786440 | tf_op jit(solution)/shard_map/ppermute | solution.py:190
  48.4 7.4 %collective-permute-start.7 = (bf16[256,512]{1,0:T(8,128)(2,1)S(1)}, bf16[256,512]{1,0:T(8,128)(2,1)S(1)}, u32[]{:S(2)}, u32[]{:S(2)}) collective-permute-start(bf16[256,512]{1,0:T(8,128)(2,1)S(1)} %get-tuple-element.17), channel_id=1, source_target_pairs={{0,384},{1,49},{2,386},{3,51},{4,388},{5,53},{6,390},{7,55},{8,392... | collective-permute-start | bytes 786440 | tf_op jit(solution)/shard_map/ppermute | solution.py:190
  50.4 9.2 %collective-permute-start.6 = (bf16[256,512]{1,0:T(8,128)(2,1)S(1)}, bf16[256,512]{1,0:T(8,128)(2,1)S(1)}, u32[]{:S(2)}, u32[]{:S(2)}) collective-permute-start(bf16[256,512]{1,0:T(8,128)(2,1)S(1)} %get-tuple-element.18), channel_id=1, source_target_pairs={{0,128},{1,17},{2,130},{3,19},{4,132},{5,21},{6,134},{7,23},{8,136... | collective-permute-start | bytes 786440 | tf_op jit(solution)/shard_map/ppermute | solution.py:190
  85.4 9.8 %collective-permute-start.8 = (f32[16,512]{1,0:T(8,128)S(1)}, f32[16,512]{1,0:T(8,128)S(1)}, u32[]{:S(2)}, u32[]{:S(2)}) collective-permute-start(f32[16,512]{1,0:T(8,128)S(1)} %convert_reduce_fusion.owned_ref), channel_id=1, source_target_pairs={{0,1},{1,0},{2,3},{3,2},{4,5},{5,4},{6,7},{7,6},{8,9},{9,8},{10,11... | collective-permute-start | bytes 98312 | tf_op jit(solution)/shard_map/ppermute | solution.py:195

commit v4 on v3

--- a/solution.py
+++ b/solution.py
@@ -9,7 +9,6 @@
 from jax.sharding import PartitionSpec as P
 
 ALL = ("node", "fsdp", "rep")
-OWNERS = ("node", "fsdp")
 NY, NZH, NX, NZL, NC = 4, 2, 4, 8, 2
 INDEX = np.arange(NY * NZH * NX * NZL * NC).reshape(NY, NZH, NX, NZL, NC)
 TILE = 128
@@ -29,6 +28,13 @@
     return [
         [int(INDEX[y, z // NZL, x, z % NZL, c]) for z in range(NZH * NZL)]
         for y in range(NY) for x in range(NX) for c in range(NC)
+    ]
+
+
+def level_groups():
+    return [
+        [int(INDEX[y, zh, x, zl, c]) for y in range(NY) for x in range(NX) for c in range(NC)]
+        for zh in range(NZH) for zl in range(NZL)
     ]
 
 
@@ -103,71 +109,79 @@
     return total.astype(jnp.bfloat16)
 
 
-def rows_of_both(owned_ref, arrived_ref):
+BLOCKS = 8
+
+
+def told_kernel(owned_ref, key_weight_ref, value_weight_ref, gain_ref, told_ref):
+    x, y, z_lo, keys_here = coordinates()
+    owned = owned_ref[...]
+    rows = owned.shape[0]
+    fsdp = lax.axis_index("fsdp")
+    here = pl.ds(pl.multiple_of(fsdp * rows, rows), rows)
+    weight = jnp.where(keys_here, key_weight_ref[here, :], value_weight_ref[here, :]).astype(jnp.float32)
+    sums = jnp.sum(owned * weight, axis=1, keepdims=True)
+    gain_row = gain_ref[pl.ds(lax.axis_index("node") * (NX * NZL // BLOCKS) + x, 1), :]
+    lane = lax.broadcasted_iota(jnp.int32, (rows, TILE), 1)
+    row = lax.broadcasted_iota(jnp.int32, (rows, TILE), 0)
+    gains = jnp.sum(jnp.where(lane == z_lo * rows + row, gain_row, 0.0), axis=1, keepdims=True)
+    block = lax.rem(y * NX + x + z_lo, BLOCKS)
+    terms = jnp.where(lane == block * rows + row, sums / gains, 0.0)
+    told_ref[0:1, :] = jnp.sum(terms, axis=0, keepdims=True)
+    mine = lane[:1] == jnp.where(keys_here, 0, 1)
+    told_ref[1:2, :] = jnp.where(mine, jnp.max(jnp.abs(owned)), 0.0)
+
+
+def level_kernel(heard_ref, told_ref):
+    heard = heard_ref[...]
+    row = lax.broadcasted_iota(jnp.int32, heard.shape, 0)
+    terms = jnp.where(row % 2 == 0, heard, 0.0)
+    told_ref[0:2, :] = jnp.sum(terms.reshape(2, -1, TILE), axis=1)
+    told_ref[2:3, :] = jnp.max(jnp.where(row % 2 == 0, 0.0, heard), axis=0, keepdims=True)
+    told_ref[3:4, :] = jnp.zeros((1, TILE), jnp.float32)
+
+
+def output_kernel(owned_ref, arrived_ref, heard_ref, key_scaled_ref, value_scaled_ref, amax_ref, gain_grad_ref):
     keys_here = coordinates()[3]
     owned, arrived = owned_ref[...], arrived_ref[...]
-    return jnp.where(keys_here, owned, arrived), jnp.where(keys_here, arrived, owned)
-
-
-def told_kernel(owned_ref, arrived_ref, key_weight_ref, value_weight_ref, gain_ref, told_ref):
-    key_part, value_part = rows_of_both(owned_ref, arrived_ref)
-    rows = key_part.shape[0]
-    z_lo = coordinates()[2]
-    node, fsdp = lax.axis_index("node"), lax.axis_index("fsdp")
-    here = pl.ds(pl.multiple_of(fsdp * rows, rows), rows)
-    products = key_part * key_weight_ref[here, :].astype(jnp.float32)
-    products += value_part * value_weight_ref[here, :].astype(jnp.float32)
-    gain_column = jnp.sum(products, axis=1, keepdims=True)
-    lane = lax.broadcasted_iota(jnp.int32, (rows, TILE), 1)
-    row = lax.broadcasted_iota(jnp.int32, (rows, TILE), 0)
-    terms = jnp.sum(jnp.where(lane == z_lo * rows + row, gain_column, 0.0), axis=0, keepdims=True)
-    terms = terms / gain_ref[pl.ds((node * NX * NZL + fsdp) // NZL, 1), :]
-    key_peak = jnp.max(jnp.abs(key_part))
-    value_peak = jnp.max(jnp.abs(value_part))
-    free = jnp.where(z_lo < NZL // 2, TILE // 2, 0)
-    lane = lane[:1]
-    terms = jnp.where(lane == free, key_peak, terms)
-    told_ref[...] = jnp.where(lane == free + 1, value_peak, terms)
-
-
-def output_kernel(owned_ref, arrived_ref, heard_ref, key_scaled_ref, value_scaled_ref, amax_ref, gain_grad_ref):
-    key_part, value_part = rows_of_both(owned_ref, arrived_ref)
-    heard = heard_ref[...]
-    lane = lax.broadcasted_iota(jnp.int32, heard.shape, 1)
-    row = lax.broadcasted_iota(jnp.int32, heard.shape, 0)
-    is_gain = (row % NZL < NZL // 2) == (lane < TILE // 2)
-    gain_grad_ref[...] = jnp.sum(jnp.where(is_gain, heard, 0.0).reshape(-1, NZL, TILE), axis=1)
-    peaks = jnp.max(jnp.where(is_gain, 0.0, heard), axis=0, keepdims=True)
-    place = lane[:1] % (TILE // 2)
-    for which, (part, out_ref) in enumerate(((key_part, key_scaled_ref), (value_part, value_scaled_ref))):
-        peak = jnp.max(jnp.where(place == which, peaks, 0.0), axis=1, keepdims=True)
-        out_ref[...] = part * (6.0 / (peak + 1e-06))
+    span = TILE // BLOCKS
+    heard = heard_ref[...].reshape(NZH, NZL, 4, TILE)
+    lane_block = lax.broadcasted_iota(jnp.int32, heard.shape, 3) // span
+    z_lo = lax.broadcasted_iota(jnp.int32, heard.shape, 1)
+    for which in range(BLOCKS):
+        terms = jnp.sum(jnp.where(lane_block == (which + z_lo) % BLOCKS, heard, 0.0), axis=1)
+        for zh in range(NZH):
+            turned = pltpu.roll(terms[zh], (TILE - which * span) % TILE, 1)
+            for half in range(2):
+                y, x = (half * BLOCKS + which) // NX, which % NX
+                out_row = (y * NZH + zh) * NX + x
+                gain_grad_ref[out_row:out_row + 1, :] = turned[half:half + 1]
+    peaks = jnp.max(jnp.max(heard[:, :, 2:3, :], axis=1), axis=0)
+    lane = lax.broadcasted_iota(jnp.int32, peaks.shape, 1)
+    parts = ((owned, arrived, key_scaled_ref), (arrived, owned, value_scaled_ref))
+    for which, (of_keys, of_values, out_ref) in enumerate(parts):
+        peak = jnp.max(jnp.where(lane == which, peaks, 0.0), axis=1, keepdims=True)
+        out_ref[...] = jnp.where(keys_here, of_keys, of_values) * (6.0 / (peak + 1e-06))
         amax_ref[which] = peak[0, 0]
 
 
-def tell(owned, arrived, key_weight, value_weight, gain):
+def small_call(kernel, out_shape, out_specs, *operands):
     return pl.pallas_call(
-        told_kernel,
-        out_shape=jax.ShapeDtypeStruct((1, TILE), jnp.float32),
-        in_specs=[VMEM_BLOCK] * 5,
-        out_specs=VMEM_BLOCK,
+        kernel,
+        out_shape=out_shape,
+        in_specs=[VMEM_BLOCK] * len(operands),
+        out_specs=out_specs,
         compiler_params=SMALL,
-    )(owned, arrived, key_weight, value_weight, gain)
-
-
-def outputs(owned, arrived, heard):
-    return pl.pallas_call(
-        output_kernel,
-        out_shape=(
-            jax.ShapeDtypeStruct(owned.shape, jnp.float32),
-            jax.ShapeDtypeStruct(owned.shape, jnp.float32),
-            jax.ShapeDtypeStruct((2,), jnp.float32),
-            jax.ShapeDtypeStruct((heard.shape[0] // NZL, TILE), jnp.float32),
-        ),
-        in_specs=[VMEM_BLOCK] * 3,
-        out_specs=(VMEM_BLOCK, VMEM_BLOCK, SMEM_BLOCK, VMEM_BLOCK),
-        compiler_params=SMALL,
-    )(owned, arrived, heard)
+    )(*operands)
+
+
+def floats(*shape):
+    return jax.ShapeDtypeStruct(shape, jnp.float32)
+
+
+def told_to(groups, told):
+    everyone = jnp.broadcast_to(told[None], (len(groups[0]),) + told.shape)
+    heard = lax.all_to_all(everyone, ALL, 0, 0, tiled=True, axis_index_groups=groups)
+    return heard.reshape(-1, TILE)
 
 
 def per_device(hidden_in, inv_rms, norm_gain, key_grad, value_grad, key_weight, value_weight):
@@ -193,10 +207,16 @@
     heard = lax.all_to_all(plane_sum, ALL, 0, 0, tiled=True, axis_index_groups=z_groups())
     owned = jnp.sum(heard.astype(jnp.float32), axis=0)
     arrived = lax.ppermute(owned, ALL, SWAP)
-    told = tell(owned, arrived, key_weight, value_weight, norm_gain.reshape(-1, TILE))
-    owners = lax.axis_size("node") * lax.axis_size("fsdp")
-    heard = lax.all_to_all(jnp.broadcast_to(told, (owners, TILE)), OWNERS, 0, 0, tiled=True)
-    key_scaled, value_scaled, grad_amax, gain_grad = outputs(owned, arrived, heard)
+    gain_rows = norm_gain.reshape(-1, TILE)
+    told = small_call(told_kernel, floats(2, TILE), VMEM_BLOCK, owned, key_weight, value_weight, gain_rows)
+    told = small_call(level_kernel, floats(4, TILE), VMEM_BLOCK, told_to(level_groups(), told))
+    heard = told_to(z_groups(), told)
+    key_scaled, value_scaled, grad_amax, gain_grad = small_call(
+        output_kernel,
+        (floats(*owned.shape), floats(*owned.shape), floats(2), floats(*gain_rows.shape)),
+        (VMEM_BLOCK, VMEM_BLOCK, SMEM_BLOCK, VMEM_BLOCK),
+        owned, arrived, heard,
+    )
     return (key_scaled, value_scaled, grad_amax, gain_grad.reshape(-1))
 
 

time: 125 us -> 122 us (0.976)
  blocking collectives: 53.4 us -> 43.3 us
  waiting for transfers between devices: 26.5 us -> 34.5 us
    all_to_all x1, blocking collectives: 27.9 us -> 17.8 us  [told_to(): lax.all_to_all(everyone, ALL, 0, 0, tiled=True, axis_index_groups=groups)]
    all_to_all x0 -> x1, waiting for transfers between devices: none -> 8.04 us  [told_to(): lax.all_to_all(everyone, ALL, 0, 0, tiled=True, axis_index_groups=groups)]
    ppermute x1, starting transfers between devices: 8.96 us -> 2.58 us  [per_device(): arrived = lax.ppermute(owned, ALL, SWAP)]
    all_to_all x0 -> x1, starting transfers between devices: none -> 5.28 us  [told_to(): lax.all_to_all(everyone, ALL, 0, 0, tiled=True, axis_index_groups=groups)]
  transfers between devices with their start and end apart: 9 -> 10, of which waited for: 7 -> 8; matrix products, arithmetic and copies ran while one was open for 0% -> 0% of each run, Pallas kernels for 2% -> 2%
where the time goes in v4:
time: 122 us; the launch traced here: 121 us
  blocking collectives  43.3 us (35%)
  waiting for transfers between devices  34.5 us (28%)
  starting transfers between devices  34.3 us (28%)
  Pallas kernels  4.16 us (3%)
  other arithmetic  3.65 us (3%)
    all_to_all x1, blocking collectives, per_device(): lax.all_to_all(plane_sum, ALL, 0, 0, tiled=True, axis_index_groups=z_grou...  25.5 us
    all_to_all x1, blocking collectives, told_to(): lax.all_to_all(everyone, ALL, 0, 0, tiled=True, axis_index_groups=groups)  17.8 us
    ppermute x3, waiting for transfers between devices, per_device(): chunk = lax.ppermute(chunk, ALL, plane_pairs(0, offset))  17.7 us
    ppermute x1, starting transfers between devices, per_device(): other = lax.ppermute(own, ALL, SWAP)  8.79 us
    ppermute x3, starting transfers between devices, per_device(): chunk = lax.ppermute(chunk, ALL, plane_pairs(0, offset))  8.41 us
    all_to_all x1, waiting for transfers between devices, told_to(): lax.all_to_all(everyone, ALL, 0, 0, tiled=True, axis_index_groups=groups)  8.04 us
    ppermute x3, starting transfers between devices, per_device(): line_sum = lax.ppermute(line_sum, ALL, plane_pairs(1, offset))  7.33 us
    ppermute x3, waiting for transfers between devices, per_device(): line_sum = lax.ppermute(line_sum, ALL, plane_pairs(1, offset))  5.82 us
  transfers between devices with their start and end apart: 10, of which 8 were waited for; matrix products, arithmetic and copies ran while one was open for 0% of the time, Pallas kernels for 2%

profile of v4, /device:TPU:1, one launch (start us, length us, event | category | flops | bytes accessed | tf_op | source)
XLA Modules:
  0.0 121.5 jit_solution(16112944558439285559)
XLA Ops:
  0.6 0.7 convert_element_type.88
  1.3 0.0 copy-start.2
  1.3 0.0 copy-start.3
  1.3 2.3 %multiply_convert_fusion.own_ref = bf16[256,4096]{1,0:T(8,128)(2,1)S(1)} fusion(bf16[256,4096]{1,0:T(8,128)(2,1)} %param.7, f32[4096]{0:T(1024)} %param.9, f32[256]{0:T(256)S(1)} %convert_element_type.88), kind=kLoop, calls=%fused_computation | loop fusion | flops 4194304 | bytes 4211712 | tf_op jit(solution)/shard_map/convert_element_type | solution.py:192
  3.6 8.8 %collective-permute-start = (bf16[256,4096]{1,0:T(8,128)(2,1)S(1)}, bf16[256,4096]{1,0:T(8,128)(2,1)S(1)}, u32[]{:S(2)}, u32[]{:S(2)}) collective-permute-start(bf16[256,4096]{1,0:T(8,128)(2,1)S(1)} %multiply_convert_fusion.own_ref), channel_id=1, source_target_pairs={{0,1},{1,0},{2,3},{3,2},{4,5},{5,4},{6,7},{7,6},{8,9},{9,8},{10,11... | collective-permute-start | bytes 6291464 | tf_op jit(solution)/shard_map/ppermute | solution.py:193
  12.4 0.0 copy-done.2
  12.4 0.0 copy-done.3
  12.4 0.1 shard_map.102
  12.4 1.9 %collective-permute-start.1 = (bf16[256,512]{1,0:T(8,128)(2,1)S(1)}, bf16[256,512]{1,0:T(8,128)(2,1)S(1)}, u32[]{:S(2)}, u32[]{:S(2)}) collective-permute-start(bf16[256,512]{1,0:T(8,128)(2,1)S(1)} %get-tuple-element.11), channel_id=1, source_target_pairs={{0,1},{1,0},{2,3},{3,2},{4,5},{5,4},{6,7},{7,6},{8,9},{9,8},{10,11... | collective-permute-start | bytes 786440 | tf_op jit(solution)/shard_map/ppermute | solution.py:190
  14.4 2.1 %collective-permute-done.1.other_grad_ref = bf16[256,512]{1,0:T(8,128)(2,1)S(1)} collective-permute-done((bf16[256,512]{1,0:T(8,128)(2,1)S(1)}, bf16[256,512]{1,0:T(8,128)(2,1)S(1)}, u32[]{:S(2)}, u32[]{:S(2)}) %collective-permute-start.1) | collective-permute-done | bytes 262176 | tf_op jit(solution)/shard_map/ppermute | solution.py:190
  16.5 0.0 collective-permute-done.other_ref
  16.5 0.8 shard_map.103
  17.3 1.9 %collective-permute-start.2 = (bf16[1024,512]{1,0:T(8,128)(2,1)S(1)}, bf16[1024,512]{1,0:T(8,128)(2,1)S(1)}, u32[]{:S(2)}, u32[]{:S(2)}) collective-permute-start(bf16[1024,512]{1,0:T(8,128)(2,1)S(1)} %shard_map.103), channel_id=1, source_target_pairs={{0,32},{1,257},{2,34},{3,259},{4,36},{5,261},{6,38},{7,263},{8,40}... | collective-permute-start | bytes 3145736 | tf_op jit(solution)/shard_map/ppermute | solution.py:198
  19.3 0.8 shard_map.104
  20.1 1.9 %collective-permute-start.3 = (bf16[1024,512]{1,0:T(8,128)(2,1)S(1)}, bf16[1024,512]{1,0:T(8,128)(2,1)S(1)}, u32[]{:S(2)}, u32[]{:S(2)}) collective-permute-start(bf16[1024,512]{1,0:T(8,128)(2,1)S(1)} %shard_map.104), channel_id=1, source_target_pairs={{0,16},{1,129},{2,18},{3,131},{4,20},{5,133},{6,22},{7,135},{8,24}... | collective-permute-start | bytes 3145736 | tf_op jit(solution)/shard_map/ppermute | solution.py:198
  22.0 0.8 shard_map.105
  22.8 4.6 %collective-permute-start.4 = (bf16[1024,512]{1,0:T(8,128)(2,1)S(1)}, bf16[1024,512]{1,0:T(8,128)(2,1)S(1)}, u32[]{:S(2)}, u32[]{:S(2)}) collective-permute-start(bf16[1024,512]{1,0:T(8,128)(2,1)S(1)} %shard_map.105), channel_id=1, source_target_pairs={{0,48},{1,385},{2,50},{3,387},{4,52},{5,389},{6,54},{7,391},{8,56}... | collective-permute-start | bytes 3145736 | tf_op jit(solution)/shard_map/ppermute | solution.py:198
  27.4 0.8 shard_map.106
  28.2 6.5 %collective-permute-done.2 = bf16[1024,512]{1,0:T(8,128)(2,1)S(1)} collective-permute-done((bf16[1024,512]{1,0:T(8,128)(2,1)S(1)}, bf16[1024,512]{1,0:T(8,128)(2,1)S(1)}, u32[]{:S(2)}, u32[]{:S(2)}) %collective-permute-start.2) | collective-permute-done | bytes 1048608 | tf_op jit(solution)/shard_map/ppermute | solution.py:198
  34.7 11.2 %collective-permute-done.3 = bf16[1024,512]{1,0:T(8,128)(2,1)S(1)} collective-permute-done((bf16[1024,512]{1,0:T(8,128)(2,1)S(1)}, bf16[1024,512]{1,0:T(8,128)(2,1)S(1)}, u32[]{:S(2)}, u32[]{:S(2)}) %collective-permute-start.3) | collective-permute-done | bytes 1048608 | tf_op jit(solution)/shard_map/ppermute | solution.py:198
  45.9 0.0 collective-permute-done.4
  45.9 0.4 add_convert_fusion.4
  46.3 0.0 copy-start
  46.4 0.0 copy-start.1
  46.4 0.0 copy-start.4
  46.4 2.1 %collective-permute-start.5 = (bf16[256,512]{1,0:T(8,128)(2,1)S(1)}, bf16[256,512]{1,0:T(8,128)(2,1)S(1)}, u32[]{:S(2)}, u32[]{:S(2)}) collective-permute-start(bf16[256,512]{1,0:T(8,128)(2,1)S(1)} %get-tuple-element.16), channel_id=1, source_target_pairs={{0,256},{1,33},{2,258},{3,35},{4,260},{5,37},{6,262},{7,39},{8,264... | collective-permute-start | bytes 786440 | tf_op jit(solution)/shard_map/ppermute | solution.py:204
  48.4 1.9 %collective-permute-start.7 = (bf16[256,512]{1,0:T(8,128)(2,1)S(1)}, bf16[256,512]{1,0:T(8,128)(2,1)S(1)}, u32[]{:S(2)}, u32[]{:S(2)}) collective-permute-start(bf16[256,512]{1,0:T(8,128)(2,1)S(1)} %get-tuple-element.17), channel_id=1, source_target_pairs={{0,384},{1,49},{2,386},{3,51},{4,388},{5,53},{6,390},{7,55},{8,392... | collective-permute-start | bytes 786440 | tf_op jit(solution)/shard_map/ppermute | solution.py:204
  50.4 3.4 %collective-permute-start.6 = (bf16[256,512]{1,0:T(8,128)(2,1)S(1)}, bf16[256,512]{1,0:T(8,128)(2,1)S(1)}, u32[]{:S(2)}, u32[]{:S(2)}) collective-permute-start(bf16[256,512]{1,0:T(8,128)(2,1)S(1)} %get-tuple-element.18), channel_id=1, source_target_pairs={{0,128},{1,17},{2,130},{3,19},{4,132},{5,21},{6,134},{7,23},{8,136... | collective-permute-start | bytes 786440 | tf_op jit(solution)/shard_map/ppermute | solution.py:204
  53.7 1.7 %collective-permute-done.5 = bf16[256,512]{1,0:T(8,128)(2,1)S(1)} collective-permute-done((bf16[256,512]{1,0:T(8,128)(2,1)S(1)}, bf16[256,512]{1,0:T(8,128)(2,1)S(1)}, u32[]{:S(2)}, u32[]{:S(2)}) %collective-permute-start.5) | collective-permute-done | bytes 262176 | tf_op jit(solution)/shard_map/ppermute | solution.py:204
  55.4 0.4 collective-permute-done.7
  55.9 3.7 %collective-permute-done.6 = bf16[256,512]{1,0:T(8,128)(2,1)S(1)} collective-permute-done((bf16[256,512]{1,0:T(8,128)(2,1)S(1)}, bf16[256,512]{1,0:T(8,128)(2,1)S(1)}, u32[]{:S(2)}, u32[]{:S(2)}) %collective-permute-start.6) | collective-permute-done | bytes 262176 | tf_op jit(solution)/shard_map/ppermute | solution.py:204
  59.6 0.2 add_convert_fusion
  59.8 25.5 %all_to_all.15 = bf16[16,16,512]{2,1,0:T(8,128)(2,1)S(1)} all-to-all(bf16[16,16,512]{2,1,0:T(8,128)(2,1)S(1)} %bitcast.8), channel_id=1, replica_groups={{0,2,4,6,8,10,12,14,64,66,68,70,72,74,76,78},{1,3,5,7,9,11,13,15,65,67,..., dimensions={0} | all-to-all | bytes 524288 | tf_op jit(solution)/shard_map/all_to_all | solution.py:207
  85.4 0.0 copy-done
  85.4 0.0 copy-done.1
  85.4 0.0 copy-done.4
  85.4 0.1 shard_map.107
  85.5 17.8 %all_to_all.16 = f32[32,2,128]{2,1,0:T(2,128)S(1)} all-to-all(f32[32,2,128]{2,1,0:T(2,128)S(1)} %broadcast_in_dim.4), channel_id=1, replica_groups={{0,1,16,17,32,33,48,49,128,129,144,145,160,161,176,177,256,257,272,273,..., dimensions={0} | all-to-all | bytes 65536 | tf_op jit(solution)/shard_map/all_to_all | solution.py:183
  103.4 0.6 broadcast_in_dim.5
  104.0 5.3 %all-to-all-start.2 = ((f32[16,4,128]{2,1,0:T(4,128)}), f32[16,4,128]{2,1,0:T(4,128)S(1)}, u32[]{:S(2)}, u32[]{:S(2)}) async-start(f32[16,4,128]{2,1,0:T(4,128)} %broadcast_in_dim.5), calls=%async_computation.2 | async-start | bytes 65536 | tf_op jit(solution)/shard_map/all_to_all | solution.py:183
  109.3 2.6 %collective-permute-start.8 = (f32[16,512]{1,0:T(8,128)S(1)}, f32[16,512]{1,0:T(8,128)S(1)}, u32[]{:S(2)}, u32[]{:S(2)}) collective-permute-start(f32[16,512]{1,0:T(8,128)S(1)} %convert_reduce_fusion.owned_ref), channel_id=1, source_target_pairs={{0,1},{1,0},{2,3},{3,2},{4,5},{5,4},{6,7},{7,6},{8,9},{9,8},{10,11... | collective-permute-start | bytes 98312 | tf_op jit(solution)/shard_map/ppermute | solution.py:209
  111.9 0.8 collective-permute-done.8.arrived_ref
  112.7 8.0 %all-to-all-done.2 = f32[16,4,128]{2,1,0:T(4,128)S(1)} async-done(((f32[16,4,128]{2,1,0:T(4,128)}), f32[16,4,128]{2,1,0:T(4,128)S(1)}, u32[]{:S(2)}, u32[]{:S(2)}) %all-to-all-start.2) | async-done | bytes 32800 | tf_op jit(solution)/shard_map/all_to_all | solution.py:183
  120.8 0.7 shard_map.109
  (3 shorter events, 0.1 us)
Async XLA Ops:
  1.3 11.1 %copy-start.2 = (bf16[256,512]{1,0:T(8,128)(2,1)S(1)}, bf16[256,512]{1,0:T(8,128)(2,1)}, u32[]{:S(2)}) copy-start(bf16[256,512]{1,0:T(8,128)(2,1)} %key_grad_ref.1) | copy-start | bytes 786436
  1.3 11.1 %copy-start.3 = (bf16[256,512]{1,0:T(8,128)(2,1)S(1)}, bf16[256,512]{1,0:T(8,128)(2,1)}, u32[]{:S(2)}) copy-start(bf16[256,512]{1,0:T(8,128)(2,1)} %value_grad_ref.1) | copy-start | bytes 786436
  3.6 12.9 %collective-permute-start = (bf16[256,4096]{1,0:T(8,128)(2,1)S(1)}, bf16[256,4096]{1,0:T(8,128)(2,1)S(1)}, u32[]{:S(2)}, u32[]{:S(2)}) collective-permute-start(bf16[256,4096]{1,0:T(8,128)(2,1)S(1)} %multiply_convert_fusion.own_ref), channel_id=1, source_target_pairs={{0,1},{1,0},{2,3},{3,2},{4,5},{5,4},{6,7},{7,6},{8,9},{9,8},{10,11... | collective-permute-start | bytes 6291464 | tf_op jit(solution)/shard_map/ppermute | solution.py:193
  12.4 4.1 %collective-permute-start.1 = (bf16[256,512]{1,0:T(8,128)(2,1)S(1)}, bf16[256,512]{1,0:T(8,128)(2,1)S(1)}, u32[]{:S(2)}, u32[]{:S(2)}) collective-permute-start(bf16[256,512]{1,0:T(8,128)(2,1)S(1)} %get-tuple-element.11), channel_id=1, source_target_pairs={{0,1},{1,0},{2,3},{3,2},{4,5},{5,4},{6,7},{7,6},{8,9},{9,8},{10,11... | collective-permute-start | bytes 786440 | tf_op jit(solution)/shard_map/ppermute | solution.py:190
  17.3 17.4 %collective-permute-start.2 = (bf16[1024,512]{1,0:T(8,128)(2,1)S(1)}, bf16[1024,512]{1,0:T(8,128)(2,1)S(1)}, u32[]{:S(2)}, u32[]{:S(2)}) collective-permute-start(bf16[1024,512]{1,0:T(8,128)(2,1)S(1)} %shard_map.103), channel_id=1, source_target_pairs={{0,32},{1,257},{2,34},{3,259},{4,36},{5,261},{6,38},{7,263},{8,40}... | collective-permute-start | bytes 3145736 | tf_op jit(solution)/shard_map/ppermute | solution.py:198
  20.1 25.8 %collective-permute-start.3 = (bf16[1024,512]{1,0:T(8,128)(2,1)S(1)}, bf16[1024,512]{1,0:T(8,128)(2,1)S(1)}, u32[]{:S(2)}, u32[]{:S(2)}) collective-permute-start(bf16[1024,512]{1,0:T(8,128)(2,1)S(1)} %shard_map.104), channel_id=1, source_target_pairs={{0,16},{1,129},{2,18},{3,131},{4,20},{5,133},{6,22},{7,135},{8,24}... | collective-permute-start | bytes 3145736 | tf_op jit(solution)/shard_map/ppermute | solution.py:198
  22.8 23.1 %collective-permute-start.4 = (bf16[1024,512]{1,0:T(8,128)(2,1)S(1)}, bf16[1024,512]{1,0:T(8,128)(2,1)S(1)}, u32[]{:S(2)}, u32[]{:S(2)}) collective-permute-start(bf16[1024,512]{1,0:T(8,128)(2,1)S(1)} %shard_map.105), channel_id=1, source_target_pairs={{0,48},{1,385},{2,50},{3,387},{4,52},{5,389},{6,54},{7,391},{8,56}... | collective-permute-start | bytes 3145736 | tf_op jit(solution)/shard_map/ppermute | solution.py:198
  46.3 39.0 %copy-start = (bf16[512,512]{1,0:T(8,128)(2,1)S(1)}, bf16[512,512]{1,0:T(8,128)(2,1)}, u32[]{:S(2)}) copy-start(bf16[512,512]{1,0:T(8,128)(2,1)} %key_weight_ref.1) | copy-start | bytes 1572868
  46.4 39.0 %copy-start.1 = (bf16[512,512]{1,0:T(8,128)(2,1)S(1)}, bf16[512,512]{1,0:T(8,128)(2,1)}, u32[]{:S(2)}) copy-start(bf16[512,512]{1,0:T(8,128)(2,1)} %value_weight_ref.1) | copy-start | bytes 1572868
  46.4 39.0 %copy-start.4 = (f32[4096]{0:T(1024)S(1)}, f32[4096]{0:T(1024)}, u32[]{:S(2)}) copy-start(f32[4096]{0:T(1024)} %param.9) | copy-start | bytes 49156
  46.4 9.0 %collective-permute-start.5 = (bf16[256,512]{1,0:T(8,128)(2,1)S(1)}, bf16[256,512]{1,0:T(8,128)(2,1)S(1)}, u32[]{:S(2)}, u32[]{:S(2)}) collective-permute-start(bf16[256,512]{1,0:T(8,128)(2,1)S(1)} %get-tuple-element.16), channel_id=1, source_target_pairs={{0,256},{1,33},{2,258},{3,35},{4,260},{5,37},{6,262},{7,39},{8,264... | collective-permute-start | bytes 786440 | tf_op jit(solution)/shard_map/ppermute | solution.py:204
  48.4 7.4 %collective-permute-start.7 = (bf16[256,512]{1,0:T(8,128)(2,1)S(1)}, bf16[256,512]{1,0:T(8,128)(2,1)S(1)}, u32[]{:S(2)}, u32[]{:S(2)}) collective-permute-start(bf16[256,512]{1,0:T(8,128)(2,1)S(1)} %get-tuple-element.17), channel_id=1, source_target_pairs={{0,384},{1,49},{2,386},{3,51},{4,388},{5,53},{6,390},{7,55},{8,392... | collective-permute-start | bytes 786440 | tf_op jit(solution)/shard_map/ppermute | solution.py:204
  50.4 9.2 %collective-permute-start.6 = (bf16[256,512]{1,0:T(8,128)(2,1)S(1)}, bf16[256,512]{1,0:T(8,128)(2,1)S(1)}, u32[]{:S(2)}, u32[]{:S(2)}) collective-permute-start(bf16[256,512]{1,0:T(8,128)(2,1)S(1)} %get-tuple-element.18), channel_id=1, source_target_pairs={{0,128},{1,17},{2,130},{3,19},{4,132},{5,21},{6,134},{7,23},{8,136... | collective-permute-start | bytes 786440 | tf_op jit(solution)/shard_map/ppermute | solution.py:204
  104.0 16.8 %all-to-all-start.2 = ((f32[16,4,128]{2,1,0:T(4,128)}), f32[16,4,128]{2,1,0:T(4,128)S(1)}, u32[]{:S(2)}, u32[]{:S(2)}) async-start(f32[16,4,128]{2,1,0:T(4,128)} %broadcast_in_dim.5), calls=%async_computation.2 | async-start | bytes 65536 | tf_op jit(solution)/shard_map/all_to_all | solution.py:183
  109.3 3.4 %collective-permute-start.8 = (f32[16,512]{1,0:T(8,128)S(1)}, f32[16,512]{1,0:T(8,128)S(1)}, u32[]{:S(2)}, u32[]{:S(2)}) collective-permute-start(f32[16,512]{1,0:T(8,128)S(1)} %convert_reduce_fusion.owned_ref), channel_id=1, source_target_pairs={{0,1},{1,0},{2,3},{3,2},{4,5},{5,4},{6,7},{7,6},{8,9},{9,8},{10,11... | collective-permute-start | bytes 98312 | tf_op jit(solution)/shard_map/ppermute | solution.py:209

commit v5 on v4

--- a/solution.py
+++ b/solution.py
@@ -52,10 +52,10 @@
     sent_ref[...] = jnp.where(keys_here, value_grad_ref[...], key_grad_ref[...])
 
 
-def product_kernel(offset, own_ref, other_ref, own_grad_ref, other_grad_ref, out_ref):
+def product_kernel(offset, steps, own_ref, other_ref, own_grad_ref, other_grad_ref, out_ref):
     x_here, y_here, _, x_first = coordinates()
     first = lax.rem(jnp.where(x_first, x_here, y_here) + offset, 4)
-    for step in range(4):
+    for at, step in enumerate(steps):
         second = lax.rem(jnp.where(x_first, y_here, x_here) + step, 4)
         y = jnp.where(x_first, second, first)
         x = jnp.where(x_first, first, second)
@@ -67,7 +67,7 @@
                 )
                 for tokens, grads in ((own_ref, own_grad_ref), (other_ref, other_grad_ref))
             )
-            rows = pl.ds((step * NZH + zh) * TILE, TILE)
+            rows = pl.ds((at * NZH + zh) * TILE, TILE)
             out_ref[rows, :] = total.astype(jnp.bfloat16)
 
 
@@ -87,11 +87,11 @@
     )(key_grad, value_grad)
 
 
-def chunk_product(offset, own, other, own_grad, other_grad):
+def chunk_product(offset, steps, own, other, own_grad, other_grad):
     tokens, feats = own.shape
-    rows, width = feats // 4, own_grad.shape[1]
+    rows, width = feats // 16 * len(steps), own_grad.shape[1]
     return pl.pallas_call(
-        functools.partial(product_kernel, offset),
+        functools.partial(product_kernel, offset, steps),
         out_shape=jax.ShapeDtypeStruct((rows, width), jnp.bfloat16),
         in_specs=[VMEM_BLOCK] * 4,
         out_specs=VMEM_BLOCK,
@@ -106,7 +106,7 @@
     total = arrays[0].astype(jnp.float32)
     for array in arrays[1:]:
         total = total + array.astype(jnp.float32)
-    return total.astype(jnp.bfloat16)
+    return total
 
 
 BLOCKS = 8
@@ -191,19 +191,20 @@
     scaled = hidden_in.astype(jnp.float32) * inv_rms.astype(jnp.float32)[:, None]
     own = (scaled * norm_gain[None, :]).astype(jnp.bfloat16)
     other = lax.ppermute(own, ALL, SWAP)
-    chunks = []
-    for offset in (2, 1, 3, 0):
-        chunk = chunk_product(offset, own, other, own_grad, other_grad)
-        if offset:
-            chunk = lax.ppermute(chunk, ALL, plane_pairs(0, offset))
-        chunks.append(chunk.reshape(4, -1, width))
-    planes = []
-    for offset in (2, 1, 3, 0):
-        line_sum = total_of([chunk[offset] for chunk in chunks])
-        if offset:
-            line_sum = lax.ppermute(line_sum, ALL, plane_pairs(1, offset))
-        planes.append(line_sum)
-    plane_sum = total_of(planes).reshape(NZH * NZL, -1, width)
+    product = lambda offset, steps: chunk_product(offset, steps, own, other, own_grad, other_grad)
+    passed, kept = (2, 1, 3), (0,)
+    lines = {step: [] for step in passed + kept}
+    for steps in (passed, kept):
+        for offset in (2, 1, 3):
+            chunk = lax.ppermute(product(offset, steps), ALL, plane_pairs(0, offset))
+            for step, block in zip(steps, chunk.reshape(len(steps), -1, width)):
+                lines[step].append(block)
+    for step, block in zip(passed + kept, product(0, passed + kept).reshape(4, -1, width)):
+        lines[step].append(block)
+    planes = [
+        lax.ppermute(total_of(lines[step]).astype(jnp.bfloat16), ALL, plane_pairs(1, step)) for step in passed
+    ]
+    plane_sum = total_of(lines[0] + planes).astype(jnp.bfloat16).reshape(NZH * NZL, -1, width)
     heard = lax.all_to_all(plane_sum, ALL, 0, 0, tiled=True, axis_index_groups=z_groups())
     owned = jnp.sum(heard.astype(jnp.float32), axis=0)
     arrived = lax.ppermute(owned, ALL, SWAP)

time: 122 us -> 116 us (0.951)
  waiting for transfers between devices: 34.5 us -> 17.9 us
  starting transfers between devices: 34.3 us -> 44.5 us
    ppermute x6 -> x9, waiting for transfers between devices: 23.5 us -> 6.87 us  [the longest x3 5.79 us: per_device(): lax.ppermute(total_of(lines[step]).astype(jnp.bfloat16), ALL, plane_pairs...]
    ppermute x6 -> x9, starting transfers between devices: 15.7 us -> 25.9 us  [the longest x6 18.6 us: per_device(): chunk = lax.ppermute(product(offset, steps), ALL, plane_pairs(0, offset))]
    pallas_call x4 -> x7, Pallas kernels: 3.22 us -> 3.9 us  [chunk_product(): pl.pallas_call(functools.partial(product_kernel, offset, steps), out_shap...]
  transfers between devices with their start and end apart: 10 -> 13, of which waited for: 8 -> 7; matrix products, arithmetic and copies ran while one was open for 0% -> 0% of each run, Pallas kernels for 2% -> 3%
where the time goes in v5:
time: 116 us
  starting transfers between devices  44.5 us (38%)
  blocking collectives  43.3 us (37%)
  waiting for transfers between devices  17.9 us (15%)
  Pallas kernels  4.85 us (4%)
  other arithmetic  3.65 us (3%)
    all_to_all x1, blocking collectives, per_device(): lax.all_to_all(plane_sum, ALL, 0, 0, tiled=True, axis_index_groups=z_grou...  25.5 us
    ppermute x6, starting transfers between devices, per_device(): chunk = lax.ppermute(product(offset, steps), ALL, plane_pairs(0, offset))  18.6 us
    all_to_all x1, blocking collectives, told_to(): lax.all_to_all(everyone, ALL, 0, 0, tiled=True, axis_index_groups=groups)  17.8 us
    ppermute x1, starting transfers between devices, per_device(): other = lax.ppermute(own, ALL, SWAP)  8.79 us
    all_to_all x1, waiting for transfers between devices, told_to(): lax.all_to_all(everyone, ALL, 0, 0, tiled=True, axis_index_groups=groups)  8.04 us
    ppermute x3, starting transfers between devices, per_device(): lax.ppermute(total_of(lines[step]).astype(jnp.bfloat16), ALL, plane_pairs...  7.33 us
    ppermute x3, waiting for transfers between devices, per_device(): lax.ppermute(total_of(lines[step]).astype(jnp.bfloat16), ALL, plane_pairs...  5.79 us
    all_to_all x1, starting transfers between devices, told_to(): lax.all_to_all(everyone, ALL, 0, 0, tiled=True, axis_index_groups=groups)  5.28 us
  transfers between devices with their start and end apart: 13, of which 7 were waited for; matrix products, arithmetic and copies ran while one was open for 0% of the time, Pallas kernels for 3%

profile of v5, /device:TPU:1, one launch (start us, length us, event | category | flops | bytes accessed | tf_op | source)
XLA Modules:
  0.0 115.7 jit_solution(3597122468664881459)
XLA Ops:
  0.6 0.7 convert_element_type.82
  1.3 0.0 copy-start.2
  1.3 0.0 copy-start.3
  1.3 2.3 %multiply_convert_fusion.own_ref = bf16[256,4096]{1,0:T(8,128)(2,1)S(1)} fusion(bf16[256,4096]{1,0:T(8,128)(2,1)} %param.7, f32[4096]{0:T(1024)} %param.9, f32[256]{0:T(256)S(1)} %convert_element_type.82), kind=kLoop, calls=%fused_computation | loop fusion | flops 4194304 | bytes 4211712 | tf_op jit(solution)/shard_map/convert_element_type | solution.py:192
  3.6 8.8 %collective-permute-start = (bf16[256,4096]{1,0:T(8,128)(2,1)S(1)}, bf16[256,4096]{1,0:T(8,128)(2,1)S(1)}, u32[]{:S(2)}, u32[]{:S(2)}) collective-permute-start(bf16[256,4096]{1,0:T(8,128)(2,1)S(1)} %multiply_convert_fusion.own_ref), channel_id=1, source_target_pairs={{0,1},{1,0},{2,3},{3,2},{4,5},{5,4},{6,7},{7,6},{8,9},{9,8},{10,11... | collective-permute-start | bytes 6291464 | tf_op jit(solution)/shard_map/ppermute | solution.py:193
  12.4 0.0 copy-done.2
  12.4 0.0 copy-done.3
  12.4 0.1 shard_map.102
  12.4 1.9 %collective-permute-start.1 = (bf16[256,512]{1,0:T(8,128)(2,1)S(1)}, bf16[256,512]{1,0:T(8,128)(2,1)S(1)}, u32[]{:S(2)}, u32[]{:S(2)}) collective-permute-start(bf16[256,512]{1,0:T(8,128)(2,1)S(1)} %get-tuple-element.11), channel_id=1, source_target_pairs={{0,1},{1,0},{2,3},{3,2},{4,5},{5,4},{6,7},{7,6},{8,9},{9,8},{10,11... | collective-permute-start | bytes 786440 | tf_op jit(solution)/shard_map/ppermute | solution.py:190
  14.4 2.1 %collective-permute-done.1.other_grad_ref = bf16[256,512]{1,0:T(8,128)(2,1)S(1)} collective-permute-done((bf16[256,512]{1,0:T(8,128)(2,1)S(1)}, bf16[256,512]{1,0:T(8,128)(2,1)S(1)}, u32[]{:S(2)}, u32[]{:S(2)}) %collective-permute-start.1) | collective-permute-done | bytes 262176 | tf_op jit(solution)/shard_map/ppermute | solution.py:190
  16.5 0.0 collective-permute-done.other_ref
  16.5 0.7 shard_map.107
  17.2 1.9 %collective-permute-start.5 = (bf16[768,512]{1,0:T(8,128)(2,1)S(1)}, bf16[768,512]{1,0:T(8,128)(2,1)S(1)}, u32[]{:S(2)}, u32[]{:S(2)}) collective-permute-start(bf16[768,512]{1,0:T(8,128)(2,1)S(1)} %shard_map.107), channel_id=1, source_target_pairs={{0,32},{1,257},{2,34},{3,259},{4,36},{5,261},{6,38},{7,263},{8,40}... | collective-permute-start | bytes 2359304 | tf_op jit(solution)/shard_map/ppermute | solution.py:199
  19.1 0.7 shard_map.108
  19.8 1.9 %collective-permute-start.6 = (bf16[768,512]{1,0:T(8,128)(2,1)S(1)}, bf16[768,512]{1,0:T(8,128)(2,1)S(1)}, u32[]{:S(2)}, u32[]{:S(2)}) collective-permute-start(bf16[768,512]{1,0:T(8,128)(2,1)S(1)} %shard_map.108), channel_id=1, source_target_pairs={{0,16},{1,129},{2,18},{3,131},{4,20},{5,133},{6,22},{7,135},{8,24}... | collective-permute-start | bytes 2359304 | tf_op jit(solution)/shard_map/ppermute | solution.py:199
  21.7 0.7 shard_map.109
  22.4 4.6 %collective-permute-start.7 = (bf16[768,512]{1,0:T(8,128)(2,1)S(1)}, bf16[768,512]{1,0:T(8,128)(2,1)S(1)}, u32[]{:S(2)}, u32[]{:S(2)}) collective-permute-start(bf16[768,512]{1,0:T(8,128)(2,1)S(1)} %shard_map.109), channel_id=1, source_target_pairs={{0,48},{1,385},{2,50},{3,387},{4,52},{5,389},{6,54},{7,391},{8,56}... | collective-permute-start | bytes 2359304 | tf_op jit(solution)/shard_map/ppermute | solution.py:199
  27.0 0.4 shard_map.103
  27.3 3.7 %collective-permute-start.2 = (bf16[256,512]{1,0:T(8,128)(2,1)S(1)}, bf16[256,512]{1,0:T(8,128)(2,1)S(1)}, u32[]{:S(2)}, u32[]{:S(2)}) collective-permute-start(bf16[256,512]{1,0:T(8,128)(2,1)S(1)} %shard_map.103), channel_id=1, source_target_pairs={{0,32},{1,257},{2,34},{3,259},{4,36},{5,261},{6,38},{7,263},{8,40}... | collective-permute-start | bytes 786440 | tf_op jit(solution)/shard_map/ppermute | solution.py:199
  31.0 0.4 shard_map.104
  31.4 1.9 %collective-permute-start.3 = (bf16[256,512]{1,0:T(8,128)(2,1)S(1)}, bf16[256,512]{1,0:T(8,128)(2,1)S(1)}, u32[]{:S(2)}, u32[]{:S(2)}) collective-permute-start(bf16[256,512]{1,0:T(8,128)(2,1)S(1)} %shard_map.104), channel_id=1, source_target_pairs={{0,16},{1,129},{2,18},{3,131},{4,20},{5,133},{6,22},{7,135},{8,24}... | collective-permute-start | bytes 786440 | tf_op jit(solution)/shard_map/ppermute | solution.py:199
  33.3 0.4 shard_map.105
  33.7 0.8 shard_map.106
  34.5 0.0 collective-permute-done.5
  34.5 4.6 %collective-permute-start.4 = (bf16[256,512]{1,0:T(8,128)(2,1)S(1)}, bf16[256,512]{1,0:T(8,128)(2,1)S(1)}, u32[]{:S(2)}, u32[]{:S(2)}) collective-permute-start(bf16[256,512]{1,0:T(8,128)(2,1)S(1)} %shard_map.105), channel_id=1, source_target_pairs={{0,48},{1,385},{2,50},{3,387},{4,52},{5,389},{6,54},{7,391},{8,56}... | collective-permute-start | bytes 786440 | tf_op jit(solution)/shard_map/ppermute | solution.py:199
  39.1 1.1 collective-permute-done.6
  40.1 0.0 collective-permute-done.7
  40.1 0.4 add_convert_fusion.3
  40.6 0.0 copy-start
  40.6 0.0 copy-start.1
  40.6 0.0 copy-start.4
  40.6 2.1 %collective-permute-start.8 = (bf16[256,512]{1,0:T(8,128)(2,1)S(1)}, bf16[256,512]{1,0:T(8,128)(2,1)S(1)}, u32[]{:S(2)}, u32[]{:S(2)}) collective-permute-start(bf16[256,512]{1,0:T(8,128)(2,1)S(1)} %get-tuple-element.16), channel_id=1, source_target_pairs={{0,256},{1,33},{2,258},{3,35},{4,260},{5,37},{6,262},{7,39},{8,264... | collective-permute-start | bytes 786440 | tf_op jit(solution)/shard_map/ppermute | solution.py:205
  42.7 1.9 %collective-permute-start.10 = (bf16[256,512]{1,0:T(8,128)(2,1)S(1)}, bf16[256,512]{1,0:T(8,128)(2,1)S(1)}, u32[]{:S(2)}, u32[]{:S(2)}) collective-permute-start(bf16[256,512]{1,0:T(8,128)(2,1)S(1)} %get-tuple-element.17), channel_id=1, source_target_pairs={{0,384},{1,49},{2,386},{3,51},{4,388},{5,53},{6,390},{7,55},{8,392... | collective-permute-start | bytes 786440 | tf_op jit(solution)/shard_map/ppermute | solution.py:205
  44.6 0.0 collective-permute-done.2
  44.6 3.4 %collective-permute-start.9 = (bf16[256,512]{1,0:T(8,128)(2,1)S(1)}, bf16[256,512]{1,0:T(8,128)(2,1)S(1)}, u32[]{:S(2)}, u32[]{:S(2)}) collective-permute-start(bf16[256,512]{1,0:T(8,128)(2,1)S(1)} %get-tuple-element.18), channel_id=1, source_target_pairs={{0,128},{1,17},{2,130},{3,19},{4,132},{5,21},{6,134},{7,23},{8,136... | collective-permute-start | bytes 786440 | tf_op jit(solution)/shard_map/ppermute | solution.py:205
  48.0 0.0 collective-permute-done.3
  48.0 0.0 collective-permute-done.4
  48.0 1.7 %collective-permute-done.8 = bf16[256,512]{1,0:T(8,128)(2,1)S(1)} collective-permute-done((bf16[256,512]{1,0:T(8,128)(2,1)S(1)}, bf16[256,512]{1,0:T(8,128)(2,1)S(1)}, u32[]{:S(2)}, u32[]{:S(2)}) %collective-permute-start.8) | collective-permute-done | bytes 262176 | tf_op jit(solution)/shard_map/ppermute | solution.py:205
  49.7 0.4 collective-permute-done.10
  50.1 3.7 %collective-permute-done.9 = bf16[256,512]{1,0:T(8,128)(2,1)S(1)} collective-permute-done((bf16[256,512]{1,0:T(8,128)(2,1)S(1)}, bf16[256,512]{1,0:T(8,128)(2,1)S(1)}, u32[]{:S(2)}, u32[]{:S(2)}) %collective-permute-start.9) | collective-permute-done | bytes 262176 | tf_op jit(solution)/shard_map/ppermute | solution.py:205
  53.8 0.2 add_convert_fusion
  54.1 25.5 %all_to_all.15 = bf16[16,16,512]{2,1,0:T(8,128)(2,1)S(1)} all-to-all(bf16[16,16,512]{2,1,0:T(8,128)(2,1)S(1)} %bitcast.8), channel_id=1, replica_groups={{0,2,4,6,8,10,12,14,64,66,68,70,72,74,76,78},{1,3,5,7,9,11,13,15,65,67,..., dimensions={0} | all-to-all | bytes 524288 | tf_op jit(solution)/shard_map/all_to_all | solution.py:208
  79.6 0.0 copy-done
  79.6 0.0 copy-done.1
  79.6 0.0 copy-done.4
  79.6 0.1 shard_map.110
  79.8 17.8 %all_to_all.16 = f32[32,2,128]{2,1,0:T(2,128)S(1)} all-to-all(f32[32,2,128]{2,1,0:T(2,128)S(1)} %broadcast_in_dim.4), channel_id=1, replica_groups={{0,1,16,17,32,33,48,49,128,129,144,145,160,161,176,177,256,257,272,273,..., dimensions={0} | all-to-all | bytes 65536 | tf_op jit(solution)/shard_map/all_to_all | solution.py:183
  97.6 0.6 broadcast_in_dim.5
  98.2 5.3 %all-to-all-start.2 = ((f32[16,4,128]{2,1,0:T(4,128)}), f32[16,4,128]{2,1,0:T(4,128)S(1)}, u32[]{:S(2)}, u32[]{:S(2)}) async-start(f32[16,4,128]{2,1,0:T(4,128)} %broadcast_in_dim.5), calls=%async_computation.2 | async-start | bytes 65536 | tf_op jit(solution)/shard_map/all_to_all | solution.py:183
  103.5 2.6 %collective-permute-start.11 = (f32[16,512]{1,0:T(8,128)S(1)}, f32[16,512]{1,0:T(8,128)S(1)}, u32[]{:S(2)}, u32[]{:S(2)}) collective-permute-start(f32[16,512]{1,0:T(8,128)S(1)} %convert_reduce_fusion.owned_ref), channel_id=1, source_target_pairs={{0,1},{1,0},{2,3},{3,2},{4,5},{5,4},{6,7},{7,6},{8,9},{9,8},{10,11... | collective-permute-start | bytes 98312 | tf_op jit(solution)/shard_map/ppermute | solution.py:210
  106.1 0.8 collective-permute-done.11.arrived_ref
  107.0 8.0 %all-to-all-done.2 = f32[16,4,128]{2,1,0:T(4,128)S(1)} async-done(((f32[16,4,128]{2,1,0:T(4,128)}), f32[16,4,128]{2,1,0:T(4,128)S(1)}, u32[]{:S(2)}, u32[]{:S(2)}) %all-to-all-start.2) | async-done | bytes 32800 | tf_op jit(solution)/shard_map/all_to_all | solution.py:183
  115.0 0.7 shard_map.112
  (3 shorter events, 0.1 us)
Async XLA Ops:
  1.3 11.1 %copy-start.2 = (bf16[256,512]{1,0:T(8,128)(2,1)S(1)}, bf16[256,512]{1,0:T(8,128)(2,1)}, u32[]{:S(2)}) copy-start(bf16[256,512]{1,0:T(8,128)(2,1)} %key_grad_ref.1) | copy-start | bytes 786436
  1.3 11.1 %copy-start.3 = (bf16[256,512]{1,0:T(8,128)(2,1)S(1)}, bf16[256,512]{1,0:T(8,128)(2,1)}, u32[]{:S(2)}) copy-start(bf16[256,512]{1,0:T(8,128)(2,1)} %value_grad_ref.1) | copy-start | bytes 786436
  3.6 12.9 %collective-permute-start = (bf16[256,4096]{1,0:T(8,128)(2,1)S(1)}, bf16[256,4096]{1,0:T(8,128)(2,1)S(1)}, u32[]{:S(2)}, u32[]{:S(2)}) collective-permute-start(bf16[256,4096]{1,0:T(8,128)(2,1)S(1)} %multiply_convert_fusion.own_ref), channel_id=1, source_target_pairs={{0,1},{1,0},{2,3},{3,2},{4,5},{5,4},{6,7},{7,6},{8,9},{9,8},{10,11... | collective-permute-start | bytes 6291464 | tf_op jit(solution)/shard_map/ppermute | solution.py:193
  12.4 4.1 %collective-permute-start.1 = (bf16[256,512]{1,0:T(8,128)(2,1)S(1)}, bf16[256,512]{1,0:T(8,128)(2,1)S(1)}, u32[]{:S(2)}, u32[]{:S(2)}) collective-permute-start(bf16[256,512]{1,0:T(8,128)(2,1)S(1)} %get-tuple-element.11), channel_id=1, source_target_pairs={{0,1},{1,0},{2,3},{3,2},{4,5},{5,4},{6,7},{7,6},{8,9},{9,8},{10,11... | collective-permute-start | bytes 786440 | tf_op jit(solution)/shard_map/ppermute | solution.py:190
  17.2 17.3 %collective-permute-start.5 = (bf16[768,512]{1,0:T(8,128)(2,1)S(1)}, bf16[768,512]{1,0:T(8,128)(2,1)S(1)}, u32[]{:S(2)}, u32[]{:S(2)}) collective-permute-start(bf16[768,512]{1,0:T(8,128)(2,1)S(1)} %shard_map.107), channel_id=1, source_target_pairs={{0,32},{1,257},{2,34},{3,259},{4,36},{5,261},{6,38},{7,263},{8,40}... | collective-permute-start | bytes 2359304 | tf_op jit(solution)/shard_map/ppermute | solution.py:199
  19.8 20.4 %collective-permute-start.6 = (bf16[768,512]{1,0:T(8,128)(2,1)S(1)}, bf16[768,512]{1,0:T(8,128)(2,1)S(1)}, u32[]{:S(2)}, u32[]{:S(2)}) collective-permute-start(bf16[768,512]{1,0:T(8,128)(2,1)S(1)} %shard_map.108), channel_id=1, source_target_pairs={{0,16},{1,129},{2,18},{3,131},{4,20},{5,133},{6,22},{7,135},{8,24}... | collective-permute-start | bytes 2359304 | tf_op jit(solution)/shard_map/ppermute | solution.py:199
  22.4 17.8 %collective-permute-start.7 = (bf16[768,512]{1,0:T(8,128)(2,1)S(1)}, bf16[768,512]{1,0:T(8,128)(2,1)S(1)}, u32[]{:S(2)}, u32[]{:S(2)}) collective-permute-start(bf16[768,512]{1,0:T(8,128)(2,1)S(1)} %shard_map.109), channel_id=1, source_target_pairs={{0,48},{1,385},{2,50},{3,387},{4,52},{5,389},{6,54},{7,391},{8,56}... | collective-permute-start | bytes 2359304 | tf_op jit(solution)/shard_map/ppermute | solution.py:199
  27.3 17.3 %collective-permute-start.2 = (bf16[256,512]{1,0:T(8,128)(2,1)S(1)}, bf16[256,512]{1,0:T(8,128)(2,1)S(1)}, u32[]{:S(2)}, u32[]{:S(2)}) collective-permute-start(bf16[256,512]{1,0:T(8,128)(2,1)S(1)} %shard_map.103), channel_id=1, source_target_pairs={{0,32},{1,257},{2,34},{3,259},{4,36},{5,261},{6,38},{7,263},{8,40}... | collective-permute-start | bytes 786440 | tf_op jit(solution)/shard_map/ppermute | solution.py:199
  31.4 16.6 %collective-permute-start.3 = (bf16[256,512]{1,0:T(8,128)(2,1)S(1)}, bf16[256,512]{1,0:T(8,128)(2,1)S(1)}, u32[]{:S(2)}, u32[]{:S(2)}) collective-permute-start(bf16[256,512]{1,0:T(8,128)(2,1)S(1)} %shard_map.104), channel_id=1, source_target_pairs={{0,16},{1,129},{2,18},{3,131},{4,20},{5,133},{6,22},{7,135},{8,24}... | collective-permute-start | bytes 786440 | tf_op jit(solution)/shard_map/ppermute | solution.py:199
  34.5 13.5 %collective-permute-start.4 = (bf16[256,512]{1,0:T(8,128)(2,1)S(1)}, bf16[256,512]{1,0:T(8,128)(2,1)S(1)}, u32[]{:S(2)}, u32[]{:S(2)}) collective-permute-start(bf16[256,512]{1,0:T(8,128)(2,1)S(1)} %shard_map.105), channel_id=1, source_target_pairs={{0,48},{1,385},{2,50},{3,387},{4,52},{5,389},{6,54},{7,391},{8,56}... | collective-permute-start | bytes 786440 | tf_op jit(solution)/shard_map/ppermute | solution.py:199
  40.6 39.0 %copy-start = (bf16[512,512]{1,0:T(8,128)(2,1)S(1)}, bf16[512,512]{1,0:T(8,128)(2,1)}, u32[]{:S(2)}) copy-start(bf16[512,512]{1,0:T(8,128)(2,1)} %key_weight_ref.1) | copy-start | bytes 1572868
  40.6 39.0 %copy-start.1 = (bf16[512,512]{1,0:T(8,128)(2,1)S(1)}, bf16[512,512]{1,0:T(8,128)(2,1)}, u32[]{:S(2)}) copy-start(bf16[512,512]{1,0:T(8,128)(2,1)} %value_weight_ref.1) | copy-start | bytes 1572868
  40.6 39.0 %copy-start.4 = (f32[4096]{0:T(1024)S(1)}, f32[4096]{0:T(1024)}, u32[]{:S(2)}) copy-start(f32[4096]{0:T(1024)} %param.9) | copy-start | bytes 49156
  40.6 9.0 %collective-permute-start.8 = (bf16[256,512]{1,0:T(8,128)(2,1)S(1)}, bf16[256,512]{1,0:T(8,128)(2,1)S(1)}, u32[]{:S(2)}, u32[]{:S(2)}) collective-permute-start(bf16[256,512]{1,0:T(8,128)(2,1)S(1)} %get-tuple-element.16), channel_id=1, source_target_pairs={{0,256},{1,33},{2,258},{3,35},{4,260},{5,37},{6,262},{7,39},{8,264... | collective-permute-start | bytes 786440 | tf_op jit(solution)/shard_map/ppermute | solution.py:205
  42.7 7.4 %collective-permute-start.10 = (bf16[256,512]{1,0:T(8,128)(2,1)S(1)}, bf16[256,512]{1,0:T(8,128)(2,1)S(1)}, u32[]{:S(2)}, u32[]{:S(2)}) collective-permute-start(bf16[256,512]{1,0:T(8,128)(2,1)S(1)} %get-tuple-element.17), channel_id=1, source_target_pairs={{0,384},{1,49},{2,386},{3,51},{4,388},{5,53},{6,390},{7,55},{8,392... | collective-permute-start | bytes 786440 | tf_op jit(solution)/shard_map/ppermute | solution.py:205
  44.6 9.2 %collective-permute-start.9 = (bf16[256,512]{1,0:T(8,128)(2,1)S(1)}, bf16[256,512]{1,0:T(8,128)(2,1)S(1)}, u32[]{:S(2)}, u32[]{:S(2)}) collective-permute-start(bf16[256,512]{1,0:T(8,128)(2,1)S(1)} %get-tuple-element.18), channel_id=1, source_target_pairs={{0,128},{1,17},{2,130},{3,19},{4,132},{5,21},{6,134},{7,23},{8,136... | collective-permute-start | bytes 786440 | tf_op jit(solution)/shard_map/ppermute | solution.py:205
  98.2 16.8 %all-to-all-start.2 = ((f32[16,4,128]{2,1,0:T(4,128)}), f32[16,4,128]{2,1,0:T(4,128)S(1)}, u32[]{:S(2)}, u32[]{:S(2)}) async-start(f32[16,4,128]{2,1,0:T(4,128)} %broadcast_in_dim.5), calls=%async_computation.2 | async-start | bytes 65536 | tf_op jit(solution)/shard_map/all_to_all | solution.py:183
  103.5 3.4 %collective-permute-start.11 = (f32[16,512]{1,0:T(8,128)S(1)}, f32[16,512]{1,0:T(8,128)S(1)}, u32[]{:S(2)}, u32[]{:S(2)}) collective-permute-start(f32[16,512]{1,0:T(8,128)S(1)} %convert_reduce_fusion.owned_ref), channel_id=1, source_target_pairs={{0,1},{1,0},{2,3},{3,2},{4,5},{5,4},{6,7},{7,6},{8,9},{9,8},{10,11... | collective-permute-start | bytes 98312 | tf_op jit(solution)/shard_map/ppermute | solution.py:210

commit v6 on v5

--- a/solution.py
+++ b/solution.py
@@ -46,13 +46,15 @@
     return fsdp // NZL, node // NZH, fsdp % NZL, lax.axis_index("rep") == 0
 
 
-def column_kernel(key_grad_ref, value_grad_ref, own_ref, sent_ref):
+def column_kernel(key_grad_ref, value_grad_ref, inv_ref, own_ref, sent_ref):
     keys_here = coordinates()[3]
+    width = key_grad_ref.shape[1]
     own_ref[...] = jnp.where(keys_here, key_grad_ref[...], value_grad_ref[...])
-    sent_ref[...] = jnp.where(keys_here, value_grad_ref[...], key_grad_ref[...])
-
-
-def product_kernel(offset, steps, own_ref, other_ref, own_grad_ref, other_grad_ref, out_ref):
+    sent_ref[:, :width] = jnp.where(keys_here, value_grad_ref[...], key_grad_ref[...])
+    sent_ref[:, width:] = jnp.broadcast_to(inv_ref[...], (inv_ref.shape[0], TILE))
+
+
+def product_kernel(offset, steps, own_ref, other_ref, own_grad_ref, other_pack_ref, gain_ref, out_ref):
     x_here, y_here, _, x_first = coordinates()
     first = lax.rem(jnp.where(x_first, x_here, y_here) + offset, 4)
     for at, step in enumerate(steps):
@@ -61,11 +63,12 @@
         x = jnp.where(x_first, first, second)
         for zh in range(NZH):
             columns = pl.ds(pl.multiple_of((y * 8 + zh * 4 + x) * TILE, TILE), TILE)
+            width = own_grad_ref.shape[1]
+            scaled = other_ref[:, columns].astype(jnp.float32) * other_pack_ref[:, width:].astype(jnp.float32)
+            other = (scaled * gain_ref[:, columns]).astype(jnp.bfloat16)
             total = sum(
-                lax.dot_general(
-                    tokens[:, columns], grads[...], (((0,), (0,)), ((), ())), preferred_element_type=jnp.float32
-                )
-                for tokens, grads in ((own_ref, own_grad_ref), (other_ref, other_grad_ref))
+                lax.dot_general(tokens, grads, (((0,), (0,)), ((), ())), preferred_element_type=jnp.float32)
+                for tokens, grads in ((own_ref[:, columns], own_grad_ref[...]), (other, other_pack_ref[:, :width]))
             )
             rows = pl.ds((at * NZH + zh) * TILE, TILE)
             out_ref[rows, :] = total.astype(jnp.bfloat16)
@@ -76,30 +79,33 @@
 SMALL = pltpu.CompilerParams(vmem_limit_bytes=4 * 1024 * 1024)
 
 
-def columns_of(key_grad, value_grad):
-    shape = jax.ShapeDtypeStruct(key_grad.shape, key_grad.dtype)
+def columns_of(key_grad, value_grad, inv_column):
+    tokens, width = key_grad.shape
     return pl.pallas_call(
         column_kernel,
-        out_shape=(shape, shape),
-        in_specs=[VMEM_BLOCK] * 2,
+        out_shape=(
+            jax.ShapeDtypeStruct((tokens, width), key_grad.dtype),
+            jax.ShapeDtypeStruct((tokens, width + TILE), key_grad.dtype),
+        ),
+        in_specs=[VMEM_BLOCK] * 3,
         out_specs=(VMEM_BLOCK, VMEM_BLOCK),
         compiler_params=SMALL,
-    )(key_grad, value_grad)
-
-
-def chunk_product(offset, steps, own, other, own_grad, other_grad):
+    )(key_grad, value_grad, inv_column)
+
+
+def chunk_product(offset, steps, own, other, own_grad, other_pack, gain):
     tokens, feats = own.shape
     rows, width = feats // 16 * len(steps), own_grad.shape[1]
     return pl.pallas_call(
         functools.partial(product_kernel, offset, steps),
         out_shape=jax.ShapeDtypeStruct((rows, width), jnp.bfloat16),
-        in_specs=[VMEM_BLOCK] * 4,
+        in_specs=[VMEM_BLOCK] * 5,
         out_specs=VMEM_BLOCK,
         cost_estimate=pl.CostEstimate(
             flops=4 * tokens * rows * width, bytes_accessed=rows * (4 * tokens + 2 * width), transcendentals=0
         ),
         compiler_params=pltpu.CompilerParams(vmem_limit_bytes=12 * 1024 * 1024),
-    )(own, other, own_grad, other_grad)
+    )(own, other, own_grad, other_pack, gain)
 
 
 def total_of(arrays):
@@ -186,12 +192,14 @@
 
 def per_device(hidden_in, inv_rms, norm_gain, key_grad, value_grad, key_weight, value_weight):
     width = key_grad.shape[1]
-    own_grad, sent_grad = columns_of(key_grad, value_grad)
-    other_grad = lax.ppermute(sent_grad, ALL, SWAP)
-    scaled = hidden_in.astype(jnp.float32) * inv_rms.astype(jnp.float32)[:, None]
+    other = lax.ppermute(hidden_in, ALL, SWAP)
+    inv_column = lax.optimization_barrier(inv_rms[:, None])
+    own_grad, sent_pack = columns_of(key_grad, value_grad, inv_column)
+    other_pack = lax.ppermute(sent_pack, ALL, SWAP)
+    scaled = hidden_in.astype(jnp.float32) * inv_column.astype(jnp.float32)
     own = (scaled * norm_gain[None, :]).astype(jnp.bfloat16)
-    other = lax.ppermute(own, ALL, SWAP)
-    product = lambda offset, steps: chunk_product(offset, steps, own, other, own_grad, other_grad)
+    gain = norm_gain[None, :]
+    product = lambda offset, steps: chunk_product(offset, steps, own, other, own_grad, other_pack, gain)
     passed, kept = (2, 1, 3), (0,)
     lines = {step: [] for step in passed + kept}
     for steps in (passed, kept):

time: 116 us -> 116 us (level)
  local copies, waits for them, and re-layouts: 0.66 us -> 3.35 us
  waiting for transfers between devices: 17.9 us -> 15.8 us
    ppermute x2, waiting for transfers between devices: 2.13 us -> 0.01 us  [the longest x1 0.01 us: per_device(): other = lax.ppermute(hidden_in, ALL, SWAP)]
    unnamed x10, local copies, waits for them, and re-layouts: 0.03 us -> 1.91 us
  transfers between devices with their start and end apart: 13 -> 13, of which waited for: 7 -> 6; matrix products, arithmetic and copies ran while one was open for 0% -> 3% of each run, Pallas kernels for 3% -> 3%
where the time goes in v6:
time: 116 us
  starting transfers between devices  44.5 us (38%)
  blocking collectives  43.3 us (37%)
  waiting for transfers between devices  15.8 us (14%)
  Pallas kernels  4.86 us (4%)
  local copies, waits for them, and re-layouts  3.35 us (3%)
  other arithmetic  2.95 us (3%)
    all_to_all x1, blocking collectives, per_device(): lax.all_to_all(plane_sum, ALL, 0, 0, tiled=True, axis_index_groups=z_grou...  25.5 us
    ppermute x6, starting transfers between devices, per_device(): chunk = lax.ppermute(product(offset, steps), ALL, plane_pairs(0, offset))  18.6 us
    all_to_all x1, blocking collectives, told_to(): lax.all_to_all(everyone, ALL, 0, 0, tiled=True, axis_index_groups=groups)  17.8 us
    ppermute x1, starting transfers between devices, per_device(): other = lax.ppermute(hidden_in, ALL, SWAP)  8.79 us
    all_to_all x1, waiting for transfers between devices, told_to(): lax.all_to_all(everyone, ALL, 0, 0, tiled=True, axis_index_groups=groups)  8.04 us
    ppermute x3, starting transfers between devices, per_device(): lax.ppermute(total_of(lines[step]).astype(jnp.bfloat16), ALL, plane_pairs...  7.33 us
    ppermute x3, waiting for transfers between devices, per_device(): lax.ppermute(total_of(lines[step]).astype(jnp.bfloat16), ALL, plane_pairs...  5.79 us
    all_to_all x1, starting transfers between devices, told_to(): lax.all_to_all(everyone, ALL, 0, 0, tiled=True, axis_index_groups=groups)  5.34 us
  transfers between devices with their start and end apart: 13, of which 6 were waited for; matrix products, arithmetic and copies ran while one was open for 3% of the time, Pallas kernels for 3%

profile of v6, /device:TPU:1, one launch (start us, length us, event | category | flops | bytes accessed | tf_op | source)
XLA Modules:
  0.0 115.7 jit_solution(8542428270878091554)
XLA Ops:
  0.6 8.8 %collective-permute-start = (bf16[256,4096]{1,0:T(8,128)(2,1)}, bf16[256,4096]{1,0:T(8,128)(2,1)S(1)}, u32[]{:S(2)}, u32[]{:S(2)}) collective-permute-start(bf16[256,4096]{1,0:T(8,128)(2,1)} %param.7), channel_id=1, source_target_pairs={{0,1},{1,0},{2,3},{3,2},{4,5},{5,4},{6,7},{7,6},{8,9},{9,8},{10,11... | collective-permute-start | bytes 6291464 | tf_op jit(solution)/shard_map/ppermute | solution.py:195
  9.4 0.7 broadcast_in_dim.8
  10.1 0.1 copy.11.inv_ref
  10.2 0.0 copy-start.3
  10.2 0.9 copy-done.3
  11.2 0.0 copy-start.4
  11.2 0.9 copy-done.4
  12.1 0.1 shard_map.102
  12.2 1.9 %collective-permute-start.1 = (bf16[256,640]{1,0:T(8,128)(2,1)S(1)}, bf16[256,640]{1,0:T(8,128)(2,1)S(1)}, u32[]{:S(2)}, u32[]{:S(2)}) collective-permute-start(bf16[256,640]{1,0:T(8,128)(2,1)S(1)} %get-tuple-element.11), channel_id=1, source_target_pairs={{0,1},{1,0},{2,3},{3,2},{4,5},{5,4},{6,7},{7,6},{8,9},{9,8},{10,11... | collective-permute-start | bytes 983048 | tf_op jit(solution)/shard_map/ppermute | solution.py:198
  14.2 0.0 copy-start
  14.2 2.2 %multiply_convert_fusion.own_ref = bf16[256,4096]{1,0:T(8,128)(2,1)S(1)} fusion(bf16[256,4096]{1,0:T(8,128)(2,1)} %param.7, f32[4096]{0:T(1024)} %param.9, f32[256]{0:T(256)S(1)} %bitcast.18), kind=kLoop, calls=%fused_computation | loop fusion | flops 4194304 | bytes 4211712 | tf_op jit(solution)/shard_map/convert_element_type | solution.py:200
  16.4 0.0 collective-permute-done.1.other_pack_ref
  16.4 0.0 collective-permute-done.other_ref
  16.4 0.0 copy-done
  16.5 0.7 shard_map.107
  17.1 1.9 %collective-permute-start.5 = (bf16[768,512]{1,0:T(8,128)(2,1)S(1)}, bf16[768,512]{1,0:T(8,128)(2,1)S(1)}, u32[]{:S(2)}, u32[]{:S(2)}) collective-permute-start(bf16[768,512]{1,0:T(8,128)(2,1)S(1)} %shard_map.107), channel_id=1, source_target_pairs={{0,32},{1,257},{2,34},{3,259},{4,36},{5,261},{6,38},{7,263},{8,40}... | collective-permute-start | bytes 2359304 | tf_op jit(solution)/shard_map/ppermute | solution.py:207
  19.0 0.7 shard_map.108
  19.7 1.9 %collective-permute-start.6 = (bf16[768,512]{1,0:T(8,128)(2,1)S(1)}, bf16[768,512]{1,0:T(8,128)(2,1)S(1)}, u32[]{:S(2)}, u32[]{:S(2)}) collective-permute-start(bf16[768,512]{1,0:T(8,128)(2,1)S(1)} %shard_map.108), channel_id=1, source_target_pairs={{0,16},{1,129},{2,18},{3,131},{4,20},{5,133},{6,22},{7,135},{8,24}... | collective-permute-start | bytes 2359304 | tf_op jit(solution)/shard_map/ppermute | solution.py:207
  21.6 0.7 shard_map.109
  22.3 4.6 %collective-permute-start.7 = (bf16[768,512]{1,0:T(8,128)(2,1)S(1)}, bf16[768,512]{1,0:T(8,128)(2,1)S(1)}, u32[]{:S(2)}, u32[]{:S(2)}) collective-permute-start(bf16[768,512]{1,0:T(8,128)(2,1)S(1)} %shard_map.109), channel_id=1, source_target_pairs={{0,48},{1,385},{2,50},{3,387},{4,52},{5,389},{6,54},{7,391},{8,56}... | collective-permute-start | bytes 2359304 | tf_op jit(solution)/shard_map/ppermute | solution.py:207
  26.9 0.4 shard_map.103
  27.3 3.7 %collective-permute-start.2 = (bf16[256,512]{1,0:T(8,128)(2,1)S(1)}, bf16[256,512]{1,0:T(8,128)(2,1)S(1)}, u32[]{:S(2)}, u32[]{:S(2)}) collective-permute-start(bf16[256,512]{1,0:T(8,128)(2,1)S(1)} %shard_map.103), channel_id=1, source_target_pairs={{0,32},{1,257},{2,34},{3,259},{4,36},{5,261},{6,38},{7,263},{8,40}... | collective-permute-start | bytes 786440 | tf_op jit(solution)/shard_map/ppermute | solution.py:207
  30.9 0.4 shard_map.104
  31.3 1.9 %collective-permute-start.3 = (bf16[256,512]{1,0:T(8,128)(2,1)S(1)}, bf16[256,512]{1,0:T(8,128)(2,1)S(1)}, u32[]{:S(2)}, u32[]{:S(2)}) collective-permute-start(bf16[256,512]{1,0:T(8,128)(2,1)S(1)} %shard_map.104), channel_id=1, source_target_pairs={{0,16},{1,129},{2,18},{3,131},{4,20},{5,133},{6,22},{7,135},{8,24}... | collective-permute-start | bytes 786440 | tf_op jit(solution)/shard_map/ppermute | solution.py:207
  33.2 0.4 shard_map.105
  33.6 0.8 shard_map.106
  34.4 0.0 collective-permute-done.5
  34.4 4.6 %collective-permute-start.4 = (bf16[256,512]{1,0:T(8,128)(2,1)S(1)}, bf16[256,512]{1,0:T(8,128)(2,1)S(1)}, u32[]{:S(2)}, u32[]{:S(2)}) collective-permute-start(bf16[256,512]{1,0:T(8,128)(2,1)S(1)} %shard_map.105), channel_id=1, source_target_pairs={{0,48},{1,385},{2,50},{3,387},{4,52},{5,389},{6,54},{7,391},{8,56}... | collective-permute-start | bytes 786440 | tf_op jit(solution)/shard_map/ppermute | solution.py:207
  39.0 1.1 collective-permute-done.6
  40.1 0.0 collective-permute-done.7
  40.1 0.4 add_convert_fusion.3
  40.5 0.0 copy-start.1
  40.5 0.0 copy-start.2
  40.6 2.1 %collective-permute-start.8 = (bf16[256,512]{1,0:T(8,128)(2,1)S(1)}, bf16[256,512]{1,0:T(8,128)(2,1)S(1)}, u32[]{:S(2)}, u32[]{:S(2)}) collective-permute-start(bf16[256,512]{1,0:T(8,128)(2,1)S(1)} %get-tuple-element.16), channel_id=1, source_target_pairs={{0,256},{1,33},{2,258},{3,35},{4,260},{5,37},{6,262},{7,39},{8,264... | collective-permute-start | bytes 786440 | tf_op jit(solution)/shard_map/ppermute | solution.py:213
  42.6 1.9 %collective-permute-start.10 = (bf16[256,512]{1,0:T(8,128)(2,1)S(1)}, bf16[256,512]{1,0:T(8,128)(2,1)S(1)}, u32[]{:S(2)}, u32[]{:S(2)}) collective-permute-start(bf16[256,512]{1,0:T(8,128)(2,1)S(1)} %get-tuple-element.17), channel_id=1, source_target_pairs={{0,384},{1,49},{2,386},{3,51},{4,388},{5,53},{6,390},{7,55},{8,392... | collective-permute-start | bytes 786440 | tf_op jit(solution)/shard_map/ppermute | solution.py:213
  44.5 0.0 collective-permute-done.2
  44.6 3.4 %collective-permute-start.9 = (bf16[256,512]{1,0:T(8,128)(2,1)S(1)}, bf16[256,512]{1,0:T(8,128)(2,1)S(1)}, u32[]{:S(2)}, u32[]{:S(2)}) collective-permute-start(bf16[256,512]{1,0:T(8,128)(2,1)S(1)} %get-tuple-element.18), channel_id=1, source_target_pairs={{0,128},{1,17},{2,130},{3,19},{4,132},{5,21},{6,134},{7,23},{8,136... | collective-permute-start | bytes 786440 | tf_op jit(solution)/shard_map/ppermute | solution.py:213
  47.9 0.0 collective-permute-done.3
  47.9 0.0 collective-permute-done.4
  47.9 1.7 %collective-permute-done.8 = bf16[256,512]{1,0:T(8,128)(2,1)S(1)} collective-permute-done((bf16[256,512]{1,0:T(8,128)(2,1)S(1)}, bf16[256,512]{1,0:T(8,128)(2,1)S(1)}, u32[]{:S(2)}, u32[]{:S(2)}) %collective-permute-start.8) | collective-permute-done | bytes 262176 | tf_op jit(solution)/shard_map/ppermute | solution.py:213
  49.6 0.4 collective-permute-done.10
  50.0 3.7 %collective-permute-done.9 = bf16[256,512]{1,0:T(8,128)(2,1)S(1)} collective-permute-done((bf16[256,512]{1,0:T(8,128)(2,1)S(1)}, bf16[256,512]{1,0:T(8,128)(2,1)S(1)}, u32[]{:S(2)}, u32[]{:S(2)}) %collective-permute-start.9) | collective-permute-done | bytes 262176 | tf_op jit(solution)/shard_map/ppermute | solution.py:213
  53.7 0.2 add_convert_fusion
  54.0 25.5 %all_to_all.15 = bf16[16,16,512]{2,1,0:T(8,128)(2,1)S(1)} all-to-all(bf16[16,16,512]{2,1,0:T(8,128)(2,1)S(1)} %bitcast.17), channel_id=1, replica_groups={{0,2,4,6,8,10,12,14,64,66,68,70,72,74,76,78},{1,3,5,7,9,11,13,15,65,67,..., dimensions={0} | all-to-all | bytes 524288 | tf_op jit(solution)/shard_map/all_to_all | solution.py:216
  79.5 0.0 copy-done.1
  79.5 0.0 copy-done.2
  79.5 0.1 shard_map.110
  79.7 17.8 %all_to_all.16 = f32[32,2,128]{2,1,0:T(2,128)S(1)} all-to-all(f32[32,2,128]{2,1,0:T(2,128)S(1)} %broadcast_in_dim.10), channel_id=1, replica_groups={{0,1,16,17,32,33,48,49,128,129,144,145,160,161,176,177,256,257,272,273,..., dimensions={0} | all-to-all | bytes 65536 | tf_op jit(solution)/shard_map/all_to_all | solution.py:189
  97.5 0.6 broadcast_in_dim.22
  98.1 5.3 %all-to-all-start.2 = ((f32[16,4,128]{2,1,0:T(4,128)}), f32[16,4,128]{2,1,0:T(4,128)S(1)}, u32[]{:S(2)}, u32[]{:S(2)}) async-start(f32[16,4,128]{2,1,0:T(4,128)} %broadcast_in_dim.22), calls=%async_computation.2 | async-start | bytes 65536 | tf_op jit(solution)/shard_map/all_to_all | solution.py:189
  103.5 2.6 %collective-permute-start.11 = (f32[16,512]{1,0:T(8,128)S(1)}, f32[16,512]{1,0:T(8,128)S(1)}, u32[]{:S(2)}, u32[]{:S(2)}) collective-permute-start(f32[16,512]{1,0:T(8,128)S(1)} %convert_reduce_fusion.owned_ref), channel_id=1, source_target_pairs={{0,1},{1,0},{2,3},{3,2},{4,5},{5,4},{6,7},{7,6},{8,9},{9,8},{10,11... | collective-permute-start | bytes 98312 | tf_op jit(solution)/shard_map/ppermute | solution.py:218
  106.1 0.8 collective-permute-done.11.arrived_ref
  106.9 8.0 %all-to-all-done.2 = f32[16,4,128]{2,1,0:T(4,128)S(1)} async-done(((f32[16,4,128]{2,1,0:T(4,128)}), f32[16,4,128]{2,1,0:T(4,128)S(1)}, u32[]{:S(2)}, u32[]{:S(2)}) %all-to-all-start.2) | async-done | bytes 32800 | tf_op jit(solution)/shard_map/all_to_all | solution.py:189
  114.9 0.7 shard_map.112
  (4 shorter events, 0.1 us)
Async XLA Ops:
  0.6 15.8 %collective-permute-start = (bf16[256,4096]{1,0:T(8,128)(2,1)}, bf16[256,4096]{1,0:T(8,128)(2,1)S(1)}, u32[]{:S(2)}, u32[]{:S(2)}) collective-permute-start(bf16[256,4096]{1,0:T(8,128)(2,1)} %param.7), channel_id=1, source_target_pairs={{0,1},{1,0},{2,3},{3,2},{4,5},{5,4},{6,7},{7,6},{8,9},{9,8},{10,11... | collective-permute-start | bytes 6291464 | tf_op jit(solution)/shard_map/ppermute | solution.py:195
  10.2 0.9 copy-start.3
  11.2 0.9 copy-start.4
  12.2 4.2 %collective-permute-start.1 = (bf16[256,640]{1,0:T(8,128)(2,1)S(1)}, bf16[256,640]{1,0:T(8,128)(2,1)S(1)}, u32[]{:S(2)}, u32[]{:S(2)}) collective-permute-start(bf16[256,640]{1,0:T(8,128)(2,1)S(1)} %get-tuple-element.11), channel_id=1, source_target_pairs={{0,1},{1,0},{2,3},{3,2},{4,5},{5,4},{6,7},{7,6},{8,9},{9,8},{10,11... | collective-permute-start | bytes 983048 | tf_op jit(solution)/shard_map/ppermute | solution.py:198
  14.2 2.3 %copy-start = (f32[4096]{0:T(1024)S(1)}, f32[4096]{0:T(1024)}, u32[]{:S(2)}) copy-start(f32[4096]{0:T(1024)} %param.9) | copy-start | bytes 49156
  17.1 17.3 %collective-permute-start.5 = (bf16[768,512]{1,0:T(8,128)(2,1)S(1)}, bf16[768,512]{1,0:T(8,128)(2,1)S(1)}, u32[]{:S(2)}, u32[]{:S(2)}) collective-permute-start(bf16[768,512]{1,0:T(8,128)(2,1)S(1)} %shard_map.107), channel_id=1, source_target_pairs={{0,32},{1,257},{2,34},{3,259},{4,36},{5,261},{6,38},{7,263},{8,40}... | collective-permute-start | bytes 2359304 | tf_op jit(solution)/shard_map/ppermute | solution.py:207
  19.7 20.4 %collective-permute-start.6 = (bf16[768,512]{1,0:T(8,128)(2,1)S(1)}, bf16[768,512]{1,0:T(8,128)(2,1)S(1)}, u32[]{:S(2)}, u32[]{:S(2)}) collective-permute-start(bf16[768,512]{1,0:T(8,128)(2,1)S(1)} %shard_map.108), channel_id=1, source_target_pairs={{0,16},{1,129},{2,18},{3,131},{4,20},{5,133},{6,22},{7,135},{8,24}... | collective-permute-start | bytes 2359304 | tf_op jit(solution)/shard_map/ppermute | solution.py:207
  22.3 17.8 %collective-permute-start.7 = (bf16[768,512]{1,0:T(8,128)(2,1)S(1)}, bf16[768,512]{1,0:T(8,128)(2,1)S(1)}, u32[]{:S(2)}, u32[]{:S(2)}) collective-permute-start(bf16[768,512]{1,0:T(8,128)(2,1)S(1)} %shard_map.109), channel_id=1, source_target_pairs={{0,48},{1,385},{2,50},{3,387},{4,52},{5,389},{6,54},{7,391},{8,56}... | collective-permute-start | bytes 2359304 | tf_op jit(solution)/shard_map/ppermute | solution.py:207
  27.3 17.3 %collective-permute-start.2 = (bf16[256,512]{1,0:T(8,128)(2,1)S(1)}, bf16[256,512]{1,0:T(8,128)(2,1)S(1)}, u32[]{:S(2)}, u32[]{:S(2)}) collective-permute-start(bf16[256,512]{1,0:T(8,128)(2,1)S(1)} %shard_map.103), channel_id=1, source_target_pairs={{0,32},{1,257},{2,34},{3,259},{4,36},{5,261},{6,38},{7,263},{8,40}... | collective-permute-start | bytes 786440 | tf_op jit(solution)/shard_map/ppermute | solution.py:207
  31.3 16.6 %collective-permute-start.3 = (bf16[256,512]{1,0:T(8,128)(2,1)S(1)}, bf16[256,512]{1,0:T(8,128)(2,1)S(1)}, u32[]{:S(2)}, u32[]{:S(2)}) collective-permute-start(bf16[256,512]{1,0:T(8,128)(2,1)S(1)} %shard_map.104), channel_id=1, source_target_pairs={{0,16},{1,129},{2,18},{3,131},{4,20},{5,133},{6,22},{7,135},{8,24}... | collective-permute-start | bytes 786440 | tf_op jit(solution)/shard_map/ppermute | solution.py:207
  34.4 13.5 %collective-permute-start.4 = (bf16[256,512]{1,0:T(8,128)(2,1)S(1)}, bf16[256,512]{1,0:T(8,128)(2,1)S(1)}, u32[]{:S(2)}, u32[]{:S(2)}) collective-permute-start(bf16[256,512]{1,0:T(8,128)(2,1)S(1)} %shard_map.105), channel_id=1, source_target_pairs={{0,48},{1,385},{2,50},{3,387},{4,52},{5,389},{6,54},{7,391},{8,56}... | collective-permute-start | bytes 786440 | tf_op jit(solution)/shard_map/ppermute | solution.py:207
  40.5 39.0 %copy-start.1 = (bf16[512,512]{1,0:T(8,128)(2,1)S(1)}, bf16[512,512]{1,0:T(8,128)(2,1)}, u32[]{:S(2)}) copy-start(bf16[512,512]{1,0:T(8,128)(2,1)} %key_weight_ref.1) | copy-start | bytes 1572868
  40.5 39.0 %copy-start.2 = (bf16[512,512]{1,0:T(8,128)(2,1)S(1)}, bf16[512,512]{1,0:T(8,128)(2,1)}, u32[]{:S(2)}) copy-start(bf16[512,512]{1,0:T(8,128)(2,1)} %value_weight_ref.1) | copy-start | bytes 1572868
  40.6 9.0 %collective-permute-start.8 = (bf16[256,512]{1,0:T(8,128)(2,1)S(1)}, bf16[256,512]{1,0:T(8,128)(2,1)S(1)}, u32[]{:S(2)}, u32[]{:S(2)}) collective-permute-start(bf16[256,512]{1,0:T(8,128)(2,1)S(1)} %get-tuple-element.16), channel_id=1, source_target_pairs={{0,256},{1,33},{2,258},{3,35},{4,260},{5,37},{6,262},{7,39},{8,264... | collective-permute-start | bytes 786440 | tf_op jit(solution)/shard_map/ppermute | solution.py:213
  42.6 7.4 %collective-permute-start.10 = (bf16[256,512]{1,0:T(8,128)(2,1)S(1)}, bf16[256,512]{1,0:T(8,128)(2,1)S(1)}, u32[]{:S(2)}, u32[]{:S(2)}) collective-permute-start(bf16[256,512]{1,0:T(8,128)(2,1)S(1)} %get-tuple-element.17), channel_id=1, source_target_pairs={{0,384},{1,49},{2,386},{3,51},{4,388},{5,53},{6,390},{7,55},{8,392... | collective-permute-start | bytes 786440 | tf_op jit(solution)/shard_map/ppermute | solution.py:213
  44.6 9.2 %collective-permute-start.9 = (bf16[256,512]{1,0:T(8,128)(2,1)S(1)}, bf16[256,512]{1,0:T(8,128)(2,1)S(1)}, u32[]{:S(2)}, u32[]{:S(2)}) collective-permute-start(bf16[256,512]{1,0:T(8,128)(2,1)S(1)} %get-tuple-element.18), channel_id=1, source_target_pairs={{0,128},{1,17},{2,130},{3,19},{4,132},{5,21},{6,134},{7,23},{8,136... | collective-permute-start | bytes 786440 | tf_op jit(solution)/shard_map/ppermute | solution.py:213
  98.1 16.8 %all-to-all-start.2 = ((f32[16,4,128]{2,1,0:T(4,128)}), f32[16,4,128]{2,1,0:T(4,128)S(1)}, u32[]{:S(2)}, u32[]{:S(2)}) async-start(f32[16,4,128]{2,1,0:T(4,128)} %broadcast_in_dim.22), calls=%async_computation.2 | async-start | bytes 65536 | tf_op jit(solution)/shard_map/all_to_all | solution.py:189
  103.5 3.4 %collective-permute-start.11 = (f32[16,512]{1,0:T(8,128)S(1)}, f32[16,512]{1,0:T(8,128)S(1)}, u32[]{:S(2)}, u32[]{:S(2)}) collective-permute-start(f32[16,512]{1,0:T(8,128)S(1)} %convert_reduce_fusion.owned_ref), channel_id=1, source_target_pairs={{0,1},{1,0},{2,3},{3,2},{4,5},{5,4},{6,7},{7,6},{8,9},{9,8},{10,11... | collective-permute-start | bytes 98312 | tf_op jit(solution)/shard_map/ppermute | solution.py:218

commit v7 on v5

--- a/solution.py
+++ b/solution.py
@@ -126,18 +126,19 @@
     gains = jnp.sum(jnp.where(lane == z_lo * rows + row, gain_row, 0.0), axis=1, keepdims=True)
     block = lax.rem(y * NX + x + z_lo, BLOCKS)
     terms = jnp.where(lane == block * rows + row, sums / gains, 0.0)
-    told_ref[0:1, :] = jnp.sum(terms, axis=0, keepdims=True)
     mine = lane[:1] == jnp.where(keys_here, 0, 1)
-    told_ref[1:2, :] = jnp.where(mine, jnp.max(jnp.abs(owned)), 0.0)
+    peak = jnp.where(mine, jnp.max(jnp.abs(owned)), 0.0)
+    told = jnp.concatenate([jnp.sum(terms, axis=0, keepdims=True), peak], axis=0)
+    told_ref[...] = jnp.broadcast_to(told[None], told_ref.shape)
 
 
 def level_kernel(heard_ref, told_ref):
     heard = heard_ref[...]
     row = lax.broadcasted_iota(jnp.int32, heard.shape, 0)
     terms = jnp.where(row % 2 == 0, heard, 0.0)
-    told_ref[0:2, :] = jnp.sum(terms.reshape(2, -1, TILE), axis=1)
-    told_ref[2:3, :] = jnp.max(jnp.where(row % 2 == 0, 0.0, heard), axis=0, keepdims=True)
-    told_ref[3:4, :] = jnp.zeros((1, TILE), jnp.float32)
+    peaks = jnp.max(jnp.where(row % 2 == 0, 0.0, heard), axis=0, keepdims=True)
+    told = jnp.concatenate([jnp.sum(terms.reshape(2, -1, TILE), axis=1), peaks, jnp.zeros_like(peaks)], axis=0)
+    told_ref[...] = jnp.broadcast_to(told[None], told_ref.shape)
 
 
 def output_kernel(owned_ref, arrived_ref, heard_ref, key_scaled_ref, value_scaled_ref, amax_ref, gain_grad_ref):
@@ -178,9 +179,8 @@
     return jax.ShapeDtypeStruct(shape, jnp.float32)
 
 
-def told_to(groups, told):
-    everyone = jnp.broadcast_to(told[None], (len(groups[0]),) + told.shape)
-    heard = lax.all_to_all(everyone, ALL, 0, 0, tiled=True, axis_index_groups=groups)
+def exchanged(groups, told):
+    heard = lax.all_to_all(told, ALL, 0, 0, tiled=True, axis_index_groups=groups)
     return heard.reshape(-1, TILE)
 
 
@@ -209,9 +209,11 @@
     owned = jnp.sum(heard.astype(jnp.float32), axis=0)
     arrived = lax.ppermute(owned, ALL, SWAP)
     gain_rows = norm_gain.reshape(-1, TILE)
-    told = small_call(told_kernel, floats(2, TILE), VMEM_BLOCK, owned, key_weight, value_weight, gain_rows)
-    told = small_call(level_kernel, floats(4, TILE), VMEM_BLOCK, told_to(level_groups(), told))
-    heard = told_to(z_groups(), told)
+    told = small_call(
+        told_kernel, floats(NY * NX * NC, 2, TILE), VMEM_BLOCK, owned, key_weight, value_weight, gain_rows
+    )
+    told = small_call(level_kernel, floats(NZH * NZL, 4, TILE), VMEM_BLOCK, exchanged(level_groups(), told))
+    heard = exchanged(z_groups(), told)
     key_scaled, value_scaled, grad_amax, gain_grad = small_call(
         output_kernel,
         (floats(*owned.shape), floats(*owned.shape), floats(2), floats(*gain_rows.shape)),

time: 116 us -> 116 us (level)
  no operation moved by 1% of the time
where the time goes in v7:
time: 116 us
  starting transfers between devices  44.5 us (38%)
  blocking collectives  43.3 us (37%)
  waiting for transfers between devices  17.9 us (15%)
  Pallas kernels  5.47 us (5%)
  other arithmetic  3.65 us (3%)
    all_to_all x1, blocking collectives, per_device(): lax.all_to_all(plane_sum, ALL, 0, 0, tiled=True, axis_index_groups=z_grou...  25.5 us
    ppermute x6, starting transfers between devices, per_device(): chunk = lax.ppermute(product(offset, steps), ALL, plane_pairs(0, offset))  18.5 us
    all_to_all x1, blocking collectives, exchanged(): lax.all_to_all(told, ALL, 0, 0, tiled=True, axis_index_groups=groups)  17.8 us
    ppermute x1, starting transfers between devices, per_device(): other = lax.ppermute(own, ALL, SWAP)  8.79 us
    all_to_all x1, waiting for transfers between devices, exchanged(): lax.all_to_all(told, ALL, 0, 0, tiled=True, axis_index_groups=groups)  8.04 us
    ppermute x3, starting transfers between devices, per_device(): lax.ppermute(total_of(lines[step]).astype(jnp.bfloat16), ALL, plane_pairs...  7.33 us
    ppermute x3, waiting for transfers between devices, per_device(): lax.ppermute(total_of(lines[step]).astype(jnp.bfloat16), ALL, plane_pairs...  5.79 us
    all_to_all x1, starting transfers between devices, exchanged(): lax.all_to_all(told, ALL, 0, 0, tiled=True, axis_index_groups=groups)  5.28 us
  transfers between devices with their start and end apart: 13, of which 7 were waited for; matrix products, arithmetic and copies ran while one was open for 0% of the time, Pallas kernels for 3%

profile of v7, /device:TPU:1, one launch (start us, length us, event | category | flops | bytes accessed | tf_op | source)
XLA Modules:
  0.0 115.7 jit_solution(18096735409153271869)
XLA Ops:
  0.6 0.7 convert_element_type.82
  1.3 0.0 copy-start.2
  1.3 0.0 copy-start.3
  1.3 2.3 %multiply_convert_fusion.own_ref = bf16[256,4096]{1,0:T(8,128)(2,1)S(1)} fusion(bf16[256,4096]{1,0:T(8,128)(2,1)} %param.7, f32[4096]{0:T(1024)} %param.9, f32[256]{0:T(256)S(1)} %convert_element_type.82), kind=kLoop, calls=%fused_computation | loop fusion | flops 4194304 | bytes 4211712 | tf_op jit(solution)/shard_map/convert_element_type | solution.py:192
  3.6 8.8 %collective-permute-start = (bf16[256,4096]{1,0:T(8,128)(2,1)S(1)}, bf16[256,4096]{1,0:T(8,128)(2,1)S(1)}, u32[]{:S(2)}, u32[]{:S(2)}) collective-permute-start(bf16[256,4096]{1,0:T(8,128)(2,1)S(1)} %multiply_convert_fusion.own_ref), channel_id=1, source_target_pairs={{0,1},{1,0},{2,3},{3,2},{4,5},{5,4},{6,7},{7,6},{8,9},{9,8},{10,11... | collective-permute-start | bytes 6291464 | tf_op jit(solution)/shard_map/ppermute | solution.py:193
  12.4 0.0 copy-done.2
  12.4 0.0 copy-done.3
  12.4 0.1 shard_map.102
  12.4 1.9 %collective-permute-start.1 = (bf16[256,512]{1,0:T(8,128)(2,1)S(1)}, bf16[256,512]{1,0:T(8,128)(2,1)S(1)}, u32[]{:S(2)}, u32[]{:S(2)}) collective-permute-start(bf16[256,512]{1,0:T(8,128)(2,1)S(1)} %get-tuple-element.11), channel_id=1, source_target_pairs={{0,1},{1,0},{2,3},{3,2},{4,5},{5,4},{6,7},{7,6},{8,9},{9,8},{10,11... | collective-permute-start | bytes 786440 | tf_op jit(solution)/shard_map/ppermute | solution.py:190
  14.4 2.1 %collective-permute-done.1.other_grad_ref = bf16[256,512]{1,0:T(8,128)(2,1)S(1)} collective-permute-done((bf16[256,512]{1,0:T(8,128)(2,1)S(1)}, bf16[256,512]{1,0:T(8,128)(2,1)S(1)}, u32[]{:S(2)}, u32[]{:S(2)}) %collective-permute-start.1) | collective-permute-done | bytes 262176 | tf_op jit(solution)/shard_map/ppermute | solution.py:190
  16.5 0.0 collective-permute-done.other_ref
  16.5 0.7 shard_map.107
  17.2 1.9 %collective-permute-start.5 = (bf16[768,512]{1,0:T(8,128)(2,1)S(1)}, bf16[768,512]{1,0:T(8,128)(2,1)S(1)}, u32[]{:S(2)}, u32[]{:S(2)}) collective-permute-start(bf16[768,512]{1,0:T(8,128)(2,1)S(1)} %shard_map.107), channel_id=1, source_target_pairs={{0,32},{1,257},{2,34},{3,259},{4,36},{5,261},{6,38},{7,263},{8,40}... | collective-permute-start | bytes 2359304 | tf_op jit(solution)/shard_map/ppermute | solution.py:199
  19.1 0.7 shard_map.108
  19.8 1.9 %collective-permute-start.6 = (bf16[768,512]{1,0:T(8,128)(2,1)S(1)}, bf16[768,512]{1,0:T(8,128)(2,1)S(1)}, u32[]{:S(2)}, u32[]{:S(2)}) collective-permute-start(bf16[768,512]{1,0:T(8,128)(2,1)S(1)} %shard_map.108), channel_id=1, source_target_pairs={{0,16},{1,129},{2,18},{3,131},{4,20},{5,133},{6,22},{7,135},{8,24}... | collective-permute-start | bytes 2359304 | tf_op jit(solution)/shard_map/ppermute | solution.py:199
  21.7 0.7 shard_map.109
  22.4 4.6 %collective-permute-start.7 = (bf16[768,512]{1,0:T(8,128)(2,1)S(1)}, bf16[768,512]{1,0:T(8,128)(2,1)S(1)}, u32[]{:S(2)}, u32[]{:S(2)}) collective-permute-start(bf16[768,512]{1,0:T(8,128)(2,1)S(1)} %shard_map.109), channel_id=1, source_target_pairs={{0,48},{1,385},{2,50},{3,387},{4,52},{5,389},{6,54},{7,391},{8,56}... | collective-permute-start | bytes 2359304 | tf_op jit(solution)/shard_map/ppermute | solution.py:199
  27.0 0.4 shard_map.103
  27.3 3.7 %collective-permute-start.2 = (bf16[256,512]{1,0:T(8,128)(2,1)S(1)}, bf16[256,512]{1,0:T(8,128)(2,1)S(1)}, u32[]{:S(2)}, u32[]{:S(2)}) collective-permute-start(bf16[256,512]{1,0:T(8,128)(2,1)S(1)} %shard_map.103), channel_id=1, source_target_pairs={{0,32},{1,257},{2,34},{3,259},{4,36},{5,261},{6,38},{7,263},{8,40}... | collective-permute-start | bytes 786440 | tf_op jit(solution)/shard_map/ppermute | solution.py:199
  31.0 0.4 shard_map.104
  31.4 1.9 %collective-permute-start.3 = (bf16[256,512]{1,0:T(8,128)(2,1)S(1)}, bf16[256,512]{1,0:T(8,128)(2,1)S(1)}, u32[]{:S(2)}, u32[]{:S(2)}) collective-permute-start(bf16[256,512]{1,0:T(8,128)(2,1)S(1)} %shard_map.104), channel_id=1, source_target_pairs={{0,16},{1,129},{2,18},{3,131},{4,20},{5,133},{6,22},{7,135},{8,24}... | collective-permute-start | bytes 786440 | tf_op jit(solution)/shard_map/ppermute | solution.py:199
  33.3 0.4 shard_map.105
  33.7 0.8 shard_map.106
  34.5 0.0 collective-permute-done.5
  34.5 4.6 %collective-permute-start.4 = (bf16[256,512]{1,0:T(8,128)(2,1)S(1)}, bf16[256,512]{1,0:T(8,128)(2,1)S(1)}, u32[]{:S(2)}, u32[]{:S(2)}) collective-permute-start(bf16[256,512]{1,0:T(8,128)(2,1)S(1)} %shard_map.105), channel_id=1, source_target_pairs={{0,48},{1,385},{2,50},{3,387},{4,52},{5,389},{6,54},{7,391},{8,56}... | collective-permute-start | bytes 786440 | tf_op jit(solution)/shard_map/ppermute | solution.py:199
  39.1 1.1 collective-permute-done.6
  40.1 0.0 collective-permute-done.7
  40.1 0.4 add_convert_fusion.3
  40.6 0.0 copy-start
  40.6 0.0 copy-start.1
  40.6 0.0 copy-start.4
  40.6 2.1 %collective-permute-start.8 = (bf16[256,512]{1,0:T(8,128)(2,1)S(1)}, bf16[256,512]{1,0:T(8,128)(2,1)S(1)}, u32[]{:S(2)}, u32[]{:S(2)}) collective-permute-start(bf16[256,512]{1,0:T(8,128)(2,1)S(1)} %get-tuple-element.16), channel_id=1, source_target_pairs={{0,256},{1,33},{2,258},{3,35},{4,260},{5,37},{6,262},{7,39},{8,264... | collective-permute-start | bytes 786440 | tf_op jit(solution)/shard_map/ppermute | solution.py:205
  42.7 1.9 %collective-permute-start.10 = (bf16[256,512]{1,0:T(8,128)(2,1)S(1)}, bf16[256,512]{1,0:T(8,128)(2,1)S(1)}, u32[]{:S(2)}, u32[]{:S(2)}) collective-permute-start(bf16[256,512]{1,0:T(8,128)(2,1)S(1)} %get-tuple-element.17), channel_id=1, source_target_pairs={{0,384},{1,49},{2,386},{3,51},{4,388},{5,53},{6,390},{7,55},{8,392... | collective-permute-start | bytes 786440 | tf_op jit(solution)/shard_map/ppermute | solution.py:205
  44.6 0.0 collective-permute-done.2
  44.6 3.4 %collective-permute-start.9 = (bf16[256,512]{1,0:T(8,128)(2,1)S(1)}, bf16[256,512]{1,0:T(8,128)(2,1)S(1)}, u32[]{:S(2)}, u32[]{:S(2)}) collective-permute-start(bf16[256,512]{1,0:T(8,128)(2,1)S(1)} %get-tuple-element.18), channel_id=1, source_target_pairs={{0,128},{1,17},{2,130},{3,19},{4,132},{5,21},{6,134},{7,23},{8,136... | collective-permute-start | bytes 786440 | tf_op jit(solution)/shard_map/ppermute | solution.py:205
  48.0 0.0 collective-permute-done.3
  48.0 0.0 collective-permute-done.4
  48.0 1.7 %collective-permute-done.8 = bf16[256,512]{1,0:T(8,128)(2,1)S(1)} collective-permute-done((bf16[256,512]{1,0:T(8,128)(2,1)S(1)}, bf16[256,512]{1,0:T(8,128)(2,1)S(1)}, u32[]{:S(2)}, u32[]{:S(2)}) %collective-permute-start.8) | collective-permute-done | bytes 262176 | tf_op jit(solution)/shard_map/ppermute | solution.py:205
  49.7 0.4 collective-permute-done.10
  50.1 3.7 %collective-permute-done.9 = bf16[256,512]{1,0:T(8,128)(2,1)S(1)} collective-permute-done((bf16[256,512]{1,0:T(8,128)(2,1)S(1)}, bf16[256,512]{1,0:T(8,128)(2,1)S(1)}, u32[]{:S(2)}, u32[]{:S(2)}) %collective-permute-start.9) | collective-permute-done | bytes 262176 | tf_op jit(solution)/shard_map/ppermute | solution.py:205
  53.8 0.2 add_convert_fusion
  54.1 25.5 %all_to_all.15 = bf16[16,16,512]{2,1,0:T(8,128)(2,1)S(1)} all-to-all(bf16[16,16,512]{2,1,0:T(8,128)(2,1)S(1)} %bitcast.8), channel_id=1, replica_groups={{0,2,4,6,8,10,12,14,64,66,68,70,72,74,76,78},{1,3,5,7,9,11,13,15,65,67,..., dimensions={0} | all-to-all | bytes 524288 | tf_op jit(solution)/shard_map/all_to_all | solution.py:208
  79.6 0.0 copy-done
  79.6 0.0 copy-done.1
  79.6 0.0 copy-done.4
  79.6 0.1 shard_map.110
  79.7 17.8 %all_to_all.16 = f32[32,2,128]{2,1,0:T(2,128)S(1)} all-to-all(f32[32,2,128]{2,1,0:T(2,128)S(1)} %shard_map.110), channel_id=1, replica_groups={{0,1,16,17,32,33,48,49,128,129,144,145,160,161,176,177,256,257,272,273,..., dimensions={0} | all-to-all | bytes 65536 | tf_op jit(solution)/shard_map/all_to_all | solution.py:183
  97.6 0.6 shard_map.111
  98.2 5.3 %all-to-all-start.2 = ((f32[16,4,128]{2,1,0:T(4,128)}), f32[16,4,128]{2,1,0:T(4,128)S(1)}, u32[]{:S(2)}, u32[]{:S(2)}) async-start(f32[16,4,128]{2,1,0:T(4,128)} %shard_map.111), calls=%async_computation.2 | async-start | bytes 65536 | tf_op jit(solution)/shard_map/all_to_all | solution.py:183
  103.5 2.6 %collective-permute-start.11 = (f32[16,512]{1,0:T(8,128)S(1)}, f32[16,512]{1,0:T(8,128)S(1)}, u32[]{:S(2)}, u32[]{:S(2)}) collective-permute-start(f32[16,512]{1,0:T(8,128)S(1)} %convert_reduce_fusion.owned_ref), channel_id=1, source_target_pairs={{0,1},{1,0},{2,3},{3,2},{4,5},{5,4},{6,7},{7,6},{8,9},{9,8},{10,11... | collective-permute-start | bytes 98312 | tf_op jit(solution)/shard_map/ppermute | solution.py:210
  106.1 0.8 collective-permute-done.11.arrived_ref
  106.9 8.0 %all-to-all-done.2 = f32[16,4,128]{2,1,0:T(4,128)S(1)} async-done(((f32[16,4,128]{2,1,0:T(4,128)}), f32[16,4,128]{2,1,0:T(4,128)S(1)}, u32[]{:S(2)}, u32[]{:S(2)}) %all-to-all-start.2) | async-done | bytes 32800 | tf_op jit(solution)/shard_map/all_to_all | solution.py:183
  115.0 0.7 shard_map.112
  (1 shorter events, 0.0 us)
Async XLA Ops:
  1.3 11.1 %copy-start.2 = (bf16[256,512]{1,0:T(8,128)(2,1)S(1)}, bf16[256,512]{1,0:T(8,128)(2,1)}, u32[]{:S(2)}) copy-start(bf16[256,512]{1,0:T(8,128)(2,1)} %key_grad_ref.1) | copy-start | bytes 786436
  1.3 11.1 %copy-start.3 = (bf16[256,512]{1,0:T(8,128)(2,1)S(1)}, bf16[256,512]{1,0:T(8,128)(2,1)}, u32[]{:S(2)}) copy-start(bf16[256,512]{1,0:T(8,128)(2,1)} %value_grad_ref.1) | copy-start | bytes 786436
  3.6 12.9 %collective-permute-start = (bf16[256,4096]{1,0:T(8,128)(2,1)S(1)}, bf16[256,4096]{1,0:T(8,128)(2,1)S(1)}, u32[]{:S(2)}, u32[]{:S(2)}) collective-permute-start(bf16[256,4096]{1,0:T(8,128)(2,1)S(1)} %multiply_convert_fusion.own_ref), channel_id=1, source_target_pairs={{0,1},{1,0},{2,3},{3,2},{4,5},{5,4},{6,7},{7,6},{8,9},{9,8},{10,11... | collective-permute-start | bytes 6291464 | tf_op jit(solution)/shard_map/ppermute | solution.py:193
  12.4 4.1 %collective-permute-start.1 = (bf16[256,512]{1,0:T(8,128)(2,1)S(1)}, bf16[256,512]{1,0:T(8,128)(2,1)S(1)}, u32[]{:S(2)}, u32[]{:S(2)}) collective-permute-start(bf16[256,512]{1,0:T(8,128)(2,1)S(1)} %get-tuple-element.11), channel_id=1, source_target_pairs={{0,1},{1,0},{2,3},{3,2},{4,5},{5,4},{6,7},{7,6},{8,9},{9,8},{10,11... | collective-permute-start | bytes 786440 | tf_op jit(solution)/shard_map/ppermute | solution.py:190
  17.2 17.3 %collective-permute-start.5 = (bf16[768,512]{1,0:T(8,128)(2,1)S(1)}, bf16[768,512]{1,0:T(8,128)(2,1)S(1)}, u32[]{:S(2)}, u32[]{:S(2)}) collective-permute-start(bf16[768,512]{1,0:T(8,128)(2,1)S(1)} %shard_map.107), channel_id=1, source_target_pairs={{0,32},{1,257},{2,34},{3,259},{4,36},{5,261},{6,38},{7,263},{8,40}... | collective-permute-start | bytes 2359304 | tf_op jit(solution)/shard_map/ppermute | solution.py:199
  19.8 20.4 %collective-permute-start.6 = (bf16[768,512]{1,0:T(8,128)(2,1)S(1)}, bf16[768,512]{1,0:T(8,128)(2,1)S(1)}, u32[]{:S(2)}, u32[]{:S(2)}) collective-permute-start(bf16[768,512]{1,0:T(8,128)(2,1)S(1)} %shard_map.108), channel_id=1, source_target_pairs={{0,16},{1,129},{2,18},{3,131},{4,20},{5,133},{6,22},{7,135},{8,24}... | collective-permute-start | bytes 2359304 | tf_op jit(solution)/shard_map/ppermute | solution.py:199
  22.4 17.8 %collective-permute-start.7 = (bf16[768,512]{1,0:T(8,128)(2,1)S(1)}, bf16[768,512]{1,0:T(8,128)(2,1)S(1)}, u32[]{:S(2)}, u32[]{:S(2)}) collective-permute-start(bf16[768,512]{1,0:T(8,128)(2,1)S(1)} %shard_map.109), channel_id=1, source_target_pairs={{0,48},{1,385},{2,50},{3,387},{4,52},{5,389},{6,54},{7,391},{8,56}... | collective-permute-start | bytes 2359304 | tf_op jit(solution)/shard_map/ppermute | solution.py:199
  27.3 17.3 %collective-permute-start.2 = (bf16[256,512]{1,0:T(8,128)(2,1)S(1)}, bf16[256,512]{1,0:T(8,128)(2,1)S(1)}, u32[]{:S(2)}, u32[]{:S(2)}) collective-permute-start(bf16[256,512]{1,0:T(8,128)(2,1)S(1)} %shard_map.103), channel_id=1, source_target_pairs={{0,32},{1,257},{2,34},{3,259},{4,36},{5,261},{6,38},{7,263},{8,40}... | collective-permute-start | bytes 786440 | tf_op jit(solution)/shard_map/ppermute | solution.py:199
  31.4 16.6 %collective-permute-start.3 = (bf16[256,512]{1,0:T(8,128)(2,1)S(1)}, bf16[256,512]{1,0:T(8,128)(2,1)S(1)}, u32[]{:S(2)}, u32[]{:S(2)}) collective-permute-start(bf16[256,512]{1,0:T(8,128)(2,1)S(1)} %shard_map.104), channel_id=1, source_target_pairs={{0,16},{1,129},{2,18},{3,131},{4,20},{5,133},{6,22},{7,135},{8,24}... | collective-permute-start | bytes 786440 | tf_op jit(solution)/shard_map/ppermute | solution.py:199
  34.5 13.5 %collective-permute-start.4 = (bf16[256,512]{1,0:T(8,128)(2,1)S(1)}, bf16[256,512]{1,0:T(8,128)(2,1)S(1)}, u32[]{:S(2)}, u32[]{:S(2)}) collective-permute-start(bf16[256,512]{1,0:T(8,128)(2,1)S(1)} %shard_map.105), channel_id=1, source_target_pairs={{0,48},{1,385},{2,50},{3,387},{4,52},{5,389},{6,54},{7,391},{8,56}... | collective-permute-start | bytes 786440 | tf_op jit(solution)/shard_map/ppermute | solution.py:199
  40.6 39.0 %copy-start = (bf16[512,512]{1,0:T(8,128)(2,1)S(1)}, bf16[512,512]{1,0:T(8,128)(2,1)}, u32[]{:S(2)}) copy-start(bf16[512,512]{1,0:T(8,128)(2,1)} %key_weight_ref.1) | copy-start | bytes 1572868
  40.6 39.0 %copy-start.1 = (bf16[512,512]{1,0:T(8,128)(2,1)S(1)}, bf16[512,512]{1,0:T(8,128)(2,1)}, u32[]{:S(2)}) copy-start(bf16[512,512]{1,0:T(8,128)(2,1)} %value_weight_ref.1) | copy-start | bytes 1572868
  40.6 39.0 %copy-start.4 = (f32[4096]{0:T(1024)S(1)}, f32[4096]{0:T(1024)}, u32[]{:S(2)}) copy-start(f32[4096]{0:T(1024)} %param.9) | copy-start | bytes 49156
  40.6 9.0 %collective-permute-start.8 = (bf16[256,512]{1,0:T(8,128)(2,1)S(1)}, bf16[256,512]{1,0:T(8,128)(2,1)S(1)}, u32[]{:S(2)}, u32[]{:S(2)}) collective-permute-start(bf16[256,512]{1,0:T(8,128)(2,1)S(1)} %get-tuple-element.16), channel_id=1, source_target_pairs={{0,256},{1,33},{2,258},{3,35},{4,260},{5,37},{6,262},{7,39},{8,264... | collective-permute-start | bytes 786440 | tf_op jit(solution)/shard_map/ppermute | solution.py:205
  42.7 7.4 %collective-permute-start.10 = (bf16[256,512]{1,0:T(8,128)(2,1)S(1)}, bf16[256,512]{1,0:T(8,128)(2,1)S(1)}, u32[]{:S(2)}, u32[]{:S(2)}) collective-permute-start(bf16[256,512]{1,0:T(8,128)(2,1)S(1)} %get-tuple-element.17), channel_id=1, source_target_pairs={{0,384},{1,49},{2,386},{3,51},{4,388},{5,53},{6,390},{7,55},{8,392... | collective-permute-start | bytes 786440 | tf_op jit(solution)/shard_map/ppermute | solution.py:205
  44.6 9.2 %collective-permute-start.9 = (bf16[256,512]{1,0:T(8,128)(2,1)S(1)}, bf16[256,512]{1,0:T(8,128)(2,1)S(1)}, u32[]{:S(2)}, u32[]{:S(2)}) collective-permute-start(bf16[256,512]{1,0:T(8,128)(2,1)S(1)} %get-tuple-element.18), channel_id=1, source_target_pairs={{0,128},{1,17},{2,130},{3,19},{4,132},{5,21},{6,134},{7,23},{8,136... | collective-permute-start | bytes 786440 | tf_op jit(solution)/shard_map/ppermute | solution.py:205
  98.2 16.8 %all-to-all-start.2 = ((f32[16,4,128]{2,1,0:T(4,128)}), f32[16,4,128]{2,1,0:T(4,128)S(1)}, u32[]{:S(2)}, u32[]{:S(2)}) async-start(f32[16,4,128]{2,1,0:T(4,128)} %shard_map.111), calls=%async_computation.2 | async-start | bytes 65536 | tf_op jit(solution)/shard_map/all_to_all | solution.py:183
  103.5 3.4 %collective-permute-start.11 = (f32[16,512]{1,0:T(8,128)S(1)}, f32[16,512]{1,0:T(8,128)S(1)}, u32[]{:S(2)}, u32[]{:S(2)}) collective-permute-start(f32[16,512]{1,0:T(8,128)S(1)} %convert_reduce_fusion.owned_ref), channel_id=1, source_target_pairs={{0,1},{1,0},{2,3},{3,2},{4,5},{5,4},{6,7},{7,6},{8,9},{9,8},{10,11... | collective-permute-start | bytes 98312 | tf_op jit(solution)/shard_map/ppermute | solution.py:210
